TPU v7x, 32 devices: a whole 2x2x4 slice. The times are simulated.
32 devices in a mesh: seq: 2 (over x), ctx: 8 (over z, y), wsh: 2 (over core).
Axes of the slice: x: 2, y: 2, z: 4, core: 2. Of those that a mesh axis runs over, the one named last changes fastest.
Arguments:
- tokens: bfloat16 [4, 1024, 768], P(('seq', 'wsh'), 'ctx'), may hold values from -6 to 6
- w_qkv: bfloat16 [768, 2304], P('wsh'), may hold values from -0.21875 to 0.21875
- w_out: bfloat16 [768, 768], P('wsh'), may hold values from -4 to 4
- w_in: bfloat16 [768, 2304], P('wsh'), may hold values from -0.21875 to 0.21875
- w_mlp: bfloat16 [1152, 768], P('wsh'), may hold values from -0.1875 to 0.1875
- gain_attn: bfloat16 [768], P('wsh'), may hold values from 0.099609375 to 1.8984375
- gain_mlp: bfloat16 [768], P('wsh'), may hold values from 0.099609375 to 1.8984375
- cotangent: bfloat16 [4, 1024, 768], P(('seq', 'wsh'), 'ctx'), may hold values from -6 to 6
Outputs:
- layer_out: bfloat16 [4, 1024, 768], P(('seq', 'wsh'), 'ctx')
- tokens_grad: bfloat16 [4, 1024, 768], P(('seq', 'wsh'), 'ctx')
- w_qkv_grad: float32 [768, 2304], P('wsh')
- w_out_grad: float32 [768, 768], P('wsh')
- w_in_grad: float32 [768, 2304], P('wsh')
- w_mlp_grad: float32 [1152, 768], P('wsh')
- gain_attn_grad: float32 [768], P('wsh')
- gain_mlp_grad: float32 [768], P('wsh')
All inputs are finite; a program needn't handle non-finite values.
Results may differ from a plain program's by a relative error of at most 0.018.
Values may be sent and summed in bfloat16 or wider, within the bound.
No kernel may reach another device: no remote copies, remote signals or barrier semaphores. Data moves between devices by JAX's collectives and lax.ppermute only.
A program may use at most 128 MiB of HBM per device.

v0:
```python
from functools import partial
import math

import jax
import jax.numpy as jnp
from jax import lax
from jax.sharding import PartitionSpec as P

HEADS = 12
FF = 1152


EPSILON = 1e-05
THETA = 160000.0


def shifted(block, axis, distance):
    devices = range(lax.axis_size(axis))
    route = [((i - distance) % len(devices), i) for i in devices]
    return lax.ppermute(block, axis, route)


def normalize(inputs):
    average = jnp.mean(inputs, axis=-1, keepdims=True)
    centred = inputs - average
    variance = jnp.mean(centred * centred, axis=-1, keepdims=True)
    rstd_rows = lax.rsqrt(variance + EPSILON)
    return (centred * rstd_rows, rstd_rows)


def norm_back(grad_rows, normed, rstd_rows, gain_vec):
    scaled = grad_rows * gain_vec.astype(jnp.float32)
    inner = jnp.mean(scaled * normed, axis=-1, keepdims=True)
    result = rstd_rows * (scaled - jnp.mean(scaled, axis=-1, keepdims=True) - normed * inner)
    return (result, jnp.sum(grad_rows * normed, axis=0))


def rotary_tables(positions, head_dim):
    half_dim = head_dim // 2
    inverse = jnp.power(
        jnp.float32(THETA), -(jnp.arange(half_dim, dtype=jnp.float32) * (2.0 / head_dim))
    )
    angles = positions[:, None] * inverse[None, :]
    return (jnp.cos(angles), jnp.sin(angles))


def rotate(vectors, cos_table, sin_table):
    half_dim = vectors.shape[-1] // 2
    first_half = vectors[..., :half_dim]
    second_half = vectors[..., half_dim:]
    cos_rows = cos_table[:, None, :]
    sin_rows = sin_table[:, None, :]
    return jnp.concatenate(
        [
            first_half * cos_rows - second_half * sin_rows,
            second_half * cos_rows + first_half * sin_rows,
        ],
        axis=-1,
    )


def unrotate(vectors, cos_table, sin_table):
    half_dim = vectors.shape[-1] // 2
    first_half = vectors[..., :half_dim]
    second_half = vectors[..., half_dim:]
    cos_rows = cos_table[:, None, :]
    sin_rows = sin_table[:, None, :]
    return jnp.concatenate(
        [
            first_half * cos_rows + second_half * sin_rows,
            second_half * cos_rows - first_half * sin_rows,
        ],
        axis=-1,
    )


def contract_rows(left_rows, right_rows):
    return lax.dot_general(
        left_rows, right_rows, (((0,), (0,)), ((), ())), preferred_element_type=jnp.float32
    )


def times_transposed(left_rows, right_rows):
    return lax.dot_general(
        left_rows, right_rows, (((1,), (1,)), ((), ())), preferred_element_type=jnp.float32
    )


def forward_attention(queries, key_rows, values, head_count):
    seqs_here, row_count, model_width = queries.shape
    head_dim = model_width // head_count
    score_scale = head_dim ** (-0.5)
    query_heads = queries.reshape(seqs_here, row_count, head_count, head_dim)
    start_state = (
        jnp.full((seqs_here, head_count, row_count), -jnp.inf, jnp.float32),
        jnp.zeros((seqs_here, head_count, row_count), jnp.float32),
        jnp.zeros((seqs_here, head_count, row_count, head_dim), jnp.float32),
    )
    key_piece = lax.all_gather(key_rows, "ctx", axis=1, tiled=True)
    value_piece = lax.all_gather(values, "ctx", axis=1, tiled=True)
    key_count = key_piece.shape[1]
    key_width = math.gcd(key_count, 512)

    def one_block(block_index, inner):
        row_peak, row_total, weighted = inner
        key_block = lax.dynamic_slice_in_dim(key_piece, block_index * key_width, key_width, 1)
        value_block = lax.dynamic_slice_in_dim(value_piece, block_index * key_width, key_width, 1)
        key_block = key_block.reshape(seqs_here, key_width, head_count, head_dim)
        value_block = value_block.reshape(seqs_here, key_width, head_count, head_dim)
        scores = (
            jnp.einsum(
                "sqhd,skhd->shqk", query_heads, key_block, preferred_element_type=jnp.float32
            )
            * score_scale
        )
        new_peak = jnp.maximum(row_peak, jnp.max(scores, axis=-1))
        factor = jnp.exp(row_peak - new_peak)
        weights = jnp.exp(scores - new_peak[..., None])
        row_total = row_total * factor + jnp.sum(weights, axis=-1)
        update = jnp.einsum(
            "shqk,skhd->shqd",
            weights.astype(jnp.bfloat16),
            value_block,
            preferred_element_type=jnp.float32,
        )
        return (new_peak, row_total, weighted * factor[..., None] + update)

    row_peak, row_total, weighted = lax.fori_loop(0, key_count // key_width, one_block, start_state)
    attended = jnp.transpose(weighted / row_total[..., None], (0, 2, 1, 3)).reshape(
        seqs_here, row_count, model_width
    )
    return (attended, row_peak + jnp.log(row_total))


def pair_grads(query_rows, grad_rows, log_total, delta_rows, key_rows, value_rows, head_count):
    seqs_here, query_count, model_width = query_rows.shape
    key_count = key_rows.shape[1]
    head_dim = model_width // head_count
    score_scale = head_dim ** (-0.5)
    query_heads = query_rows.reshape(seqs_here, query_count, head_count, head_dim)
    grad_heads = grad_rows.reshape(seqs_here, query_count, head_count, head_dim)
    key_heads = key_rows.reshape(seqs_here, key_count, head_count, head_dim)
    value_heads = value_rows.reshape(seqs_here, key_count, head_count, head_dim)
    scores = (
        jnp.einsum("sqhd,skhd->shqk", query_heads, key_heads, preferred_element_type=jnp.float32)
        * score_scale
    )
    probabilities = jnp.exp(scores - log_total[..., None])
    grad_probs = jnp.einsum(
        "sqhd,skhd->shqk", grad_heads, value_heads, preferred_element_type=jnp.float32
    )
    grad_scores = (probabilities * (grad_probs - delta_rows[..., None])).astype(jnp.bfloat16)
    grad_values = jnp.einsum(
        "shqk,sqhd->skhd",
        probabilities.astype(jnp.bfloat16),
        grad_heads,
        preferred_element_type=jnp.float32,
    )
    grad_queries = (
        jnp.einsum("shqk,skhd->sqhd", grad_scores, key_heads, preferred_element_type=jnp.float32)
        * score_scale
    )
    grad_keys = (
        jnp.einsum("shqk,sqhd->skhd", grad_scores, query_heads, preferred_element_type=jnp.float32)
        * score_scale
    )
    return (
        grad_queries.reshape(seqs_here, query_count, model_width),
        grad_keys.reshape(seqs_here, key_count, model_width),
        grad_values.reshape(seqs_here, key_count, model_width),
    )


def pass_key_grads(stacked):
    return shifted(stacked.astype(jnp.bfloat16), "ctx", 1).astype(stacked.dtype)


def local(tokens, w_qkv, w_out, w_in, w_mlp, gain_attn, gain_mlp, cotangent):
    seqs_here, block_rows, model_width = tokens.shape
    head_dim = model_width // HEADS
    hidden_width = FF
    full_qkv, full_out, full_in, full_mlp, attn_gain, mlp_gain = (
        lax.all_gather(w_qkv, "wsh", axis=0, tiled=True),
        lax.all_gather(w_out, "wsh", axis=0, tiled=True),
        lax.all_gather(w_in, "wsh", axis=0, tiled=True),
        lax.all_gather(w_mlp, "wsh", axis=0, tiled=True),
        lax.all_gather(gain_attn, "wsh", axis=0, tiled=True),
        lax.all_gather(gain_mlp, "wsh", axis=0, tiled=True),
    )
    inputs = tokens.astype(jnp.float32).reshape(seqs_here * block_rows, model_width)
    normed_one, rstd_one = normalize(inputs)
    first_in = (normed_one * attn_gain.astype(jnp.float32)).astype(jnp.bfloat16)
    projected = jnp.dot(first_in, full_qkv, preferred_element_type=jnp.float32)
    positions = (
        lax.axis_index("ctx") * block_rows + jnp.arange(block_rows, dtype=jnp.int32)
    ).astype(jnp.float32)
    cos_table, sin_table = rotary_tables(positions, head_dim)

    def shaped(columns):
        return columns.reshape(seqs_here, block_rows, HEADS, head_dim)

    queries = rotate(shaped(projected[:, :model_width]), cos_table, sin_table).astype(jnp.bfloat16)
    queries = queries.reshape(seqs_here, block_rows, model_width)
    key_rows = rotate(
        shaped(projected[:, model_width : 2 * model_width]), cos_table, sin_table
    ).astype(jnp.bfloat16)
    key_rows = key_rows.reshape(seqs_here, block_rows, model_width)
    values = (
        projected[:, 2 * model_width :]
        .astype(jnp.bfloat16)
        .reshape(seqs_here, block_rows, model_width)
    )
    attended, log_total = forward_attention(queries, key_rows, values, HEADS)
    attended_low = attended.astype(jnp.bfloat16).reshape(seqs_here * block_rows, model_width)
    middle = inputs + jnp.dot(attended_low, full_out, preferred_element_type=jnp.float32)
    normed_two, rstd_two = normalize(middle)
    second_in = (normed_two * mlp_gain.astype(jnp.float32)).astype(jnp.bfloat16)
    gate_up = jnp.dot(second_in, full_in, preferred_element_type=jnp.float32)
    gate_half = gate_up[:, :hidden_width]
    up_half = gate_up[:, hidden_width:]
    activated, gelu_pull = jax.vjp(partial(jax.nn.gelu, approximate=False), gate_half)
    hidden = (activated * up_half).astype(jnp.bfloat16)
    layer_out = (middle + jnp.dot(hidden, full_mlp, preferred_element_type=jnp.float32)).astype(
        jnp.bfloat16
    )
    back_qkv, back_out, back_in, back_mlp, back_attn_gain, back_mlp_gain = (
        lax.all_gather(w_qkv, "wsh", axis=0, tiled=True),
        lax.all_gather(w_out, "wsh", axis=0, tiled=True),
        lax.all_gather(w_in, "wsh", axis=0, tiled=True),
        lax.all_gather(w_mlp, "wsh", axis=0, tiled=True),
        lax.all_gather(gain_attn, "wsh", axis=0, tiled=True),
        lax.all_gather(gain_mlp, "wsh", axis=0, tiled=True),
    )
    upstream = cotangent.reshape(seqs_here * block_rows, model_width)
    grad_mlp = contract_rows(hidden, upstream)
    grad_hidden = times_transposed(upstream, back_mlp).astype(jnp.bfloat16).astype(jnp.float32)
    grad_gate = gelu_pull(grad_hidden * up_half)[0]
    grad_gate_up = jnp.concatenate([grad_gate, grad_hidden * activated], axis=-1).astype(
        jnp.bfloat16
    )
    grad_in = contract_rows(second_in, grad_gate_up)
    grad_second = times_transposed(grad_gate_up, back_in)
    grad_middle_norm, grad_mlp_gain = norm_back(grad_second, normed_two, rstd_two, back_mlp_gain)
    grad_middle = upstream.astype(jnp.float32) + grad_middle_norm
    grad_branch = grad_middle.astype(jnp.bfloat16)
    grad_out = contract_rows(attended_low, grad_branch)
    grad_attended = times_transposed(grad_branch, back_out).astype(jnp.bfloat16)
    grad_attended = grad_attended.reshape(seqs_here, block_rows, model_width)
    delta_rows = jnp.einsum(
        "sqhd,sqhd->shq", shaped(grad_attended.astype(jnp.float32)), shaped(attended)
    )
    turn_count = lax.axis_size("ctx")
    own_query_grad, own_key_grad, own_value_grad = pair_grads(
        queries, grad_attended, log_total, delta_rows, key_rows, values, HEADS
    )

    def key_turn(turn_index, running):
        key_pair, key_grads, query_grads = running
        key_pair = shifted(key_pair, "ctx", 1)
        key_grads = pass_key_grads(key_grads)
        part_query, part_key, part_value = pair_grads(
            queries, grad_attended, log_total, delta_rows, key_pair[0], key_pair[1], HEADS
        )
        return (key_pair, key_grads + jnp.stack([part_key, part_value]), query_grads + part_query)

    start_state = (
        jnp.stack([key_rows, values]),
        jnp.stack([own_key_grad, own_value_grad]),
        own_query_grad,
    )
    _, key_grads, grad_queries = lax.fori_loop(1, turn_count, key_turn, start_state)
    key_grads = pass_key_grads(key_grads)
    grad_keys = key_grads[0]
    grad_values = key_grads[1]
    grad_queries = unrotate(shaped(grad_queries), cos_table, sin_table).reshape(
        seqs_here * block_rows, model_width
    )
    grad_keys = unrotate(shaped(grad_keys), cos_table, sin_table).reshape(
        seqs_here * block_rows, model_width
    )
    grad_projected = jnp.concatenate(
        [grad_queries, grad_keys, grad_values.reshape(seqs_here * block_rows, model_width)], axis=-1
    ).astype(jnp.bfloat16)
    grad_qkv = contract_rows(first_in, grad_projected)
    grad_first = times_transposed(grad_projected, back_qkv)
    grad_input_norm, grad_attn_gain = norm_back(grad_first, normed_one, rstd_one, back_attn_gain)
    tokens_grad = (
        (grad_middle + grad_input_norm)
        .astype(jnp.bfloat16)
        .reshape(seqs_here, block_rows, model_width)
    )
    owned = (
        lax.psum_scatter(
            grad_qkv.astype(jnp.bfloat16), "wsh", scatter_dimension=0, tiled=True
        ).astype(jnp.float32),
        lax.psum_scatter(
            grad_out.astype(jnp.bfloat16), "wsh", scatter_dimension=0, tiled=True
        ).astype(jnp.float32),
        lax.psum_scatter(
            grad_in.astype(jnp.bfloat16), "wsh", scatter_dimension=0, tiled=True
        ).astype(jnp.float32),
        lax.psum_scatter(
            grad_mlp.astype(jnp.bfloat16), "wsh", scatter_dimension=0, tiled=True
        ).astype(jnp.float32),
        lax.psum_scatter(
            grad_attn_gain.astype(jnp.bfloat16), "wsh", scatter_dimension=0, tiled=True
        ).astype(jnp.float32),
        lax.psum_scatter(
            grad_mlp_gain.astype(jnp.bfloat16), "wsh", scatter_dimension=0, tiled=True
        ).astype(jnp.float32),
    )
    summed = lax.psum((owned[0], owned[1], owned[2], owned[3], owned[4], owned[5]), ("seq", "ctx"))
    return (
        layer_out.reshape(seqs_here, block_rows, model_width),
        tokens_grad,
        summed[0],
        summed[1],
        summed[2],
        summed[3],
        summed[4],
        summed[5],
    )


def solution(mesh):
    placed = (
        P(("seq", "wsh"), "ctx", None),
        P("wsh", None),
        P("wsh", None),
        P("wsh", None),
        P("wsh", None),
        P("wsh"),
        P("wsh"),
        P(("seq", "wsh"), "ctx", None),
    )
    return jax.shard_map(
        local,
        mesh=mesh,
        in_specs=placed,
        out_specs=(
            P(("seq", "wsh"), "ctx", None),
            P(("seq", "wsh"), "ctx", None),
            P("wsh", None),
            P("wsh", None),
            P("wsh", None),
            P("wsh", None),
            P("wsh"),
            P("wsh"),
        ),
        check_vma=False,
    )
```

profile of v0, /device:TPU:0, one launch (start us, length us, event | category | flops | bytes accessed | tf_op | source)
XLA Modules:
  0.0 775.8 jit_solution(3231144598718454828)
XLA Ops:
  10.3 14.7 %all-gather.10.cloned.1.call-done = bf16[768,2304]{1,0:T(8,128)(2,1)} async-done(((bf16[384,2304]{1,0:T(8,128)(2,1)}), bf16[768,2304]{1,0:T(8,128)(2,1)}) %all-gather.10.cloned.1.call-update) | async-done | bytes 3538960 | tf_op jit(solution)/shard_map/all_gather | solution.py:183
  33.8 40.2 %all-gather.20.cloned.1.call-done = bf16[1024,768]{1,0:T(8,128)(2,1)} async-done(((bf16[128,768]{1,0:T(8,128)(2,1)}), bf16[1024,768]{1,0:T(8,128)(2,1)}) %all-gather.20.cloned.1.call-update) | async-done | bytes 1572880 | tf_op jit(solution)/shard_map/all_gather | solution.py:100
  74.0 46.8 %all-gather.12.cloned.1.call-done = bf16[1,1024,768]{1,2,0:T(8,128)(2,1)} async-done(((bf16[1,128,768]{1,2,0:T(8,128)(2,1)}), bf16[1,1024,768]{1,2,0:T(8,128)(2,1)}) %all-gather.12.cloned.1.call-update) | async-done | bytes 1572880 | tf_op jit(solution)/shard_map/all_gather | solution.py:99
  120.8 9.6 %while.33 = (s32[]{:T(128)}, f32[1,12,128]{2,1,0:T(8,128)S(1)}, f32[1,12,128]{2,1,0:T(8,128)S(1)}, f32[1,12,128,64]{2,3,1,0:T(8,128)S(1)}, bf16[1,1024,768]{1,2,...) while((s32[]{:T(128)}, f32[1,12,128]{2,1,0:T(8,128)S(1)}, ...), condition=%wide.region_5.0_spmd.clone, body=%wide.region_2.0_spmd.clone.sunk | while | flops 207922176 | bytes 16810168 | solution.py:128
  132.4 12.5 %all-gather.16.cloned.1.call-done = bf16[768,2304]{1,0:T(8,128)(2,1)} async-done(((bf16[384,2304]{1,0:T(8,128)(2,1)}), bf16[768,2304]{1,0:T(8,128)(2,1)}) %all-gather.16.cloned.1.call-update) | async-done | bytes 3538960 | tf_op jit(solution)/shard_map/all_gather | solution.py:185
  147.6 10.0 %all-gather.18.cloned.1.call-done = bf16[1152,768]{1,0:T(8,128)(2,1)} async-done(((bf16[576,768]{1,0:T(8,128)(2,1)}), bf16[1152,768]{1,0:T(8,128)(2,1)}) %all-gather.18.cloned.1.call-update) | async-done | bytes 1769488 | tf_op jit(solution)/shard_map/all_gather | solution.py:186
  157.6 3.3 add_convert_fusion
  177.8 3.0 convolution_convert_fusion
  180.8 146.4 %while.32 = (s32[]{:T(128)}, bf16[2,1,128,768]{2,3,1,0:T(8,128)(2,1)}, bf16[2,1,128,768]{2,3,1,0:T(8,128)(2,1)}, f32[1,128,768]{1,2,0:T(8,128)S(1)}, bf16[1,128,...) while((s32[]{:T(128)}, ...), condition=%wide.region_11.0_spmd, body=%wide.region_10.0_spmd.sunk | while | flops 128090112 | bytes 13578413 | solution.py:271
  184.1 11.6 %collective-permute-done = bf16[2,1,128,768]{2,3,1,0:T(8,128)(2,1)S(1)} collective-permute-done((bf16[2,1,128,768]{2,3,1,0:T(8,128)(2,1)}, bf16[2,1,128,768]{2,3,1,0:T(8,128)(2,1)S(1)}, u32[]{:S(2)}, u32[]{:S(2)}) %collective-permute-start) | collective-permute-done | bytes 393248 | tf_op jit(solution)/shard_map/while/body/eval_jaxpr/ppermute | solution.py:20
  198.3 5.3 collective-permute-done.1
  205.8 13.6 %collective-permute-done = bf16[2,1,128,768]{2,3,1,0:T(8,128)(2,1)S(1)} collective-permute-done((bf16[2,1,128,768]{2,3,1,0:T(8,128)(2,1)}, bf16[2,1,128,768]{2,3,1,0:T(8,128)(2,1)S(1)}, u32[]{:S(2)}, u32[]{:S(2)}) %collective-permute-start) | collective-permute-done | bytes 393248 | tf_op jit(solution)/shard_map/while/body/eval_jaxpr/ppermute | solution.py:20
  222.0 4.4 collective-permute-done.1
  227.2 15.0 %collective-permute-done = bf16[2,1,128,768]{2,3,1,0:T(8,128)(2,1)S(1)} collective-permute-done((bf16[2,1,128,768]{2,3,1,0:T(8,128)(2,1)}, bf16[2,1,128,768]{2,3,1,0:T(8,128)(2,1)S(1)}, u32[]{:S(2)}, u32[]{:S(2)}) %collective-permute-start) | collective-permute-done | bytes 393248 | tf_op jit(solution)/shard_map/while/body/eval_jaxpr/ppermute | solution.py:20
  244.7 3.5 collective-permute-done.1
  249.1 15.0 %collective-permute-done = bf16[2,1,128,768]{2,3,1,0:T(8,128)(2,1)S(1)} collective-permute-done((bf16[2,1,128,768]{2,3,1,0:T(8,128)(2,1)}, bf16[2,1,128,768]{2,3,1,0:T(8,128)(2,1)S(1)}, u32[]{:S(2)}, u32[]{:S(2)}) %collective-permute-start) | collective-permute-done | bytes 393248 | tf_op jit(solution)/shard_map/while/body/eval_jaxpr/ppermute | solution.py:20
  270.0 15.0 %collective-permute-done = bf16[2,1,128,768]{2,3,1,0:T(8,128)(2,1)S(1)} collective-permute-done((bf16[2,1,128,768]{2,3,1,0:T(8,128)(2,1)}, bf16[2,1,128,768]{2,3,1,0:T(8,128)(2,1)S(1)}, u32[]{:S(2)}, u32[]{:S(2)}) %collective-permute-start) | collective-permute-done | bytes 393248 | tf_op jit(solution)/shard_map/while/body/eval_jaxpr/ppermute | solution.py:20
  290.0 14.0 %collective-permute-done = bf16[2,1,128,768]{2,3,1,0:T(8,128)(2,1)S(1)} collective-permute-done((bf16[2,1,128,768]{2,3,1,0:T(8,128)(2,1)}, bf16[2,1,128,768]{2,3,1,0:T(8,128)(2,1)S(1)}, u32[]{:S(2)}, u32[]{:S(2)}) %collective-permute-start) | collective-permute-done | bytes 393248 | tf_op jit(solution)/shard_map/while/body/eval_jaxpr/ppermute | solution.py:20
  309.1 13.1 %collective-permute-done = bf16[2,1,128,768]{2,3,1,0:T(8,128)(2,1)S(1)} collective-permute-done((bf16[2,1,128,768]{2,3,1,0:T(8,128)(2,1)}, bf16[2,1,128,768]{2,3,1,0:T(8,128)(2,1)S(1)}, u32[]{:S(2)}, u32[]{:S(2)}) %collective-permute-start) | collective-permute-done | bytes 393248 | tf_op jit(solution)/shard_map/while/body/eval_jaxpr/ppermute | solution.py:20
  327.2 10.7 %collective-permute-done.2 = bf16[2,1,128,768]{2,3,1,0:T(8,128)(2,1)S(1)} collective-permute-done((bf16[2,1,128,768]{2,3,1,0:T(8,128)(2,1)}, bf16[2,1,128,768]{2,3,1,0:T(8,128)(2,1)S(1)}, u32[]{:S(2)}, u32[]{:S(2)}) %collective-permute-start.2) | collective-permute-done | bytes 393248 | tf_op jit(solution)/shard_map/ppermute | solution.py:20
  338.2 3.0 convolution_convert_fusion.1
  343.1 3.0 fusion.31
  346.1 3.6 fusion.52
  353.3 415.6 %all-reduce.5 = (f32[384,2304]{1,0:T(8,128)}, f32[384,768]{1,0:T(8,128)}, f32[384,2304]{1,0:T(8,128)}, f32[576,768]{1,0:T(8,128)}, f32[384]{0:T(512)}, /*index=5*/f32[384]{0:T(512)}) all-reduce(bf16[384,2304]{1,0:T(8,128)(2,1)} %reduce-scatter.5.cloned.1.call-done, ...), channel_id=1, replica_groups=mesh['seq'=2,'ctx'=8,'wsh'=2] {'seq','ctx'}, use_global_device_ids=true, to_apply=%region_15.0 | all-reduce | flops 2507520 | bytes 15046656 | tf_op jit(solution)/shard_map/psum | solution.py:312
  (271 shorter events, 82.9 us)
Async XLA Ops:
  7.2 17.8 %all-gather.10.cloned.1.call-start = ((), (), s32[]{:S(2)}) async-start(), calls=%async_computation.4 | async-start | bytes 5308416 | tf_op jit(solution)/shard_map/all_gather | solution.py:183
  7.9 66.1 %all-gather.20.cloned.1.call-start = ((), (), s32[]{:S(2)}) async-start(), calls=%async_computation.13 | async-start | bytes 1769472 | tf_op jit(solution)/shard_map/all_gather | solution.py:100
  28.5 92.3 %all-gather.12.cloned.1.call-start = ((), (), s32[]{:S(2)}) async-start(), calls=%async_computation.5 | async-start | bytes 1769472 | tf_op jit(solution)/shard_map/all_gather | solution.py:99
  29.8 100.6 %all-gather.14.cloned.1.call-start = ((), (), s32[]{:S(2)}) async-start(), calls=%async_computation.6 | async-start | bytes 1769472 | tf_op jit(solution)/shard_map/all_gather | solution.py:184
  30.4 114.5 %all-gather.16.cloned.1.call-start = ((), (), s32[]{:S(2)}) async-start(), calls=%async_computation.7 | async-start | bytes 5308416 | tf_op jit(solution)/shard_map/all_gather | solution.py:185
  31.0 126.6 %all-gather.18.cloned.1.call-start = ((), (), s32[]{:S(2)}) async-start(), calls=%async_computation.8 | async-start | bytes 2654208 | tf_op jit(solution)/shard_map/all_gather | solution.py:186
  31.6 321.7 %reduce-scatter.7.cloned.1.call-start = ((), (), s32[]{:S(2)}) async-start(), calls=%async_computation.10 | async-start | bytes 1769472 | tf_op jit(solution)/shard_map/reduce_scatter | solution.py:296
  165.9 187.4 %reduce-scatter.11.cloned.1.call-start = ((), (), s32[]{:S(2)}) async-start(), calls=%async_computation.12 | async-start | bytes 2654208 | tf_op jit(solution)/shard_map/reduce_scatter | solution.py:302
  167.9 185.4 %reduce-scatter.9.cloned.1.call-start = ((), (), s32[]{:S(2)}) async-start(), calls=%async_computation.11 | async-start | bytes 5308416 | tf_op jit(solution)/shard_map/reduce_scatter | solution.py:299
  180.8 172.5 %reduce-scatter.5.cloned.1.call-start = ((), (), s32[]{:S(2)}) async-start(), calls=%async_computation.9 | async-start | bytes 5308416 | tf_op jit(solution)/shard_map/reduce_scatter | solution.py:293
  180.9 14.9 %collective-permute-start = (bf16[2,1,128,768]{2,3,1,0:T(8,128)(2,1)}, bf16[2,1,128,768]{2,3,1,0:T(8,128)(2,1)S(1)}, u32[]{:S(2)}, u32[]{:S(2)}) collective-permute-start(bf16[2,1,128,768]{2,3,1,0:T(8,128)(2,1)} %get-tuple-element.475), channel_id=1, source_target_pairs={{14,0},{0,2},{2,4},{4,6},{6,8},{8,10},{10,12},{12,14},{15,1},{1,3}... | collective-permute-start | bytes 1179656 | tf_op jit(solution)/shard_map/while/body/eval_jaxpr/ppermute | solution.py:20
  182.7 21.0 %collective-permute-start.1 = (bf16[2,1,128,768]{2,3,1,0:T(8,128)(2,1)}, bf16[2,1,128,768]{2,3,1,0:T(8,128)(2,1)S(1)}, u32[]{:S(2)}, u32[]{:S(2)}) collective-permute-start(bf16[2,1,128,768]{2,3,1,0:T(8,128)(2,1)} %get-tuple-element.476), channel_id=1, source_target_pairs={{14,0},{0,2},{2,4},{4,6},{6,8},{8,10},{10,12},{12,14},{15,1},{1,3}... | collective-permute-start | bytes 1179656 | tf_op jit(solution)/shard_map/while/body/eval_jaxpr/ppermute | solution.py:20
  204.5 14.9 %collective-permute-start = (bf16[2,1,128,768]{2,3,1,0:T(8,128)(2,1)}, bf16[2,1,128,768]{2,3,1,0:T(8,128)(2,1)S(1)}, u32[]{:S(2)}, u32[]{:S(2)}) collective-permute-start(bf16[2,1,128,768]{2,3,1,0:T(8,128)(2,1)} %get-tuple-element.475), channel_id=1, source_target_pairs={{14,0},{0,2},{2,4},{4,6},{6,8},{8,10},{10,12},{12,14},{15,1},{1,3}... | collective-permute-start | bytes 1179656 | tf_op jit(solution)/shard_map/while/body/eval_jaxpr/ppermute | solution.py:20
  204.5 21.9 %collective-permute-start.1 = (bf16[2,1,128,768]{2,3,1,0:T(8,128)(2,1)}, bf16[2,1,128,768]{2,3,1,0:T(8,128)(2,1)S(1)}, u32[]{:S(2)}, u32[]{:S(2)}) collective-permute-start(bf16[2,1,128,768]{2,3,1,0:T(8,128)(2,1)} %get-tuple-element.476), channel_id=1, source_target_pairs={{14,0},{0,2},{2,4},{4,6},{6,8},{8,10},{10,12},{12,14},{15,1},{1,3}... | collective-permute-start | bytes 1179656 | tf_op jit(solution)/shard_map/while/body/eval_jaxpr/ppermute | solution.py:20
  227.2 15.0 %collective-permute-start = (bf16[2,1,128,768]{2,3,1,0:T(8,128)(2,1)}, bf16[2,1,128,768]{2,3,1,0:T(8,128)(2,1)S(1)}, u32[]{:S(2)}, u32[]{:S(2)}) collective-permute-start(bf16[2,1,128,768]{2,3,1,0:T(8,128)(2,1)} %get-tuple-element.475), channel_id=1, source_target_pairs={{14,0},{0,2},{2,4},{4,6},{6,8},{8,10},{10,12},{12,14},{15,1},{1,3}... | collective-permute-start | bytes 1179656 | tf_op jit(solution)/shard_map/while/body/eval_jaxpr/ppermute | solution.py:20
  227.2 21.0 %collective-permute-start.1 = (bf16[2,1,128,768]{2,3,1,0:T(8,128)(2,1)}, bf16[2,1,128,768]{2,3,1,0:T(8,128)(2,1)S(1)}, u32[]{:S(2)}, u32[]{:S(2)}) collective-permute-start(bf16[2,1,128,768]{2,3,1,0:T(8,128)(2,1)} %get-tuple-element.476), channel_id=1, source_target_pairs={{14,0},{0,2},{2,4},{4,6},{6,8},{8,10},{10,12},{12,14},{15,1},{1,3}... | collective-permute-start | bytes 1179656 | tf_op jit(solution)/shard_map/while/body/eval_jaxpr/ppermute | solution.py:20
  249.1 15.0 %collective-permute-start = (bf16[2,1,128,768]{2,3,1,0:T(8,128)(2,1)}, bf16[2,1,128,768]{2,3,1,0:T(8,128)(2,1)S(1)}, u32[]{:S(2)}, u32[]{:S(2)}) collective-permute-start(bf16[2,1,128,768]{2,3,1,0:T(8,128)(2,1)} %get-tuple-element.475), channel_id=1, source_target_pairs={{14,0},{0,2},{2,4},{4,6},{6,8},{8,10},{10,12},{12,14},{15,1},{1,3}... | collective-permute-start | bytes 1179656 | tf_op jit(solution)/shard_map/while/body/eval_jaxpr/ppermute | solution.py:20
  249.1 20.1 %collective-permute-start.1 = (bf16[2,1,128,768]{2,3,1,0:T(8,128)(2,1)}, bf16[2,1,128,768]{2,3,1,0:T(8,128)(2,1)S(1)}, u32[]{:S(2)}, u32[]{:S(2)}) collective-permute-start(bf16[2,1,128,768]{2,3,1,0:T(8,128)(2,1)} %get-tuple-element.476), channel_id=1, source_target_pairs={{14,0},{0,2},{2,4},{4,6},{6,8},{8,10},{10,12},{12,14},{15,1},{1,3}... | collective-permute-start | bytes 1179656 | tf_op jit(solution)/shard_map/while/body/eval_jaxpr/ppermute | solution.py:20
  270.0 15.0 %collective-permute-start = (bf16[2,1,128,768]{2,3,1,0:T(8,128)(2,1)}, bf16[2,1,128,768]{2,3,1,0:T(8,128)(2,1)S(1)}, u32[]{:S(2)}, u32[]{:S(2)}) collective-permute-start(bf16[2,1,128,768]{2,3,1,0:T(8,128)(2,1)} %get-tuple-element.475), channel_id=1, source_target_pairs={{14,0},{0,2},{2,4},{4,6},{6,8},{8,10},{10,12},{12,14},{15,1},{1,3}... | collective-permute-start | bytes 1179656 | tf_op jit(solution)/shard_map/while/body/eval_jaxpr/ppermute | solution.py:20
  270.0 19.2 %collective-permute-start.1 = (bf16[2,1,128,768]{2,3,1,0:T(8,128)(2,1)}, bf16[2,1,128,768]{2,3,1,0:T(8,128)(2,1)S(1)}, u32[]{:S(2)}, u32[]{:S(2)}) collective-permute-start(bf16[2,1,128,768]{2,3,1,0:T(8,128)(2,1)} %get-tuple-element.476), channel_id=1, source_target_pairs={{14,0},{0,2},{2,4},{4,6},{6,8},{8,10},{10,12},{12,14},{15,1},{1,3}... | collective-permute-start | bytes 1179656 | tf_op jit(solution)/shard_map/while/body/eval_jaxpr/ppermute | solution.py:20
  290.0 14.0 %collective-permute-start = (bf16[2,1,128,768]{2,3,1,0:T(8,128)(2,1)}, bf16[2,1,128,768]{2,3,1,0:T(8,128)(2,1)S(1)}, u32[]{:S(2)}, u32[]{:S(2)}) collective-permute-start(bf16[2,1,128,768]{2,3,1,0:T(8,128)(2,1)} %get-tuple-element.475), channel_id=1, source_target_pairs={{14,0},{0,2},{2,4},{4,6},{6,8},{8,10},{10,12},{12,14},{15,1},{1,3}... | collective-permute-start | bytes 1179656 | tf_op jit(solution)/shard_map/while/body/eval_jaxpr/ppermute | solution.py:20
  290.0 18.2 %collective-permute-start.1 = (bf16[2,1,128,768]{2,3,1,0:T(8,128)(2,1)}, bf16[2,1,128,768]{2,3,1,0:T(8,128)(2,1)S(1)}, u32[]{:S(2)}, u32[]{:S(2)}) collective-permute-start(bf16[2,1,128,768]{2,3,1,0:T(8,128)(2,1)} %get-tuple-element.476), channel_id=1, source_target_pairs={{14,0},{0,2},{2,4},{4,6},{6,8},{8,10},{10,12},{12,14},{15,1},{1,3}... | collective-permute-start | bytes 1179656 | tf_op jit(solution)/shard_map/while/body/eval_jaxpr/ppermute | solution.py:20
  309.1 13.1 %collective-permute-start = (bf16[2,1,128,768]{2,3,1,0:T(8,128)(2,1)}, bf16[2,1,128,768]{2,3,1,0:T(8,128)(2,1)S(1)}, u32[]{:S(2)}, u32[]{:S(2)}) collective-permute-start(bf16[2,1,128,768]{2,3,1,0:T(8,128)(2,1)} %get-tuple-element.475), channel_id=1, source_target_pairs={{14,0},{0,2},{2,4},{4,6},{6,8},{8,10},{10,12},{12,14},{15,1},{1,3}... | collective-permute-start | bytes 1179656 | tf_op jit(solution)/shard_map/while/body/eval_jaxpr/ppermute | solution.py:20
  309.1 17.3 %collective-permute-start.1 = (bf16[2,1,128,768]{2,3,1,0:T(8,128)(2,1)}, bf16[2,1,128,768]{2,3,1,0:T(8,128)(2,1)S(1)}, u32[]{:S(2)}, u32[]{:S(2)}) collective-permute-start(bf16[2,1,128,768]{2,3,1,0:T(8,128)(2,1)} %get-tuple-element.476), channel_id=1, source_target_pairs={{14,0},{0,2},{2,4},{4,6},{6,8},{8,10},{10,12},{12,14},{15,1},{1,3}... | collective-permute-start | bytes 1179656 | tf_op jit(solution)/shard_map/while/body/eval_jaxpr/ppermute | solution.py:20
  (41 other events, 756.1 us)
Sparse Core Ops, SparseCore 0:
  9.6 15.3 all-gather.9
  28.6 45.3 all-gather.19
  76.7 44.0 all-gather.11
  122.2 7.4 all-gather.13
  131.0 13.8 all-gather.15
  146.3 11.2 all-gather.17
  166.0 9.8 reduce-scatter.6
  178.8 10.4 reduce-scatter.10
  192.2 12.5 reduce-scatter.8
  341.3 8.2 reduce-scatter.4
where the time goes:
time: 776 us
  blocking collectives  422 us (54%)
  waiting for transfers between devices  255 us (33%)
  matrix products  46 us (6%)
  local copies, waits for them, and re-layouts  18.6 us (2%)
  between operations  15.6 us (2%)
  other arithmetic  13.1 us (2%)
    psum x1, blocking collectives, local(): lax.psum((owned[0], owned[1], owned[2], owned[3], owned[4], owned[5]), ('...  416 us
    ppermute x15, waiting for transfers between devices, shifted(): return lax.ppermute(block, axis, route)  129 us
    all_gather x1, waiting for transfers between devices, forward_attention(): key_piece = lax.all_gather(key_rows, 'ctx', axis=1, tiled=True)  46.8 us
    all_gather x1, waiting for transfers between devices, forward_attention(): value_piece = lax.all_gather(values, 'ctx', axis=1, tiled=True)  40.2 us
  transfers between devices with their start and end apart: 25, of which 20 were waited for; matrix products, arithmetic and copies ran while one was open for 8% of the time, Pallas kernels for 0%

commit v1 on v0

v1 whole, which is shorter than its diff:
```python
from functools import partial

import jax
import jax.numpy as jnp
from jax import lax
from jax.experimental import pallas as pl
from jax.experimental.pallas import tpu as pltpu
from jax.sharding import PartitionSpec as P

HEADS = 12
FF = 1152
EPSILON = 1e-05
THETA = 160000.0
LANES = 128
PIECE = 2 * HEADS
NORMED_AT = 640
ATTENDED_AT = 1024
HALVES_WIDTH = 1408
MIB = 1 << 20
BF16 = jnp.bfloat16
F32 = jnp.float32


def bits_of(axis):
    return [(axis, k) for k in range((lax.axis_size(axis) - 1).bit_length())]


def my_bit(axis, k):
    return (lax.axis_index(axis) >> k) & 1


def flip(block, first, second):
    n_seq, n_ctx = lax.axis_size("seq"), lax.axis_size("ctx")
    route = []
    for s in range(n_seq):
        for t in range(n_ctx):
            for core, (axis, k) in enumerate((first, second)):
                s2, t2 = (s ^ (1 << k), t) if axis == "seq" else (s, t ^ (1 << k))
                route.append(((s * n_ctx + t) * 2 + core, (s2 * n_ctx + t2) * 2 + core))
    return lax.ppermute(block, ("seq", "ctx", "wsh"), route)


def swap_cores(block):
    return lax.ppermute(block, "wsh", [(0, 1), (1, 0)])


def gather_orders():
    bits = bits_of("ctx")
    return bits[::-1], bits[:1] + bits[:0:-1]


def gather_context(block):
    stages = list(zip(*gather_orders()))
    for first, second in stages[:-1]:
        block = jnp.concatenate([block, flip(block, first, second)], axis=0)
    return block, flip(block, *stages[-1])


def gathered_blocks():
    tables = []
    for order in gather_orders():
        slots = [0]
        for _, k in order:
            slots = slots + [slot | (1 << k) for slot in slots]
        tables.append(slots)
    mine = jnp.where(lax.axis_index("wsh") == 0, jnp.array(tables[0]), jnp.array(tables[1]))
    return mine ^ lax.axis_index("ctx")


def sum_orders():
    seq, ctx = bits_of("seq"), bits_of("ctx")
    return list(zip(seq + ctx[1:2] + ctx[:1] + ctx[2:], ctx[:2] + seq + ctx[2:]))


def stage_bit(first, second):
    return jnp.where(lax.axis_index("wsh") == 0, my_bit(*first), my_bit(*second))


def scatter_sum(rows):
    parts = [rows]
    for first, second in sum_orders():
        bit = stage_bit(first, second)
        half = parts[0].shape[0] // 2

        def side(which):
            cut = [lax.dynamic_slice_in_dim(part, which * half, half, 0) for part in parts]
            if len(cut) == 1:
                return cut[0]
            return (cut[0].astype(F32) + cut[1].astype(F32)).astype(BF16)

        away = side(1 - bit)
        parts = [side(bit), flip(away, first, second)]
    return (parts[0].astype(F32) + parts[1].astype(F32)).astype(BF16)


def gather_rows(rows):
    stages = sum_orders()[::-1]
    for first, second in stages[:-1]:
        bit = stage_bit(first, second)
        other = flip(rows, first, second)
        low = jnp.where(bit == 0, rows, other)
        high = jnp.where(bit == 0, other, rows)
        rows = jnp.concatenate([low, high], axis=0)
    return rows, flip(rows, *stages[-1]), stage_bit(*stages[-1])


def both_halves(block):
    other = swap_cores(block)
    core = lax.axis_index("wsh")
    return jnp.concatenate(
        [jnp.where(core == 0, block, other), jnp.where(core == 0, other, block)], axis=0
    )


def dot_nn(a, b):
    return lax.dot_general(a, b, (((1,), (0,)), ((), ())), preferred_element_type=F32)


def dot_nt(a, b):
    return lax.dot_general(a, b, (((1,), (1,)), ((), ())), preferred_element_type=F32)


def dot_tn(a, b):
    return lax.dot_general(a, b, (((0,), (0,)), ((), ())), preferred_element_type=F32)


def cost(flops, moved):
    return pl.CostEstimate(flops=int(flops), bytes_accessed=int(moved), transcendentals=0)


PARAMS = pltpu.CompilerParams(vmem_limit_bytes=40 * MIB)


def normalize(inputs):
    average = jnp.mean(inputs, axis=-1, keepdims=True)
    centred = inputs - average
    variance = jnp.mean(centred * centred, axis=-1, keepdims=True)
    rstd = lax.rsqrt(variance + EPSILON)
    return centred * rstd, rstd


def norm_back(grad_rows, normed, rstd, gain):
    scaled = grad_rows * gain
    inner = jnp.mean(scaled * normed, axis=-1, keepdims=True)
    return rstd * (scaled - jnp.mean(scaled, axis=-1, keepdims=True) - normed * inner)


def lane_of(shape):
    return lax.broadcasted_iota(jnp.int32, shape, len(shape) - 1)


def halves_swapped(vectors):
    first = (lane_of(vectors.shape) & 63) < 32
    return jnp.where(first, pltpu.roll(vectors, LANES - 32, 1), pltpu.roll(vectors, 32, 1))


def project_kernel(tokens, weights, gain, cos, sin, out):
    normed, _ = normalize(tokens[...].astype(F32))
    low = (normed * gain[...].astype(F32)).astype(BF16)
    width = tokens.shape[1]
    cos_rows, sin_rows = cos[...], sin[...]
    for part in range(3):
        columns = dot_nn(low, weights[:, part * width : (part + 1) * width])
        for j in range(width // LANES):
            piece = columns[:, j * LANES : (j + 1) * LANES]
            if part < 2:
                piece = piece * cos_rows + halves_swapped(piece) * sin_rows
            if part == 0:
                piece = piece * 0.125
            at = part * width + j * LANES
            out[:, at : at + LANES] = piece.astype(BF16)


def project(tokens, weights, gain, cos, sin):
    rows, width = tokens.shape
    step = min(rows, 256)
    return pl.pallas_call(
        project_kernel,
        grid=(rows // step,),
        in_specs=[
            pl.BlockSpec((step, width), lambda i: (i, 0)),
            pl.BlockSpec((width, 3 * width), lambda i: (0, 0)),
            pl.BlockSpec((1, width), lambda i: (0, 0)),
            pl.BlockSpec((step, LANES), lambda i: (i, 0)),
            pl.BlockSpec((step, LANES), lambda i: (i, 0)),
        ],
        out_specs=pl.BlockSpec((step, 3 * width), lambda i: (i, 0)),
        out_shape=jax.ShapeDtypeStruct((rows, 3 * width), BF16),
        compiler_params=PARAMS,
        cost_estimate=cost(6 * rows * width * width, 8 * rows * width),
        name="project",
    )(tokens, weights, gain, cos, sin)


def two_heads(block):
    first = lane_of(block.shape) < 64
    zero = jnp.zeros_like(block)
    return jnp.concatenate([jnp.where(first, block, zero), jnp.where(first, zero, block)], axis=0)


def one_pair(stacked):
    rows = stacked.shape[0] // 2
    return jnp.where(lane_of((rows, LANES)) < 64, stacked[:rows], stacked[rows:])


def column_pair(columns, at):
    lanes = lane_of(columns.shape)
    picked = [
        jnp.sum(jnp.where(lanes == at + k, columns, 0.0), axis=1, keepdims=True) for k in (0, 1)
    ]
    return jnp.concatenate(picked, axis=0)


def put_pair(ref, pair, values):
    rows = ref.shape[0]

    @pl.when(pair == 0)
    def _():
        ref[...] = jnp.zeros_like(ref)

    lanes = lane_of((rows, LANES))
    kept = jnp.where(lanes == 2 * pair, values[:rows], ref[...])
    ref[...] = jnp.where(lanes == 2 * pair + 1, values[rows:], kept)


def chunks_of(count):
    step = min(count, 1024)
    return [slice(at, at + step) for at in range(0, count, step)]


def attend_over(stacked, keys, values, peak, total, mixed):
    for at in chunks_of(keys.shape[0]):
        logits = dot_nt(stacked, keys[at, :])
        top = jnp.max(logits, axis=1, keepdims=True)
        if peak is None:
            weights = jnp.exp(logits - top)
            total = jnp.sum(weights, axis=1, keepdims=True)
            mixed = dot_nn(weights.astype(BF16), values[at, :])
        else:
            top = jnp.maximum(peak, top)
            weights = jnp.exp(logits - top)
            factor = jnp.exp(peak - top)
            total = total * factor + jnp.sum(weights, axis=1, keepdims=True)
            mixed = mixed * factor + dot_nn(weights.astype(BF16), values[at, :])
        peak = top
    return peak, total, mixed


def attend_first_kernel(queries, keys, values, out_mixed, out_peak, out_total):
    pair = pl.program_id(0)
    stacked = two_heads(queries[...])
    peak, total, mixed = attend_over(stacked, keys, values, None, None, None)
    out_mixed[...] = one_pair(mixed)
    put_pair(out_peak, pair, peak)
    put_pair(out_total, pair, total)


def attend_last_kernel(
    queries, keys, values, in_mixed, in_peak, in_total, attended, log_total
):
    pair = pl.program_id(0)
    stacked = two_heads(queries[...])
    peak = column_pair(in_peak[...], 2 * pair)
    total = column_pair(in_total[...], 2 * pair)
    mixed = jnp.concatenate([in_mixed[...]] * 2, axis=0)
    peak, total, mixed = attend_over(stacked, keys, values, peak, total, mixed)
    attended[...] = one_pair(mixed / total)
    put_pair(log_total, pair, peak + jnp.log(total))


def attend(halves, rows):
    count, width = halves[0].shape[0], halves[0].shape[1] // 3
    pairs = width // LANES
    queries = pl.BlockSpec((rows, LANES), lambda j: (0, j))
    shared = pl.BlockSpec((rows, LANES), lambda j: (0, 0))
    keys = pl.BlockSpec((count, LANES), lambda j: (0, pairs + j))
    values = pl.BlockSpec((count, LANES), lambda j: (0, 2 * pairs + j))
    wide = jax.ShapeDtypeStruct((rows, width), F32)
    thin = jax.ShapeDtypeStruct((rows, LANES), F32)
    work = cost(8 * rows * count * width, 6 * count * width)
    mixed, peak, total = pl.pallas_call(
        attend_first_kernel,
        grid=(pairs,),
        in_specs=[queries, keys, values],
        out_specs=[queries, shared, shared],
        out_shape=[wide, thin, thin],
        compiler_params=PARAMS,
        cost_estimate=work,
        name="attend_first",
    )(halves[0], halves[0], halves[0])
    return pl.pallas_call(
        attend_last_kernel,
        grid=(pairs,),
        in_specs=[queries, keys, values, queries, shared, shared],
        out_specs=[queries, shared],
        out_shape=[wide, thin],
        compiler_params=PARAMS,
        cost_estimate=work,
        name="attend_last",
    )(halves[0], halves[1], halves[1], mixed, peak, total)


def middle_kernel(
    core, tokens, attended, log_total, cotangent, w_out, w_in, w_mlp, gain,
    layer_out, own_halves, other_halves, whole,
    grad_middle, sent, logs_deltas, gain_grad,
):
    rows, width = tokens.shape
    first = core[0] == 0

    def put_halves(at, block):
        half = block.shape[1] // 2
        left, right = block[:, :half], block[:, half:]
        own_halves[:, at : at + half] = jnp.where(first, left, right)
        other_halves[:, at : at + half] = jnp.where(first, right, left)

    mixed = attended[...]
    mixed_low = mixed.astype(BF16)
    put_halves(ATTENDED_AT, mixed_low)
    middle = tokens[...].astype(F32) + dot_nn(mixed_low, w_out[...])
    normed, rstd = normalize(middle)
    gain_row = gain[...].astype(F32)
    second = (normed * gain_row).astype(BF16)
    put_halves(NORMED_AT, second)
    gate = dot_nn(second, w_in[:, :FF])
    up = dot_nn(second, w_in[:, FF:])
    cdf = 0.5 * (1.0 + lax.erf(gate * (0.5**0.5)))
    activated = gate * cdf
    hidden = (activated * up).astype(BF16)
    put_halves(0, hidden)
    layer_out[...] = (middle + dot_nn(hidden, w_mlp[...])).astype(BF16)
    upstream = cotangent[...]
    grad_hidden = dot_nt(upstream, w_mlp[...]).astype(BF16).astype(F32)
    density = jnp.exp(-0.5 * gate * gate) * 0.3989422804014327
    grad_gate = (grad_hidden * up * (cdf + gate * density)).astype(BF16)
    grad_up = (grad_hidden * activated).astype(BF16)
    whole[:, :FF] = grad_gate
    whole[:, FF : 2 * FF] = grad_up
    grad_second = dot_nt(grad_gate, w_in[:, :FF]) + dot_nt(grad_up, w_in[:, FF:])
    gain_grad[...] = jnp.sum(grad_second * normed, axis=0, keepdims=True)
    grad_mid = upstream.astype(F32) + norm_back(grad_second, normed, rstd, gain_row)
    grad_middle[...] = grad_mid
    branch = grad_mid.astype(BF16)
    whole[:, 2 * FF :] = branch
    grad_attended = dot_nt(branch, w_out[...]).astype(BF16)
    sent[:, :width] = grad_attended
    products = grad_attended.astype(F32) * mixed
    head = lax.broadcasted_iota(jnp.int32, (width, LANES), 0) // 64
    to_lane = (lane_of((width, LANES)) == head + HEADS).astype(F32)
    both = log_total[...] + lax.dot_general(
        products,
        to_lane,
        (((1,), (0,)), ((), ())),
        precision=lax.Precision.HIGHEST,
        preferred_element_type=F32,
    )
    logs_deltas[...] = both
    high = both.astype(BF16).astype(F32)
    rest = both - high
    mid = rest.astype(BF16).astype(F32)
    last = rest - mid
    packed = high + pltpu.roll(mid, PIECE, 1) + pltpu.roll(last, 2 * PIECE, 1)
    sent[:, width:] = packed.astype(BF16)


VMEM_SPEC = pl.BlockSpec(memory_space=pltpu.VMEM)


def middle_part(core, tokens, attended, log_total, cotangent, w_out, w_in, w_mlp, gain):
    rows, width = tokens.shape
    shapes = [
        ((rows, width), BF16),
        ((rows, HALVES_WIDTH), BF16),
        ((rows, HALVES_WIDTH), BF16),
        ((rows, 2 * FF + width), BF16),
        ((rows, width), F32),
        ((rows, width + LANES), BF16),
        ((rows, LANES), F32),
        ((1, width), F32),
    ]
    return pl.pallas_call(
        middle_kernel,
        in_specs=[pl.BlockSpec(memory_space=pltpu.SMEM)] + [VMEM_SPEC] * 8,
        out_shape=[jax.ShapeDtypeStruct(*shape) for shape in shapes],
        compiler_params=PARAMS,
        cost_estimate=cost(4 * rows * width * (2 * width + 6 * FF), 24 * MIB),
        name="middle",
    )(core, tokens, attended, log_total, cotangent, w_out, w_in, w_mlp, gain)


def rows_kernel(width, items, gained, *refs):
    out = refs[-1]
    at = 0
    for k, (left_lanes, right_lanes) in enumerate(items):
        left_own, left_other, right_own, right_other = refs[4 * k : 4 * k + 4]
        left = jnp.concatenate([left_own[:, left_lanes], left_other[:, left_lanes]], axis=0)
        made = left.shape[1]
        turned = left.T
        for start in range(right_lanes.start, right_lanes.stop, width):
            lanes = slice(start, start + width)
            right = jnp.concatenate([right_own[:, lanes], right_other[:, lanes]], axis=0)
            out[at : at + made, :] = dot_nn(turned, right).astype(BF16)
            at += made
    if at < out.shape[0]:
        out[at:, :] = jnp.zeros((out.shape[0] - at, width), BF16)
    if gained:
        own, other = refs[4 * len(items) : 4 * len(items) + 2]
        half = own.shape[1]
        tile = (16, half)
        top = lax.broadcasted_iota(jnp.int32, tile, 0) == 0
        row = jnp.broadcast_to(own[...] + other[...], tile)
        out[at : at + 16, :half] = jnp.where(top, row, 0.0).astype(BF16)


def grad_rows(width, pieces, items, gain=None):
    lanes, arrays, used = [], [], 0
    for left_own, left_other, left_lanes, right_own, right_other, right_lanes in items:
        arrays += [left_own, left_other, right_own, right_other]
        lanes.append((left_lanes, right_lanes))
        blocks = (right_lanes.stop - right_lanes.start) // width
        used += (left_lanes.stop - left_lanes.start) * blocks
    flops = 4 * items[0][0].shape[0] * used * width
    if gain is not None:
        arrays += gain
        used += 1
    unit = 8 * pieces
    total = (used + unit - 1) // unit * unit
    return pl.pallas_call(
        partial(rows_kernel, width, lanes, gain is not None),
        in_specs=[VMEM_SPEC] * len(arrays),
        out_shape=jax.ShapeDtypeStruct((total, width), BF16),
        compiler_params=PARAMS,
        cost_estimate=cost(flops, 4 * total * width),
        name="grad_rows",
    )(*arrays)


def unpack_kernel(places, gained, bit, own, other, *outs):
    half = own.shape[0]

    def put(low, high):
        at = 0
        for out, blocks in places:
            ref = outs[out]
            made = ref.shape[0]
            for k in range(blocks):
                columns = slice(k * low.shape[1], (k + 1) * low.shape[1])
                cut = min(max(half - at, 0), made)
                if cut > 0:
                    ref[:cut, columns] = low[at : at + cut, :].astype(F32)
                if cut < made:
                    start = at + cut - half
                    ref[cut:, columns] = high[start : start + made - cut, :].astype(F32)
                at += made
        if gained:
            ref = outs[-1]
            source, row = (low, at) if at < half else (high, at - half)
            ref[...] = source[row : row + 16, : ref.shape[1]].astype(F32)[:1]

    @pl.when(bit[0] == 0)
    def _():
        put(own, other)

    @pl.when(bit[0] != 0)
    def _():
        put(other, own)


def unpack(rows, shapes, gained=False):
    own, other, bit = gather_rows(scatter_sum(rows))
    width = own.shape[1]
    places = [(k, shape[1] // width) for k, shape in enumerate(shapes)]
    if gained:
        shapes = shapes + [(1, width // 2)]
    return pl.pallas_call(
        partial(unpack_kernel, places, gained),
        in_specs=[pl.BlockSpec(memory_space=pltpu.SMEM), VMEM_SPEC, VMEM_SPEC],
        out_shape=[jax.ShapeDtypeStruct(shape, F32) for shape in shapes],
        compiler_params=PARAMS,
        cost_estimate=cost(0, 12 * own.size),
        name="unpack",
    )(bit.reshape(1), own, other)


def unrotated(block, cos, sin):
    return block * cos - halves_swapped(block) * sin


def query_grad_kernel(
    queries, keys_a, values_a, keys_b, values_b, grads, logs_deltas, cos, sin, out
):
    pair = pl.program_id(0)
    rows = queries.shape[0]
    stacked = two_heads(queries[...])
    grads_two = two_heads(grads[...])
    logs = column_pair(logs_deltas[...], 2 * pair)
    deltas = column_pair(logs_deltas[...], HEADS + 2 * pair)
    total = jnp.zeros((2 * rows, LANES), F32)
    for keys, values in ((keys_a, values_a), (keys_b, values_b)):
        for at in chunks_of(keys.shape[0]):
            key_rows = keys[at, :]
            probs = jnp.exp(dot_nt(stacked, key_rows) - logs)
            grad_probs = dot_nt(grads_two, values[at, :])
            grad_scores = (probs * (grad_probs - deltas)).astype(BF16)
            total = total + dot_nn(grad_scores, key_rows)
    grad = one_pair(total) * 0.125
    out[...] = unrotated(grad, cos[...], sin[...]).astype(BF16)


def query_grads(halves, sent, logs_deltas, cos, sin, rows):
    count, width = halves[0].shape[0], halves[0].shape[1] // 3
    pairs = width // LANES
    queries = pl.BlockSpec((rows, LANES), lambda j: (0, j))
    shared = pl.BlockSpec((rows, LANES), lambda j: (0, 0))
    keys = pl.BlockSpec((count, LANES), lambda j: (0, pairs + j))
    values = pl.BlockSpec((count, LANES), lambda j: (0, 2 * pairs + j))
    return pl.pallas_call(
        query_grad_kernel,
        grid=(pairs,),
        in_specs=[queries, keys, values, keys, values, queries, shared, shared, shared],
        out_specs=queries,
        out_shape=jax.ShapeDtypeStruct((rows, width), BF16),
        compiler_params=PARAMS,
        cost_estimate=cost(24 * rows * count * width, 12 * count * width),
        name="query_grads",
    )(
        halves[0], halves[0], halves[0], halves[1], halves[1],
        sent, logs_deltas, cos, sin,
    )


def key_grads_over(pair, keys, values, queries, grads, packed, total_keys, total_values):
    rows = keys.shape[0]
    keys_two = two_heads(keys[...])
    values_two = two_heads(values[...])
    pick_shape = (8, LANES)
    row = lax.broadcasted_iota(jnp.int32, pick_shape, 0)
    lane = lane_of(pick_shape)
    wanted = 2 * pair + (row & 1) + jnp.where(row >= 2, HEADS, 0)
    held = (lane == wanted) | (lane == wanted + PIECE) | (lane == wanted + 2 * PIECE)
    pick = jnp.where(held, 1.0, 0.0).astype(BF16)
    for at in chunks_of(queries.shape[0]):
        query_rows, grad_rows_ = queries[at, :], grads[at, :]
        picked = dot_nt(pick, packed[at, :])
        shape = (rows, query_rows.shape[0])
        logs, deltas = (
            jnp.concatenate(
                [jnp.broadcast_to(picked[k : k + 1], shape) for k in (base, base + 1)], axis=0
            )
            for base in (0, 2)
        )
        probs = jnp.exp(dot_nt(keys_two, query_rows) - logs)
        grad_probs = dot_nt(values_two, grad_rows_)
        grad_scores = (probs * (grad_probs - deltas)).astype(BF16)
        add_values = dot_nn(probs.astype(BF16), grad_rows_)
        add_keys = dot_nn(grad_scores, query_rows)
        total_values = add_values if total_values is None else total_values + add_values
        total_keys = add_keys if total_keys is None else total_keys + add_keys
    return total_keys, total_values


def key_first_kernel(keys, values, queries, grads, packed, out_keys, out_values):
    pair = pl.program_id(0)
    grad_k, grad_v = key_grads_over(pair, keys, values, queries, grads, packed, None, None)
    out_keys[...] = one_pair(grad_k)
    out_values[...] = one_pair(grad_v)


def key_last_kernel(
    keys, values, queries, grads, packed, first_keys, first_values, cos, sin, out_keys, out_values
):
    pair = pl.program_id(0)
    grad_k, grad_v = key_grads_over(pair, keys, values, queries, grads, packed, None, None)
    grad_k = one_pair(grad_k) + first_keys[...]
    out_keys[...] = unrotated(grad_k, cos[...], sin[...]).astype(BF16)
    out_values[...] = (one_pair(grad_v) + first_values[...]).astype(BF16)


def key_grads(halves, sent_halves, cos, sin, rows):
    count, width = halves[0].shape[0], halves[0].shape[1] // 3
    pairs = width // LANES
    keys = pl.BlockSpec((rows, LANES), lambda j: (0, pairs + j))
    values = pl.BlockSpec((rows, LANES), lambda j: (0, 2 * pairs + j))
    queries = pl.BlockSpec((count, LANES), lambda j: (0, j))
    packed = pl.BlockSpec((count, LANES), lambda j: (0, pairs))
    own = pl.BlockSpec((rows, LANES), lambda j: (0, j))
    shared = pl.BlockSpec((rows, LANES), lambda j: (0, 0))
    work = cost(16 * rows * count * width, 6 * count * width)
    first = pl.pallas_call(
        key_first_kernel,
        grid=(pairs,),
        in_specs=[keys, values, queries, queries, packed],
        out_specs=[own, own],
        out_shape=[jax.ShapeDtypeStruct((rows, width), F32)] * 2,
        compiler_params=PARAMS,
        cost_estimate=work,
        name="key_grads_first",
    )(halves[0], halves[0], halves[0], sent_halves[0], sent_halves[0])
    return pl.pallas_call(
        key_last_kernel,
        grid=(pairs,),
        in_specs=[keys, values, queries, queries, packed, own, own, shared, shared],
        out_specs=[own, own],
        out_shape=[jax.ShapeDtypeStruct((rows, width), BF16)] * 2,
        compiler_params=PARAMS,
        cost_estimate=work,
        name="key_grads_last",
    )(
        halves[0], halves[0], halves[1], sent_halves[1], sent_halves[1],
        first[0], first[1], cos, sin,
    )


def last_kernel(tokens, grad_middle, grad_q, grad_k, grad_v, weights, gain, out, gain_grad):
    width = tokens.shape[1]
    normed, rstd = normalize(tokens[...].astype(F32))
    grad_first = dot_nt(grad_q[...], weights[:, :width])
    grad_first = grad_first + dot_nt(grad_k[...], weights[:, width : 2 * width])
    grad_first = grad_first + dot_nt(grad_v[...], weights[:, 2 * width :])
    gain_grad[...] = jnp.sum(grad_first * normed, axis=0, keepdims=True)
    back = norm_back(grad_first, normed, rstd, gain[...].astype(F32))
    out[...] = (grad_middle[...] + back).astype(BF16)


def last_part(tokens, grad_middle, grad_q, grad_k, grad_v, weights, gain):
    rows, width = tokens.shape
    return pl.pallas_call(
        last_kernel,
        in_specs=[VMEM_SPEC] * 7,
        out_shape=[
            jax.ShapeDtypeStruct((rows, width), BF16),
            jax.ShapeDtypeStruct((1, width), F32),
        ],
        compiler_params=PARAMS,
        cost_estimate=cost(6 * rows * width * width, 8 * MIB),
        name="last",
    )(tokens, grad_middle, grad_q, grad_k, grad_v, weights, gain)


def rotary_tables(positions, head_dim):
    half = head_dim // 2
    inverse = jnp.power(F32(THETA), -(jnp.arange(half, dtype=F32) * (2.0 / head_dim)))
    angles = positions[:, None] * inverse[None, :]
    cos, sin = jnp.cos(angles), jnp.sin(angles)
    return (
        jnp.concatenate([cos, cos, cos, cos], axis=1),
        jnp.concatenate([-sin, sin, -sin, sin], axis=1),
    )


def local(tokens, w_qkv, w_out, w_in, w_mlp, gain_attn, gain_mlp, cotangent):
    seqs_here, rows, width = tokens.shape
    half, half_ff = width // 2, FF // 2
    core = lax.axis_index("wsh")
    own = tokens.reshape(rows, width)
    upstream = cotangent.reshape(rows, width)
    pieces = lax.axis_size("seq") * lax.axis_size("ctx")

    gathered = gather_context(own)
    full_qkv = both_halves(w_qkv)
    gains = jnp.stack([gain_attn, gain_mlp])
    gains_other = swap_cores(gains)
    gains_all = jnp.concatenate(
        [jnp.where(core == 0, gains, gains_other), jnp.where(core == 0, gains_other, gains)], axis=1
    )
    attn_gain, mlp_gain = gains_all[:1], gains_all[1:]
    full_out = both_halves(w_out)
    full_in = both_halves(w_in)
    full_mlp = both_halves(w_mlp)
    upstream_other = swap_cores(upstream)
    first_in = (normalize(own.astype(F32))[0] * attn_gain.astype(F32)).astype(BF16)
    first_own = lax.dynamic_slice_in_dim(first_in, core * half, half, 1)
    first_other = swap_cores(lax.dynamic_slice_in_dim(first_in, (1 - core) * half, half, 1))

    blocks = gathered_blocks()
    positions = (blocks[:, None] * rows + jnp.arange(rows, dtype=jnp.int32)[None, :]).reshape(-1)
    cos, sin = rotary_tables(positions.astype(F32), 64)
    own_cos, own_sin = cos[:rows], sin[:rows]
    count = gathered[0].shape[0]
    halves = [
        project(
            part, full_qkv, attn_gain,
            cos[k * count : (k + 1) * count], sin[k * count : (k + 1) * count],
        )
        for k, part in enumerate(gathered)
    ]

    attended, log_total = attend(halves, rows)
    (
        layer_out, own_halves, other_halves, whole,
        grad_middle, sent, logs_deltas, gain_mlp_part,
    ) = middle_part(
        core.reshape(1), own, attended, log_total, upstream,
        full_out, full_in, full_mlp, mlp_gain,
    )

    def gain_pair(part):
        mine = lax.dynamic_slice_in_dim(part, core * half, half, 1)
        theirs = lax.dynamic_slice_in_dim(part, (1 - core) * half, half, 1)
        return [mine, swap_cores(theirs)]

    sent_halves = gather_context(sent)
    other_halves = swap_cores(other_halves)
    whole_other = swap_cores(whole)

    mlp_rows = grad_rows(
        width,
        pieces,
        [(own_halves, other_halves, slice(0, half_ff), upstream, upstream_other, slice(0, width))],
        gain_pair(gain_mlp_part),
    )
    in_rows = grad_rows(
        width,
        pieces,
        [
            (
                own_halves, other_halves, slice(NORMED_AT, NORMED_AT + half),
                whole, whole_other, slice(0, 2 * FF),
            )
        ],
    )
    grad_q = query_grads(halves, sent, logs_deltas, own_cos, own_sin, rows)
    out_rows = grad_rows(
        width,
        pieces,
        [
            (
                own_halves, other_halves, slice(ATTENDED_AT, ATTENDED_AT + half),
                whole, whole_other, slice(2 * FF, 2 * FF + width),
            ),
            (
                first_own, first_other, slice(0, half),
                grad_q, swap_cores(grad_q), slice(0, width),
            ),
        ],
    )
    grad_k, grad_v = key_grads(halves, sent_halves, own_cos, own_sin, rows)
    tokens_grad, gain_attn_part = last_part(
        own, grad_middle, grad_q, grad_k, grad_v, full_qkv, attn_gain
    )
    key_rows = grad_rows(
        width,
        pieces,
        [
            (first_own, first_other, slice(0, half), grad_k, swap_cores(grad_k), slice(0, width)),
            (first_own, first_other, slice(0, half), grad_v, swap_cores(grad_v), slice(0, width)),
        ],
        gain_pair(gain_attn_part),
    )

    mlp_grad, gain_mlp_grad = unpack(mlp_rows, [(half_ff, width)], True)
    (in_grad,) = unpack(in_rows, [(half, 2 * FF)])
    out_grad, q_grad = unpack(out_rows, [(half, width), (half, width)])
    kv_grad, gain_attn_grad = unpack(key_rows, [(half, 2 * width)], True)
    return (
        layer_out.reshape(seqs_here, rows, width),
        tokens_grad.reshape(seqs_here, rows, width),
        jnp.concatenate([q_grad, kv_grad], axis=1),
        out_grad,
        in_grad,
        mlp_grad,
        gain_attn_grad.reshape(half),
        gain_mlp_grad.reshape(half),
    )


def solution(mesh):
    placed = (
        P(("seq", "wsh"), "ctx", None),
        P("wsh", None),
        P("wsh", None),
        P("wsh", None),
        P("wsh", None),
        P("wsh"),
        P("wsh"),
        P(("seq", "wsh"), "ctx", None),
    )
    return jax.shard_map(
        local,
        mesh=mesh,
        in_specs=placed,
        out_specs=(
            P(("seq", "wsh"), "ctx", None),
            P(("seq", "wsh"), "ctx", None),
            P("wsh", None),
            P("wsh", None),
            P("wsh", None),
            P("wsh", None),
            P("wsh"),
            P("wsh"),
        ),
        check_vma=False,
    )
```

time: 776 us -> 246 us (0.32)
  blocking collectives: 422 us -> 0 us
  waiting for transfers between devices: 255 us -> 109 us
  starting transfers between devices: 5.23 us -> 53 us
  matrix products: 46 us -> 0 us
  Pallas kernels: 0 us -> 44.5 us
  between operations: 15.6 us -> 1.59 us
    psum x1 -> x0, blocking collectives: 416 us -> none  [local(): lax.psum((owned[0], owned[1], owned[2], owned[3], owned[4], owned[5]), ('...]
    all_gather x6 -> x0, waiting for transfers between devices: 124 us -> none  [the longest x1 46.8 us: forward_attention(): key_piece = lax.all_gather(key_rows, 'ctx', axis=1, tiled=True)]
    ppermute x15 -> x52, starting transfers between devices: 4.65 us -> 53 us  [the longest x38 49.6 us: flip(): return lax.ppermute(block, ('seq', 'ctx', 'wsh'), route)]
    dot_general x56 -> x0, matrix products: 46 us -> none  [the longest x4 10.1 us: times_transposed(): lax.dot_general(left_rows, right_rows, (((1,), (1,)), ((), ())), preferre...]
    pallas_call x0 -> x17, Pallas kernels: none -> 44.5 us  [the longest x4 8.01 us: unpack(): pl.pallas_call(partial(unpack_kernel, places, gained), in_specs=[pl.Block...]
    ppermute x15 -> x52, waiting for transfers between devices: 129 us -> 109 us  [the longest x38 109 us: flip(): return lax.ppermute(block, ('seq', 'ctx', 'wsh'), route)]
    unnamed x83 -> x84, local copies, waits for them, and re-layouts: 1.85 us -> 14 us
  transfers between devices with their start and end apart: 25 -> 52, of which waited for: 20 -> 22; matrix products, arithmetic and copies ran while one was open for 8% -> 7% of each run, Pallas kernels for 0% -> 17%
where the time goes in v1:
time: 246 us; the launch traced here: 245 us
  waiting for transfers between devices  109 us (44%)
  starting transfers between devices  53 us (22%)
  Pallas kernels  44.5 us (18%)
  other arithmetic  20.2 us (8%)
  local copies, waits for them, and re-layouts  16.5 us (7%)
    ppermute x38, waiting for transfers between devices, flip(): return lax.ppermute(block, ('seq', 'ctx', 'wsh'), route)  109 us
    ppermute x38, starting transfers between devices, flip(): return lax.ppermute(block, ('seq', 'ctx', 'wsh'), route)  49.6 us
    unnamed x84, local copies, waits for them, and re-layouts  14 us
    pallas_call x4, Pallas kernels, unpack(): pl.pallas_call(partial(unpack_kernel, places, gained), in_specs=[pl.Block...  8.01 us
    pallas_call x2, Pallas kernels, project(): pl.pallas_call(project_kernel, grid=(rows // step,), in_specs=[pl.BlockSp...  5.95 us
    pallas_call x1, Pallas kernels, query_grads(): pl.pallas_call(query_grad_kernel, grid=(pairs,), in_specs=[queries, keys,...  5.41 us
    pallas_call x1, Pallas kernels, middle_part(): pl.pallas_call(middle_kernel, in_specs=[pl.BlockSpec(memory_space=pltpu.S...  5.12 us
  transfers between devices with their start and end apart: 52, of which 22 were waited for; matrix products, arithmetic and copies ran while one was open for 7% of the time, Pallas kernels for 17%

profile of v1, /device:TPU:0, one launch (start us, length us, event | category | flops | bytes accessed | tf_op | source)
XLA Modules:
  0.0 245.0 jit_solution(4729344228744215559)
XLA Ops:
  2.5 3.7 %collective-permute-start = (bf16[128,768]{1,0:T(8,128)(2,1)}, bf16[128,768]{1,0:T(8,128)(2,1)S(1)}, u32[]{:S(2)}, u32[]{:S(2)}) collective-permute-start(bf16[128,768]{1,0:T(8,128)(2,1)} %bitcast.11), channel_id=1, source_target_pairs={{0,8},{1,3},{2,10},{3,1},{4,12},{5,7},{6,14},{7,5},{8,0},{9,11},{1... | collective-permute-start | bytes 589832 | tf_op jit(solution)/shard_map/ppermute | solution.py:40
  14.4 10.3 %collective-permute-done.1 = bf16[256,768]{1,0:T(8,128)(2,1)S(1)} collective-permute-done((bf16[256,768]{1,0:T(8,128)(2,1)S(1)}, bf16[256,768]{1,0:T(8,128)(2,1)S(1)}, u32[]{:S(2)}, u32[]{:S(2)}) %collective-permute-start.1) | collective-permute-done | bytes 393248 | tf_op jit(solution)/shard_map/ppermute | solution.py:40
  35.8 3.4 %attend_first.1 = (f32[128,768]{1,0:T(8,128)S(1)}, f32[128,128]{1,0:T(8,128)S(1)}, f32[128,128]{1,0:T(8,128)S(1)}) custom-call(bf16[512,2304]{1,0:T(8,128)(2,1)S(1)} %project.2.queries.keys.values.keys_a.values_a, bf16[512,2304]{1,0:T(8,128)(2,1)S(1)} %project.2.queries.keys.values.keys_a.values_a, ...), custom_call_target="tpu_custom_call" | custom-call | flops 402653184 | bytes 2359296 | tf_op jit(solution)/shard_map/attend_first/pallas_call | solution.py:281
  42.4 4.7 %attend_last.1 = (f32[128,768]{1,0:T(8,128)S(1)}, f32[128,128]{1,0:T(8,128)S(1)}) custom-call(bf16[512,2304]{1,0:T(8,128)(2,1)S(1)} %project.2.queries.keys.values.keys_a.values_a, bf16[512,2304]{1,0:T(8,128)(2,1)S(1)} %project.3.keys.values.keys_b.values_b.queries, bf16[512,2304]{1,0:T(8,128)(2,1)S(1)} %project.3.keys.values.keys_b.values_b.queries, ...), custom_call_target="tpu_custom_call" | custom-call | flops 402653184 | bytes 2359296 | tf_op jit(solution)/shard_map/attend_last/pallas_call | solution.py:291
  47.1 5.1 %middle.1 = (bf16[128,768]{1,0:T(8,128)(2,1)}, bf16[128,1408]{1,0:T(8,128)(2,1)S(1)}, bf16[128,1408]{1,0:T(8,128)(2,1)}, bf16[128,3072]{1,0:T(8,128)(2,1)S(1)}, ...) custom-call(s32[1]{0:T(128)} %bitcast.core, ...), custom_call_target="tpu_custom_call" | custom-call | flops 3321888768 | bytes 25165824 | tf_op jit(solution)/shard_map/middle/pallas_call | solution.py:381
  69.0 6.7 %collective-permute-done.8 = bf16[128,896]{1,0:T(8,128)(2,1)S(1)} collective-permute-done((bf16[128,896]{1,0:T(8,128)(2,1)}, bf16[128,896]{1,0:T(8,128)(2,1)S(1)}, u32[]{:S(2)}, u32[]{:S(2)}) %collective-permute-start.8) | collective-permute-done | bytes 229408 | tf_op jit(solution)/shard_map/ppermute | solution.py:40
  80.2 5.4 %query_grads.1.grad_q.refs_6_ = bf16[128,768]{1,0:T(8,128)(2,1)S(1)} custom-call(bf16[512,2304]{1,0:T(8,128)(2,1)S(1)} %project.2.queries.keys.values.keys_a.values_a, bf16[512,2304]{1,0:T(8,128)(2,1)S(1)} %project.2.queries.keys.values.keys_a.values_a, bf16[512,2304]{1,0:T(8,128)(2,1)S(1)} %project.2.queries.keys.values.keys_a.values_a, ...), custom_call_target="tpu_custom_call" | custom-call | flops 1207959552 | bytes 4718592 | tf_op jit(solution)/shard_map/query_grads/pallas_call | solution.py:517
  85.7 9.0 %collective-permute-done.45 = bf16[160,768]{1,0:T(8,128)(2,1)S(1)} collective-permute-done((bf16[160,768]{1,0:T(8,128)(2,1)S(1)}, bf16[160,768]{1,0:T(8,128)(2,1)S(1)}, u32[]{:S(2)}, u32[]{:S(2)}) %collective-permute-start.45) | collective-permute-done | bytes 245792 | tf_op jit(solution)/shard_map/ppermute | solution.py:40
  97.0 3.7 %key_grads_first.1 = (f32[128,768]{1,0:T(8,128)S(1)}, f32[128,768]{1,0:T(8,128)S(1)}) custom-call(bf16[512,2304]{1,0:T(8,128)(2,1)S(1)} %project.2.queries.keys.values.keys_a.values_a, bf16[512,2304]{1,0:T(8,128)(2,1)S(1)} %project.2.queries.keys.values.keys_a.values_a, bf16[512,2304]{1,0:T(8,128)(2,1)S(1)} %project.2.queries.keys.values.keys_a.values_a, ...), custom_call_target="tpu_custom_call" | custom-call | flops 805306368 | bytes 2359296 | tf_op jit(solution)/shard_map/key_grads_first/pallas_call | solution.py:589
  109.7 4.4 %collective-permute-done.48 = bf16[40,768]{1,0:T(8,128)(2,1)S(1)} collective-permute-done((bf16[40,768]{1,0:T(8,128)(2,1)S(1)}, bf16[40,768]{1,0:T(8,128)(2,1)S(1)}, u32[]{:S(2)}, u32[]{:S(2)}) %collective-permute-start.48) | collective-permute-done | bytes 61472 | tf_op jit(solution)/shard_map/ppermute | solution.py:40
  115.4 5.1 %collective-permute-done.49 = bf16[80,768]{1,0:T(8,128)(2,1)S(1)} collective-permute-done((bf16[80,768]{1,0:T(8,128)(2,1)S(1)}, bf16[80,768]{1,0:T(8,128)(2,1)S(1)}, u32[]{:S(2)}, u32[]{:S(2)}) %collective-permute-start.49) | collective-permute-done | bytes 122912 | tf_op jit(solution)/shard_map/ppermute | solution.py:40
  120.7 4.1 %key_grads_last.1 = (bf16[128,768]{1,0:T(8,128)(2,1)S(1)}, bf16[128,768]{1,0:T(8,128)(2,1)S(1)}) custom-call(bf16[512,2304]{1,0:T(8,128)(2,1)S(1)} %project.2.queries.keys.values.keys_a.values_a, bf16[512,2304]{1,0:T(8,128)(2,1)S(1)} %project.2.queries.keys.values.keys_a.values_a, bf16[512,2304]{1,0:T(8,128)(2,1)S(1)} %copy-done.1, ...), custom_call_target="tpu_custom_call" | custom-call | flops 805306368 | bytes 2359296 | tf_op jit(solution)/shard_map/key_grads_last/pallas_call | solution.py:599
  136.8 4.9 %collective-permute-done.18 = bf16[48,768]{1,0:T(8,128)(2,1)S(1)} collective-permute-done((bf16[48,768]{1,0:T(8,128)(2,1)S(1)}, bf16[48,768]{1,0:T(8,128)(2,1)S(1)}, u32[]{:S(2)}, u32[]{:S(2)}) %collective-permute-start.18) | collective-permute-done | bytes 73760 | tf_op jit(solution)/shard_map/ppermute | solution.py:40
  141.7 3.4 %collective-permute-start.19 = (bf16[48,768]{1,0:T(8,128)(2,1)S(1)}, bf16[48,768]{1,0:T(8,128)(2,1)S(1)}, u32[]{:S(2)}, u32[]{:S(2)}) collective-permute-start(bf16[48,768]{1,0:T(8,128)(2,1)S(1)} %add_convert_fusion.22), channel_id=1, source_target_pairs={{0,8},{1,9},{2,10},{3,11},{4,12},{5,13},{6,14},{7,15},{8,0},{9,1},... | collective-permute-start | bytes 221192 | tf_op jit(solution)/shard_map/ppermute | solution.py:40
  147.5 3.8 %collective-permute-done.36 = bf16[144,768]{1,0:T(8,128)(2,1)S(1)} collective-permute-done((bf16[144,768]{1,0:T(8,128)(2,1)S(1)}, bf16[144,768]{1,0:T(8,128)(2,1)S(1)}, u32[]{:S(2)}, u32[]{:S(2)}) %collective-permute-start.36) | collective-permute-done | bytes 221216 | tf_op jit(solution)/shard_map/ppermute | solution.py:40
  153.2 5.8 %collective-permute-done.37 = bf16[72,768]{1,0:T(8,128)(2,1)S(1)} collective-permute-done((bf16[72,768]{1,0:T(8,128)(2,1)S(1)}, bf16[72,768]{1,0:T(8,128)(2,1)S(1)}, u32[]{:S(2)}, u32[]{:S(2)}) %collective-permute-start.37) | collective-permute-done | bytes 110624 | tf_op jit(solution)/shard_map/ppermute | solution.py:40
  162.3 3.5 %collective-permute-done.38 = bf16[72,768]{1,0:T(8,128)(2,1)S(1)} collective-permute-done((bf16[72,768]{1,0:T(8,128)(2,1)S(1)}, bf16[72,768]{1,0:T(8,128)(2,1)S(1)}, u32[]{:S(2)}, u32[]{:S(2)}) %collective-permute-start.38) | collective-permute-done | bytes 110624 | tf_op jit(solution)/shard_map/ppermute | solution.py:40
  165.8 4.6 %collective-permute-done.27 = bf16[224,768]{1,0:T(8,128)(2,1)S(1)} collective-permute-done((bf16[224,768]{1,0:T(8,128)(2,1)S(1)}, bf16[224,768]{1,0:T(8,128)(2,1)S(1)}, u32[]{:S(2)}, u32[]{:S(2)}) %collective-permute-start.27) | collective-permute-done | bytes 344096 | tf_op jit(solution)/shard_map/ppermute | solution.py:40
  178.4 4.6 %collective-permute-done.29 = bf16[56,768]{1,0:T(8,128)(2,1)S(1)} collective-permute-done((bf16[56,768]{1,0:T(8,128)(2,1)S(1)}, bf16[56,768]{1,0:T(8,128)(2,1)S(1)}, u32[]{:S(2)}, u32[]{:S(2)}) %collective-permute-start.29) | collective-permute-done | bytes 86048 | tf_op jit(solution)/shard_map/ppermute | solution.py:40
  183.2 4.2 %collective-permute-start.40 = (bf16[288,768]{1,0:T(8,128)(2,1)S(1)}, bf16[288,768]{1,0:T(8,128)(2,1)S(1)}, u32[]{:S(2)}, u32[]{:S(2)}) collective-permute-start(bf16[288,768]{1,0:T(8,128)(2,1)S(1)} %pad_maximum_fusion.13), channel_id=1, source_target_pairs={{0,4},{1,5},{2,6},{3,7},{4,0},{5,1},{6,2},{7,3},{8,12},{9,13},{10,... | collective-permute-start | bytes 1327112 | tf_op jit(solution)/shard_map/ppermute | solution.py:40
  188.8 7.1 %collective-permute-done.31 = bf16[112,768]{1,0:T(8,128)(2,1)S(1)} collective-permute-done((bf16[112,768]{1,0:T(8,128)(2,1)S(1)}, bf16[112,768]{1,0:T(8,128)(2,1)S(1)}, u32[]{:S(2)}, u32[]{:S(2)}) %collective-permute-start.31) | collective-permute-done | bytes 172064 | tf_op jit(solution)/shard_map/ppermute | solution.py:40
  198.4 4.9 %collective-permute-done.32 = bf16[224,768]{1,0:T(8,128)(2,1)S(1)} collective-permute-done((bf16[224,768]{1,0:T(8,128)(2,1)S(1)}, bf16[224,768]{1,0:T(8,128)(2,1)S(1)}, u32[]{:S(2)}, u32[]{:S(2)}) %collective-permute-start.32) | collective-permute-done | bytes 344096 | tf_op jit(solution)/shard_map/ppermute | solution.py:40
  206.7 23.8 %collective-permute-done.51.other = bf16[320,768]{1,0:T(8,128)(2,1)S(1)} collective-permute-done((bf16[320,768]{1,0:T(8,128)(2,1)S(1)}, bf16[320,768]{1,0:T(8,128)(2,1)S(1)}, u32[]{:S(2)}, u32[]{:S(2)}) %collective-permute-start.51) | collective-permute-done | bytes 491552 | tf_op jit(solution)/shard_map/ppermute | solution.py:40
  241.7 3.3 %pad_maximum_fusion.2 = f32[384,2304]{1,0:T(8,128)} fusion(f32[384,1536]{1,0:T(8,128)S(1)} %get-tuple-element.52, f32[384,768]{1,0:T(8,128)} %copy-done.17), kind=kLoop, calls=%fused_computation.2 | loop fusion | flops 884736 | bytes 7077888 | tf_op jit(solution)/shard_map/concatenate | solution.py:758
  (261 shorter events, 104.0 us)
Async XLA Ops:
  6.2 18.6 %collective-permute-start.5 = (bf16[384,768]{1,0:T(8,128)(2,1)}, bf16[384,768]{1,0:T(8,128)(2,1)}, u32[]{:S(2)}, u32[]{:S(2)}) collective-permute-start(bf16[384,768]{1,0:T(8,128)(2,1)} %param.12), channel_id=1, source_target_pairs={{0,1},{1,0},{2,3},{3,2},{4,5},{5,4},{6,7},{7,6},{8,9},{9,8},{10,11... | collective-permute-start | bytes 1769480 | tf_op jit(solution)/shard_map/ppermute | solution.py:44
  6.2 21.9 %collective-permute-start.2 = (bf16[384,2304]{1,0:T(8,128)(2,1)}, bf16[384,2304]{1,0:T(8,128)(2,1)}, u32[]{:S(2)}, u32[]{:S(2)}) collective-permute-start(bf16[384,2304]{1,0:T(8,128)(2,1)} %param.11), channel_id=1, source_target_pairs={{0,1},{1,0},{2,3},{3,2},{4,5},{5,4},{6,7},{7,6},{8,9},{9,8},{10,11... | collective-permute-start | bytes 5308424 | tf_op jit(solution)/shard_map/ppermute | solution.py:44
  6.7 21.4 %collective-permute-start.6 = (bf16[384,2304]{1,0:T(8,128)(2,1)}, bf16[384,2304]{1,0:T(8,128)(2,1)}, u32[]{:S(2)}, u32[]{:S(2)}) collective-permute-start(bf16[384,2304]{1,0:T(8,128)(2,1)} %param.13), channel_id=1, source_target_pairs={{0,1},{1,0},{2,3},{3,2},{4,5},{5,4},{6,7},{7,6},{8,9},{9,8},{10,11... | collective-permute-start | bytes 5308424 | tf_op jit(solution)/shard_map/ppermute | solution.py:44
  12.2 15.6 %collective-permute-start.7 = (bf16[576,768]{1,0:T(8,128)(2,1)S(1)}, bf16[576,768]{1,0:T(8,128)(2,1)S(1)}, u32[]{:S(2)}, u32[]{:S(2)}) collective-permute-start(bf16[576,768]{1,0:T(8,128)(2,1)S(1)} %copy-done.36), channel_id=1, source_target_pairs={{0,1},{1,0},{2,3},{3,2},{4,5},{5,4},{6,7},{7,6},{8,9},{9,8},{10,11... | collective-permute-start | bytes 2654216 | tf_op jit(solution)/shard_map/ppermute | solution.py:44
  24.7 32.5 %collective-permute-start.42 = (bf16[128,768]{1,0:T(8,128)(2,1)S(1)}, bf16[128,768]{1,0:T(8,128)(2,1)S(1)}, u32[]{:S(2)}, u32[]{:S(2)}) collective-permute-start(bf16[128,768]{1,0:T(8,128)(2,1)S(1)} %bitcast.16), channel_id=1, source_target_pairs={{0,1},{1,0},{2,3},{3,2},{4,5},{5,4},{6,7},{7,6},{8,9},{9,8},{10,11... | collective-permute-start | bytes 589832 | tf_op jit(solution)/shard_map/ppermute | solution.py:44
  24.8 14.6 %collective-permute-start.4 = (bf16[512,768]{1,0:T(8,128)(2,1)S(1)}, bf16[512,768]{1,0:T(8,128)(2,1)S(1)}, u32[]{:S(2)}, u32[]{:S(2)}) collective-permute-start(bf16[512,768]{1,0:T(8,128)(2,1)S(1)} %pad_maximum_fusion.6.tokens), channel_id=1, source_target_pairs={{0,2},{1,5},{2,0},{3,7},{4,6},{5,1},{6,4},{7,3},{8,10},{9,13},{10,... | collective-permute-start | bytes 2359304 | tf_op jit(solution)/shard_map/ppermute | solution.py:40
  63.8 13.3 %collective-permute-start.44 = (bf16[320,768]{1,0:T(8,128)(2,1)}, bf16[320,768]{1,0:T(8,128)(2,1)}, u32[]{:S(2)}, u32[]{:S(2)}) collective-permute-start(bf16[320,768]{1,0:T(8,128)(2,1)} %constant_dynamic-slice_fusion.2), channel_id=1, source_target_pairs={{0,16},{1,3},{2,18},{3,1},{4,20},{5,7},{6,22},{7,5},{8,24},{9,11},... | collective-permute-start | bytes 1474568 | tf_op jit(solution)/shard_map/ppermute | solution.py:40
  68.4 32.3 %collective-permute-start.13 = (bf16[128,384]{1,0:T(8,128)(2,1)S(1)}, bf16[128,384]{1,0:T(8,128)(2,1)S(1)}, u32[]{:S(2)}, u32[]{:S(2)}) collective-permute-start(bf16[128,384]{1,0:T(8,128)(2,1)S(1)} %get-tuple-element.106), channel_id=1, source_target_pairs={{0,1},{1,0},{2,3},{3,2},{4,5},{5,4},{6,7},{7,6},{8,9},{9,8},{10,11... | collective-permute-start | bytes 294920 | tf_op jit(solution)/shard_map/ppermute | solution.py:44
  68.5 32.2 %collective-permute-start.12 = (bf16[128,3072]{1,0:T(8,128)(2,1)}, bf16[128,3072]{1,0:T(8,128)(2,1)S(1)}, u32[]{:S(2)}, u32[]{:S(2)}) collective-permute-start(bf16[128,3072]{1,0:T(8,128)(2,1)} %copy-done.11), channel_id=1, source_target_pairs={{0,1},{1,0},{2,3},{3,2},{4,5},{5,4},{6,7},{7,6},{8,9},{9,8},{10,11... | collective-permute-start | bytes 2359304 | tf_op jit(solution)/shard_map/ppermute | solution.py:44
  76.7 19.2 %collective-permute-start.9 = (bf16[256,896]{1,0:T(8,128)(2,1)S(1)}, bf16[256,896]{1,0:T(8,128)(2,1)S(1)}, u32[]{:S(2)}, u32[]{:S(2)}) collective-permute-start(bf16[256,896]{1,0:T(8,128)(2,1)S(1)} %pad_maximum_fusion.12), channel_id=1, source_target_pairs={{0,4},{1,9},{2,6},{3,11},{4,0},{5,13},{6,2},{7,15},{8,12},{9,1},{1... | collective-permute-start | bytes 1376264 | tf_op jit(solution)/shard_map/ppermute | solution.py:40
  78.3 16.4 %collective-permute-start.45 = (bf16[160,768]{1,0:T(8,128)(2,1)S(1)}, bf16[160,768]{1,0:T(8,128)(2,1)S(1)}, u32[]{:S(2)}, u32[]{:S(2)}) collective-permute-start(bf16[160,768]{1,0:T(8,128)(2,1)S(1)} %get-tuple-element.73), channel_id=1, source_target_pairs={{0,4},{1,5},{2,6},{3,7},{4,0},{5,1},{6,2},{7,3},{8,12},{9,13},{10,... | collective-permute-start | bytes 737288 | tf_op jit(solution)/shard_map/ppermute | solution.py:40
  85.6 15.1 %collective-permute-start.14 = (bf16[128,768]{1,0:T(8,128)(2,1)S(1)}, bf16[128,768]{1,0:T(8,128)(2,1)S(1)}, u32[]{:S(2)}, u32[]{:S(2)}) collective-permute-start(bf16[128,768]{1,0:T(8,128)(2,1)S(1)} %query_grads.1.grad_q.refs_6_), channel_id=1, source_target_pairs={{0,1},{1,0},{2,3},{3,2},{4,5},{5,4},{6,7},{7,6},{8,9},{9,8},{10,11... | collective-permute-start | bytes 589832 | tf_op jit(solution)/shard_map/ppermute | solution.py:44
  96.0 24.6 %collective-permute-start.10 = (bf16[512,896]{1,0:T(8,128)(2,1)S(1)}, bf16[512,896]{1,0:T(8,128)(2,1)S(1)}, u32[]{:S(2)}, u32[]{:S(2)}) collective-permute-start(bf16[512,896]{1,0:T(8,128)(2,1)S(1)} %constant_dynamic-update-slice_fusion.grads.packed), channel_id=1, source_target_pairs={{0,2},{1,5},{2,0},{3,7},{4,6},{5,1},{6,4},{7,3},{8,10},{9,13},{10,... | collective-permute-start | bytes 2752520 | tf_op jit(solution)/shard_map/ppermute | solution.py:40
  102.5 12.6 %collective-permute-start.15 = (bf16[384,768]{1,0:T(8,128)(2,1)S(1)}, bf16[384,768]{1,0:T(8,128)(2,1)S(1)}, u32[]{:S(2)}, u32[]{:S(2)}) collective-permute-start(bf16[384,768]{1,0:T(8,128)(2,1)S(1)} %constant_dynamic-slice_fusion.7), channel_id=1, source_target_pairs={{0,16},{1,3},{2,18},{3,1},{4,20},{5,7},{6,22},{7,5},{8,24},{9,11},... | collective-permute-start | bytes 1769480 | tf_op jit(solution)/shard_map/ppermute | solution.py:40
  108.4 19.2 %collective-permute-start.34 = (bf16[576,768]{1,0:T(8,128)(2,1)S(1)}, bf16[576,768]{1,0:T(8,128)(2,1)S(1)}, u32[]{:S(2)}, u32[]{:S(2)}) collective-permute-start(bf16[576,768]{1,0:T(8,128)(2,1)S(1)} %constant_dynamic-slice_fusion.3), channel_id=1, source_target_pairs={{0,16},{1,3},{2,18},{3,1},{4,20},{5,7},{6,22},{7,5},{8,24},{9,11},... | collective-permute-start | bytes 2654216 | tf_op jit(solution)/shard_map/ppermute | solution.py:40
  115.3 12.2 %collective-permute-start.16 = (bf16[192,768]{1,0:T(8,128)(2,1)S(1)}, bf16[192,768]{1,0:T(8,128)(2,1)S(1)}, u32[]{:S(2)}, u32[]{:S(2)}) collective-permute-start(bf16[192,768]{1,0:T(8,128)(2,1)S(1)} %get-tuple-element.69), channel_id=1, source_target_pairs={{0,4},{1,5},{2,6},{3,7},{4,0},{5,1},{6,2},{7,3},{8,12},{9,13},{10,... | collective-permute-start | bytes 884744 | tf_op jit(solution)/shard_map/ppermute | solution.py:40
  130.3 14.9 %collective-permute-start.35 = (bf16[288,768]{1,0:T(8,128)(2,1)S(1)}, bf16[288,768]{1,0:T(8,128)(2,1)S(1)}, u32[]{:S(2)}, u32[]{:S(2)}) collective-permute-start(bf16[288,768]{1,0:T(8,128)(2,1)S(1)} %get-tuple-element.65), channel_id=1, source_target_pairs={{0,4},{1,5},{2,6},{3,7},{4,0},{5,1},{6,2},{7,3},{8,12},{9,13},{10,... | collective-permute-start | bytes 1327112 | tf_op jit(solution)/shard_map/ppermute | solution.py:40
  135.3 23.9 %collective-permute-start.26 = (bf16[448,768]{1,0:T(8,128)(2,1)S(1)}, bf16[448,768]{1,0:T(8,128)(2,1)S(1)}, u32[]{:S(2)}, u32[]{:S(2)}) collective-permute-start(bf16[448,768]{1,0:T(8,128)(2,1)S(1)} %constant_dynamic-slice_fusion.4), channel_id=1, source_target_pairs={{0,16},{1,3},{2,18},{3,1},{4,20},{5,7},{6,22},{7,5},{8,24},{9,11},... | collective-permute-start | bytes 2064392 | tf_op jit(solution)/shard_map/ppermute | solution.py:40
  172.7 16.0 %collective-permute-start.21 = (bf16[192,768]{1,0:T(8,128)(2,1)S(1)}, bf16[192,768]{1,0:T(8,128)(2,1)S(1)}, u32[]{:S(2)}, u32[]{:S(2)}) collective-permute-start(bf16[192,768]{1,0:T(8,128)(2,1)S(1)} %pad_maximum_fusion.16), channel_id=1, source_target_pairs={{0,4},{1,5},{2,6},{3,7},{4,0},{5,1},{6,2},{7,3},{8,12},{9,13},{10,... | collective-permute-start | bytes 884744 | tf_op jit(solution)/shard_map/ppermute | solution.py:40
  183.2 14.9 %collective-permute-start.40 = (bf16[288,768]{1,0:T(8,128)(2,1)S(1)}, bf16[288,768]{1,0:T(8,128)(2,1)S(1)}, u32[]{:S(2)}, u32[]{:S(2)}) collective-permute-start(bf16[288,768]{1,0:T(8,128)(2,1)S(1)} %pad_maximum_fusion.13), channel_id=1, source_target_pairs={{0,4},{1,5},{2,6},{3,7},{4,0},{5,1},{6,2},{7,3},{8,12},{9,13},{10,... | collective-permute-start | bytes 1327112 | tf_op jit(solution)/shard_map/ppermute | solution.py:40
  198.4 38.3 %collective-permute-start.41 = (bf16[576,768]{1,0:T(8,128)(2,1)S(1)}, bf16[576,768]{1,0:T(8,128)(2,1)}, u32[]{:S(2)}, u32[]{:S(2)}) collective-permute-start(bf16[576,768]{1,0:T(8,128)(2,1)S(1)} %pad_maximum_fusion.5.own), channel_id=1, source_target_pairs={{0,16},{1,3},{2,18},{3,1},{4,20},{5,7},{6,22},{7,5},{8,24},{9,11},... | collective-permute-start | bytes 2654216 | tf_op jit(solution)/shard_map/ppermute | solution.py:40
  203.5 36.4 %collective-permute-start.33 = (bf16[448,768]{1,0:T(8,128)(2,1)S(1)}, bf16[448,768]{1,0:T(8,128)(2,1)}, u32[]{:S(2)}, u32[]{:S(2)}) collective-permute-start(bf16[448,768]{1,0:T(8,128)(2,1)S(1)} %pad_maximum_fusion.7.own), channel_id=1, source_target_pairs={{0,16},{1,3},{2,18},{3,1},{4,20},{5,7},{6,22},{7,5},{8,24},{9,11},... | collective-permute-start | bytes 2064392 | tf_op jit(solution)/shard_map/ppermute | solution.py:40
  203.7 28.7 %collective-permute-start.22 = (bf16[384,768]{1,0:T(8,128)(2,1)S(1)}, bf16[384,768]{1,0:T(8,128)(2,1)}, u32[]{:S(2)}, u32[]{:S(2)}) collective-permute-start(bf16[384,768]{1,0:T(8,128)(2,1)S(1)} %pad_maximum_fusion.8.own), channel_id=1, source_target_pairs={{0,16},{1,3},{2,18},{3,1},{4,20},{5,7},{6,22},{7,5},{8,24},{9,11},... | collective-permute-start | bytes 1769480 | tf_op jit(solution)/shard_map/ppermute | solution.py:40
  206.6 23.8 %collective-permute-start.51 = (bf16[320,768]{1,0:T(8,128)(2,1)S(1)}, bf16[320,768]{1,0:T(8,128)(2,1)S(1)}, u32[]{:S(2)}, u32[]{:S(2)}) collective-permute-start(bf16[320,768]{1,0:T(8,128)(2,1)S(1)} %pad_maximum_fusion.11.own), channel_id=1, source_target_pairs={{0,16},{1,3},{2,18},{3,1},{4,20},{5,7},{6,22},{7,5},{8,24},{9,11},... | collective-permute-start | bytes 1474568 | tf_op jit(solution)/shard_map/ppermute | solution.py:40
  (69 other events, 418.9 us)

commit v2 on v1

--- a/solution.py
+++ b/solution.py
@@ -12,7 +12,6 @@
 EPSILON = 1e-05
 THETA = 160000.0
 LANES = 128
-PIECE = 2 * HEADS
 NORMED_AT = 640
 ATTENDED_AT = 1024
 HALVES_WIDTH = 1408
@@ -49,11 +48,23 @@
     return bits[::-1], bits[:1] + bits[:0:-1]
 
 
-def gather_context(block):
+def gather_context(block, ready):
     stages = list(zip(*gather_orders()))
     for first, second in stages[:-1]:
         block = jnp.concatenate([block, flip(block, first, second)], axis=0)
-    return block, flip(block, *stages[-1])
+    block, ready = lax.optimization_barrier((block, ready))
+    return (block, flip(block, *stages[-1])), ready
+
+
+def scatter_context(rows):
+    parts = [rows]
+    for first, second in list(zip(*gather_orders()))[::-1]:
+        half = parts[0].shape[0] // 2
+        away, kept = (
+            sum(part[at : at + half].astype(F32) for part in parts).astype(BF16) for at in (half, 0)
+        )
+        parts = [kept, flip(away, first, second)]
+    return parts
 
 
 def gathered_blocks():
@@ -76,8 +87,7 @@
     return jnp.where(lax.axis_index("wsh") == 0, my_bit(*first), my_bit(*second))
 
 
-def scatter_sum(rows):
-    parts = [rows]
+def scatter_sum(parts):
     for first, second in sum_orders():
         bit = stage_bit(first, second)
         half = parts[0].shape[0] // 2
@@ -154,26 +164,37 @@
     return jnp.where(first, pltpu.roll(vectors, LANES - 32, 1), pltpu.roll(vectors, 32, 1))
 
 
-def project_kernel(tokens, weights, gain, cos, sin, out):
+def project_kernel(tokens, weights, gain, cos, sin, out, *out_queries):
     normed, _ = normalize(tokens[...].astype(F32))
     low = (normed * gain[...].astype(F32)).astype(BF16)
     width = tokens.shape[1]
-    cos_rows, sin_rows = cos[...], sin[...]
-    for part in range(3):
-        columns = dot_nn(low, weights[:, part * width : (part + 1) * width])
+
+    def put(ref, start, rows, columns, turned, scale):
         for j in range(width // LANES):
             piece = columns[:, j * LANES : (j + 1) * LANES]
-            if part < 2:
-                piece = piece * cos_rows + halves_swapped(piece) * sin_rows
-            if part == 0:
-                piece = piece * 0.125
-            at = part * width + j * LANES
-            out[:, at : at + LANES] = piece.astype(BF16)
-
-
-def project(tokens, weights, gain, cos, sin):
+            if turned:
+                piece = piece * cos[:rows, :] + halves_swapped(piece) * sin[:rows, :]
+            ref[:, start + j * LANES : start + (j + 1) * LANES] = (piece * scale).astype(BF16)
+
+    rows = tokens.shape[0]
+    put(out, 0, rows, dot_nn(low, weights[:, width : 2 * width]), True, 1.0)
+    put(out, width, rows, dot_nn(low, weights[:, 2 * width :]), False, 1.0)
+    for ref in out_queries:
+
+        @pl.when(pl.program_id(0) == 0)
+        def _():
+            own = ref.shape[0]
+            put(ref, 0, own, dot_nn(low[:own], weights[:, :width]), True, 0.125)
+
+
+def project(tokens, weights, gain, cos, sin, own_rows):
     rows, width = tokens.shape
     step = min(rows, 256)
+    out_specs = [pl.BlockSpec((step, 2 * width), lambda i: (i, 0))]
+    out_shape = [jax.ShapeDtypeStruct((rows, 2 * width), BF16)]
+    if own_rows:
+        out_specs.append(pl.BlockSpec((own_rows, width), lambda i: (0, 0)))
+        out_shape.append(jax.ShapeDtypeStruct((own_rows, width), BF16))
     return pl.pallas_call(
         project_kernel,
         grid=(rows // step,),
@@ -184,10 +205,10 @@
             pl.BlockSpec((step, LANES), lambda i: (i, 0)),
             pl.BlockSpec((step, LANES), lambda i: (i, 0)),
         ],
-        out_specs=pl.BlockSpec((step, 3 * width), lambda i: (i, 0)),
-        out_shape=jax.ShapeDtypeStruct((rows, 3 * width), BF16),
+        out_specs=out_specs,
+        out_shape=out_shape,
         compiler_params=PARAMS,
-        cost_estimate=cost(6 * rows * width * width, 8 * rows * width),
+        cost_estimate=cost(4 * rows * width * width, 8 * rows * width),
         name="project",
     )(tokens, weights, gain, cos, sin)
 
@@ -268,13 +289,14 @@
     put_pair(log_total, pair, peak + jnp.log(total))
 
 
-def attend(halves, rows):
-    count, width = halves[0].shape[0], halves[0].shape[1] // 3
+def attend(own_queries, halves):
+    count = halves[0].shape[0]
+    rows, width = own_queries.shape
     pairs = width // LANES
     queries = pl.BlockSpec((rows, LANES), lambda j: (0, j))
     shared = pl.BlockSpec((rows, LANES), lambda j: (0, 0))
-    keys = pl.BlockSpec((count, LANES), lambda j: (0, pairs + j))
-    values = pl.BlockSpec((count, LANES), lambda j: (0, 2 * pairs + j))
+    keys = pl.BlockSpec((count, LANES), lambda j: (0, j))
+    values = pl.BlockSpec((count, LANES), lambda j: (0, pairs + j))
     wide = jax.ShapeDtypeStruct((rows, width), F32)
     thin = jax.ShapeDtypeStruct((rows, LANES), F32)
     work = cost(8 * rows * count * width, 6 * count * width)
@@ -287,7 +309,7 @@
         compiler_params=PARAMS,
         cost_estimate=work,
         name="attend_first",
-    )(halves[0], halves[0], halves[0])
+    )(own_queries, halves[0], halves[0])
     return pl.pallas_call(
         attend_last_kernel,
         grid=(pairs,),
@@ -297,13 +319,13 @@
         compiler_params=PARAMS,
         cost_estimate=work,
         name="attend_last",
-    )(halves[0], halves[1], halves[1], mixed, peak, total)
+    )(own_queries, halves[1], halves[1], mixed, peak, total)
 
 
 def middle_kernel(
     core, tokens, attended, log_total, cotangent, w_out, w_in, w_mlp, gain,
     layer_out, own_halves, other_halves, whole,
-    grad_middle, sent, logs_deltas, gain_grad,
+    grad_middle, grads, logs_deltas, gain_grad,
 ):
     rows, width = tokens.shape
     first = core[0] == 0
@@ -343,7 +365,7 @@
     branch = grad_mid.astype(BF16)
     whole[:, 2 * FF :] = branch
     grad_attended = dot_nt(branch, w_out[...]).astype(BF16)
-    sent[:, :width] = grad_attended
+    grads[...] = grad_attended
     products = grad_attended.astype(F32) * mixed
     head = lax.broadcasted_iota(jnp.int32, (width, LANES), 0) // 64
     to_lane = (lane_of((width, LANES)) == head + HEADS).astype(F32)
@@ -354,16 +376,11 @@
         precision=lax.Precision.HIGHEST,
         preferred_element_type=F32,
     )
-    logs_deltas[...] = both
-    high = both.astype(BF16).astype(F32)
-    rest = both - high
-    mid = rest.astype(BF16).astype(F32)
-    last = rest - mid
-    packed = high + pltpu.roll(mid, PIECE, 1) + pltpu.roll(last, 2 * PIECE, 1)
-    sent[:, width:] = packed.astype(BF16)
-
-
-VMEM_SPEC = pl.BlockSpec(memory_space=pltpu.VMEM)
+    logs_deltas[...] = both.T
+
+
+SMEM_SPEC = pl.BlockSpec(memory_space=pltpu.SMEM)
+WHOLE = pl.BlockSpec()
 
 
 def middle_part(core, tokens, attended, log_total, cotangent, w_out, w_in, w_mlp, gain):
@@ -374,13 +391,13 @@
         ((rows, HALVES_WIDTH), BF16),
         ((rows, 2 * FF + width), BF16),
         ((rows, width), F32),
-        ((rows, width + LANES), BF16),
-        ((rows, LANES), F32),
+        ((rows, width), BF16),
+        ((LANES, rows), F32),
         ((1, width), F32),
     ]
     return pl.pallas_call(
         middle_kernel,
-        in_specs=[pl.BlockSpec(memory_space=pltpu.SMEM)] + [VMEM_SPEC] * 8,
+        in_specs=[SMEM_SPEC] + [WHOLE] * 8,
         out_shape=[jax.ShapeDtypeStruct(*shape) for shape in shapes],
         compiler_params=PARAMS,
         cost_estimate=cost(4 * rows * width * (2 * width + 6 * FF), 24 * MIB),
@@ -427,7 +444,7 @@
     total = (used + unit - 1) // unit * unit
     return pl.pallas_call(
         partial(rows_kernel, width, lanes, gain is not None),
-        in_specs=[VMEM_SPEC] * len(arrays),
+        in_specs=[WHOLE] * len(arrays),
         out_shape=jax.ShapeDtypeStruct((total, width), BF16),
         compiler_params=PARAMS,
         cost_estimate=cost(flops, 4 * total * width),
@@ -466,15 +483,15 @@
         put(other, own)
 
 
-def unpack(rows, shapes, gained=False):
-    own, other, bit = gather_rows(scatter_sum(rows))
+def unpack(parts, shapes, gained=False):
+    own, other, bit = gather_rows(scatter_sum(parts))
     width = own.shape[1]
     places = [(k, shape[1] // width) for k, shape in enumerate(shapes)]
     if gained:
         shapes = shapes + [(1, width // 2)]
     return pl.pallas_call(
         partial(unpack_kernel, places, gained),
-        in_specs=[pl.BlockSpec(memory_space=pltpu.SMEM), VMEM_SPEC, VMEM_SPEC],
+        in_specs=[SMEM_SPEC, WHOLE, WHOLE],
         out_shape=[jax.ShapeDtypeStruct(shape, F32) for shape in shapes],
         compiler_params=PARAMS,
         cost_estimate=cost(0, 12 * own.size),
@@ -486,155 +503,169 @@
     return block * cos - halves_swapped(block) * sin
 
 
-def query_grad_kernel(
-    queries, keys_a, values_a, keys_b, values_b, grads, logs_deltas, cos, sin, out
+def row_pair(rows, at):
+    index = lax.broadcasted_iota(jnp.int32, rows.shape, 0)
+    picked = [
+        jnp.sum(jnp.where(index == at + k, rows, 0.0), axis=0, keepdims=True) for k in (0, 1)
+    ]
+    return jnp.concatenate(picked, axis=1)
+
+
+def attend_back_kernel(
+    queries, keys_a, values_a, keys_b, values_b, grads, logs_deltas, cos, sin,
+    out_queries, out_keys, out_values,
 ):
     pair = pl.program_id(0)
-    rows = queries.shape[0]
-    stacked = two_heads(queries[...])
+    rows, count = queries.shape[0], keys_a.shape[0]
+    queries_two = two_heads(queries[...])
     grads_two = two_heads(grads[...])
-    logs = column_pair(logs_deltas[...], 2 * pair)
-    deltas = column_pair(logs_deltas[...], HEADS + 2 * pair)
+    logs = row_pair(logs_deltas[...], 2 * pair)
+    deltas = row_pair(logs_deltas[...], HEADS + 2 * pair)
     total = jnp.zeros((2 * rows, LANES), F32)
-    for keys, values in ((keys_a, values_a), (keys_b, values_b)):
-        for at in chunks_of(keys.shape[0]):
+    for base, keys, values in ((0, keys_a, values_a), (count, keys_b, values_b)):
+        for at in chunks_of(count):
+            to = slice(base + at.start, base + at.stop)
             key_rows = keys[at, :]
-            probs = jnp.exp(dot_nt(stacked, key_rows) - logs)
-            grad_probs = dot_nt(grads_two, values[at, :])
+            probs = jnp.exp(dot_nt(key_rows, queries_two) - logs)
+            grad_probs = dot_nt(values[at, :], grads_two)
             grad_scores = (probs * (grad_probs - deltas)).astype(BF16)
-            total = total + dot_nn(grad_scores, key_rows)
+            out_values[to, :] = dot_nn(probs.astype(BF16), grads_two).astype(BF16)
+            grad_keys = dot_nn(grad_scores, queries_two)
+            out_keys[to, :] = unrotated(grad_keys, cos[to, :], sin[to, :]).astype(BF16)
+            total = total + dot_tn(grad_scores, key_rows)
     grad = one_pair(total) * 0.125
-    out[...] = unrotated(grad, cos[...], sin[...]).astype(BF16)
-
-
-def query_grads(halves, sent, logs_deltas, cos, sin, rows):
-    count, width = halves[0].shape[0], halves[0].shape[1] // 3
+    out_queries[...] = unrotated(grad, cos[:rows, :], sin[:rows, :]).astype(BF16)
+
+
+def attend_back(own_queries, halves, grads, logs_deltas, cos, sin):
+    count = halves[0].shape[0]
+    rows, width = own_queries.shape
     pairs = width // LANES
     queries = pl.BlockSpec((rows, LANES), lambda j: (0, j))
-    shared = pl.BlockSpec((rows, LANES), lambda j: (0, 0))
-    keys = pl.BlockSpec((count, LANES), lambda j: (0, pairs + j))
-    values = pl.BlockSpec((count, LANES), lambda j: (0, 2 * pairs + j))
+    shared = pl.BlockSpec((LANES, rows), lambda j: (0, 0))
+    keys = pl.BlockSpec((count, LANES), lambda j: (0, j))
+    values = pl.BlockSpec((count, LANES), lambda j: (0, pairs + j))
+    table = pl.BlockSpec((2 * count, LANES), lambda j: (0, 0))
+    made = pl.BlockSpec((2 * count, LANES), lambda j: (0, j))
     return pl.pallas_call(
-        query_grad_kernel,
+        attend_back_kernel,
         grid=(pairs,),
-        in_specs=[queries, keys, values, keys, values, queries, shared, shared, shared],
-        out_specs=queries,
-        out_shape=jax.ShapeDtypeStruct((rows, width), BF16),
+        in_specs=[queries, keys, values, keys, values, queries, shared, table, table],
+        out_specs=[queries, made, made],
+        out_shape=[
+            jax.ShapeDtypeStruct((rows, width), BF16),
+            jax.ShapeDtypeStruct((2 * count, width), BF16),
+            jax.ShapeDtypeStruct((2 * count, width), BF16),
+        ],
         compiler_params=PARAMS,
-        cost_estimate=cost(24 * rows * count * width, 12 * count * width),
-        name="query_grads",
+        cost_estimate=cost(40 * rows * count * width, 20 * count * width),
+        name="attend_back",
     )(
-        halves[0], halves[0], halves[0], halves[1], halves[1],
-        sent, logs_deltas, cos, sin,
-    )
-
-
-def key_grads_over(pair, keys, values, queries, grads, packed, total_keys, total_values):
-    rows = keys.shape[0]
-    keys_two = two_heads(keys[...])
-    values_two = two_heads(values[...])
-    pick_shape = (8, LANES)
-    row = lax.broadcasted_iota(jnp.int32, pick_shape, 0)
-    lane = lane_of(pick_shape)
-    wanted = 2 * pair + (row & 1) + jnp.where(row >= 2, HEADS, 0)
-    held = (lane == wanted) | (lane == wanted + PIECE) | (lane == wanted + 2 * PIECE)
-    pick = jnp.where(held, 1.0, 0.0).astype(BF16)
-    for at in chunks_of(queries.shape[0]):
-        query_rows, grad_rows_ = queries[at, :], grads[at, :]
-        picked = dot_nt(pick, packed[at, :])
-        shape = (rows, query_rows.shape[0])
-        logs, deltas = (
-            jnp.concatenate(
-                [jnp.broadcast_to(picked[k : k + 1], shape) for k in (base, base + 1)], axis=0
-            )
-            for base in (0, 2)
+        own_queries, halves[0], halves[0], halves[1], halves[1],
+        grads, logs_deltas, cos, sin,
+    )
+
+
+def back_project_kernel(
+    core, tokens_a, tokens_b, grad_q, grad_k, grad_v, weights, gain,
+    out_first, out_own, out_other, totals, gain_total,
+):
+    step = pl.program_id(0)
+    width = tokens_a.shape[1]
+    half = width // 2
+    own_rows = grad_q.shape[0]
+    tokens = jnp.where(2 * step < pl.num_programs(0), tokens_a[...], tokens_b[...])
+    normed, _ = normalize(tokens.astype(F32))
+    low = (normed * gain[...].astype(F32)).astype(BF16)
+    grad_first = dot_nt(grad_k[...], weights[:, width : 2 * width])
+    grad_first = grad_first + dot_nt(grad_v[...], weights[:, 2 * width :])
+    turned = low.T
+
+    @pl.when(step == 0)
+    def _():
+        query_part = dot_nt(grad_q[...], weights[:, :width])
+        first = grad_first[:own_rows] + query_part
+        out_first[:own_rows, :] = first.astype(BF16)
+        out_first[own_rows:, :] = grad_first[own_rows:].astype(BF16)
+        gain_total[...] = jnp.sum(grad_first * normed, axis=0, keepdims=True) + jnp.sum(
+            query_part * normed[:own_rows], axis=0, keepdims=True
         )
-        probs = jnp.exp(dot_nt(keys_two, query_rows) - logs)
-        grad_probs = dot_nt(values_two, grad_rows_)
-        grad_scores = (probs * (grad_probs - deltas)).astype(BF16)
-        add_values = dot_nn(probs.astype(BF16), grad_rows_)
-        add_keys = dot_nn(grad_scores, query_rows)
-        total_values = add_values if total_values is None else total_values + add_values
-        total_keys = add_keys if total_keys is None else total_keys + add_keys
-    return total_keys, total_values
-
-
-def key_first_kernel(keys, values, queries, grads, packed, out_keys, out_values):
-    pair = pl.program_id(0)
-    grad_k, grad_v = key_grads_over(pair, keys, values, queries, grads, packed, None, None)
-    out_keys[...] = one_pair(grad_k)
-    out_values[...] = one_pair(grad_v)
-
-
-def key_last_kernel(
-    keys, values, queries, grads, packed, first_keys, first_values, cos, sin, out_keys, out_values
-):
-    pair = pl.program_id(0)
-    grad_k, grad_v = key_grads_over(pair, keys, values, queries, grads, packed, None, None)
-    grad_k = one_pair(grad_k) + first_keys[...]
-    out_keys[...] = unrotated(grad_k, cos[...], sin[...]).astype(BF16)
-    out_values[...] = (one_pair(grad_v) + first_values[...]).astype(BF16)
-
-
-def key_grads(halves, sent_halves, cos, sin, rows):
-    count, width = halves[0].shape[0], halves[0].shape[1] // 3
-    pairs = width // LANES
-    keys = pl.BlockSpec((rows, LANES), lambda j: (0, pairs + j))
-    values = pl.BlockSpec((rows, LANES), lambda j: (0, 2 * pairs + j))
-    queries = pl.BlockSpec((count, LANES), lambda j: (0, j))
-    packed = pl.BlockSpec((count, LANES), lambda j: (0, pairs))
-    own = pl.BlockSpec((rows, LANES), lambda j: (0, j))
-    shared = pl.BlockSpec((rows, LANES), lambda j: (0, 0))
-    work = cost(16 * rows * count * width, 6 * count * width)
-    first = pl.pallas_call(
-        key_first_kernel,
-        grid=(pairs,),
-        in_specs=[keys, values, queries, queries, packed],
-        out_specs=[own, own],
-        out_shape=[jax.ShapeDtypeStruct((rows, width), F32)] * 2,
+        totals[:, :width] = dot_nn(turned[:, :own_rows], grad_q[...])
+        totals[:, width : 2 * width] = dot_nn(turned, grad_k[...])
+        totals[:, 2 * width :] = dot_nn(turned, grad_v[...])
+
+    @pl.when(step > 0)
+    def _():
+        out_first[...] = grad_first.astype(BF16)
+        gain_total[...] += jnp.sum(grad_first * normed, axis=0, keepdims=True)
+        totals[:, width : 2 * width] += dot_nn(turned, grad_k[...])
+        totals[:, 2 * width :] += dot_nn(turned, grad_v[...])
+
+    @pl.when(step == pl.num_programs(0) - 1)
+    def _():
+        tile = (16, half)
+        top = lax.broadcasted_iota(jnp.int32, tile, 0) == 0
+        sides = gain_total[:, :half], gain_total[:, half:]
+        for out, side in ((out_own, core[0]), (out_other, 1 - core[0])):
+            start = pl.multiple_of(side * half, half)
+            for k in range(3):
+                columns = slice(k * width, (k + 1) * width)
+                out[k * half : (k + 1) * half, :] = totals[pl.ds(start, half), columns].astype(BF16)
+            out[3 * half :, :] = jnp.zeros((out.shape[0] - 3 * half, width), BF16)
+            row = jnp.broadcast_to(jnp.where(side == 0, *sides), tile)
+            out[3 * half : 3 * half + 16, :half] = jnp.where(top, row, 0.0).astype(BF16)
+
+
+def back_project(core, pieces, tokens, grad_q, grad_k, grad_v, weights, gain):
+    count, width = tokens[0].shape
+    rows, own_rows = 2 * count, grad_q.shape[0]
+    step = min(count, 2 * own_rows)
+    each = count // step
+    unit = 8 * pieces
+    total = (3 * (width // 2) + 1 + unit - 1) // unit * unit
+    block = pl.BlockSpec((step, width), lambda i: (i, 0))
+
+    def fixed(shape):
+        return pl.BlockSpec(shape, lambda i: (0, 0))
+
+    return pl.pallas_call(
+        back_project_kernel,
+        grid=(rows // step,),
+        in_specs=[
+            SMEM_SPEC,
+            pl.BlockSpec((step, width), lambda i: (jnp.minimum(i, each - 1), 0)),
+            pl.BlockSpec((step, width), lambda i: (jnp.maximum(i - each, 0), 0)),
+            fixed((own_rows, width)), block, block,
+            fixed((width, 3 * width)), fixed((1, width)),
+        ],
+        out_specs=[block, fixed((total, width)), fixed((total, width))],
+        out_shape=[
+            jax.ShapeDtypeStruct((rows, width), BF16),
+            jax.ShapeDtypeStruct((total, width), BF16),
+            jax.ShapeDtypeStruct((total, width), BF16),
+        ],
+        scratch_shapes=[pltpu.VMEM((width, 3 * width), F32), pltpu.VMEM((1, width), F32)],
         compiler_params=PARAMS,
-        cost_estimate=work,
-        name="key_grads_first",
-    )(halves[0], halves[0], halves[0], sent_halves[0], sent_halves[0])
-    return pl.pallas_call(
-        key_last_kernel,
-        grid=(pairs,),
-        in_specs=[keys, values, queries, queries, packed, own, own, shared, shared],
-        out_specs=[own, own],
-        out_shape=[jax.ShapeDtypeStruct((rows, width), BF16)] * 2,
-        compiler_params=PARAMS,
-        cost_estimate=work,
-        name="key_grads_last",
-    )(
-        halves[0], halves[0], halves[1], sent_halves[1], sent_halves[1],
-        first[0], first[1], cos, sin,
-    )
-
-
-def last_kernel(tokens, grad_middle, grad_q, grad_k, grad_v, weights, gain, out, gain_grad):
-    width = tokens.shape[1]
+        cost_estimate=cost(8 * rows * width * width, 12 * rows * width),
+        name="back_project",
+    )(core, *tokens, grad_q, grad_k, grad_v, weights, gain)
+
+
+def last_kernel(tokens, grad_middle, part_a, part_b, gain, out):
     normed, rstd = normalize(tokens[...].astype(F32))
-    grad_first = dot_nt(grad_q[...], weights[:, :width])
-    grad_first = grad_first + dot_nt(grad_k[...], weights[:, width : 2 * width])
-    grad_first = grad_first + dot_nt(grad_v[...], weights[:, 2 * width :])
-    gain_grad[...] = jnp.sum(grad_first * normed, axis=0, keepdims=True)
+    grad_first = part_a[...].astype(F32) + part_b[...].astype(F32)
     back = norm_back(grad_first, normed, rstd, gain[...].astype(F32))
     out[...] = (grad_middle[...] + back).astype(BF16)
 
 
-def last_part(tokens, grad_middle, grad_q, grad_k, grad_v, weights, gain):
-    rows, width = tokens.shape
+def last_part(tokens, grad_middle, parts, gain):
     return pl.pallas_call(
         last_kernel,
-        in_specs=[VMEM_SPEC] * 7,
-        out_shape=[
-            jax.ShapeDtypeStruct((rows, width), BF16),
-            jax.ShapeDtypeStruct((1, width), F32),
-        ],
+        out_shape=jax.ShapeDtypeStruct(tokens.shape, BF16),
         compiler_params=PARAMS,
-        cost_estimate=cost(6 * rows * width * width, 8 * MIB),
+        cost_estimate=cost(20 * tokens.size, 12 * tokens.size),
         name="last",
-    )(tokens, grad_middle, grad_q, grad_k, grad_v, weights, gain)
+    )(tokens, grad_middle, *parts, gain)
 
 
 def rotary_tables(positions, head_dim):
@@ -656,8 +687,8 @@
     upstream = cotangent.reshape(rows, width)
     pieces = lax.axis_size("seq") * lax.axis_size("ctx")
 
-    gathered = gather_context(own)
     full_qkv = both_halves(w_qkv)
+    gathered, full_qkv = gather_context(own, full_qkv)
     gains = jnp.stack([gain_attn, gain_mlp])
     gains_other = swap_cores(gains)
     gains_all = jnp.concatenate(
@@ -668,27 +699,23 @@
     full_in = both_halves(w_in)
     full_mlp = both_halves(w_mlp)
     upstream_other = swap_cores(upstream)
-    first_in = (normalize(own.astype(F32))[0] * attn_gain.astype(F32)).astype(BF16)
-    first_own = lax.dynamic_slice_in_dim(first_in, core * half, half, 1)
-    first_other = swap_cores(lax.dynamic_slice_in_dim(first_in, (1 - core) * half, half, 1))
-
     blocks = gathered_blocks()
     positions = (blocks[:, None] * rows + jnp.arange(rows, dtype=jnp.int32)[None, :]).reshape(-1)
     cos, sin = rotary_tables(positions.astype(F32), 64)
-    own_cos, own_sin = cos[:rows], sin[:rows]
     count = gathered[0].shape[0]
-    halves = [
+    (first_half, queries), (last_half,) = [
         project(
             part, full_qkv, attn_gain,
             cos[k * count : (k + 1) * count], sin[k * count : (k + 1) * count],
+            0 if k else rows,
         )
         for k, part in enumerate(gathered)
     ]
-
-    attended, log_total = attend(halves, rows)
+    halves = first_half, last_half
+    attended, log_total = attend(queries, halves)
     (
         layer_out, own_halves, other_halves, whole,
-        grad_middle, sent, logs_deltas, gain_mlp_part,
+        grad_middle, grads, logs_deltas, gain_mlp_part,
     ) = middle_part(
         core.reshape(1), own, attended, log_total, upstream,
         full_out, full_in, full_mlp, mlp_gain,
@@ -699,14 +726,21 @@
         theirs = lax.dynamic_slice_in_dim(part, (1 - core) * half, half, 1)
         return [mine, swap_cores(theirs)]
 
-    sent_halves = gather_context(sent)
     other_halves = swap_cores(other_halves)
     whole_other = swap_cores(whole)
-
     mlp_rows = grad_rows(
         width,
         pieces,
-        [(own_halves, other_halves, slice(0, half_ff), upstream, upstream_other, slice(0, width))],
+        [
+            (
+                own_halves, other_halves, slice(0, half_ff),
+                upstream, upstream_other, slice(0, width),
+            ),
+            (
+                own_halves, other_halves, slice(ATTENDED_AT, ATTENDED_AT + half),
+                whole, whole_other, slice(2 * FF, 2 * FF + width),
+            ),
+        ],
         gain_pair(gain_mlp_part),
     )
     in_rows = grad_rows(
@@ -719,43 +753,20 @@
             )
         ],
     )
-    grad_q = query_grads(halves, sent, logs_deltas, own_cos, own_sin, rows)
-    out_rows = grad_rows(
-        width,
-        pieces,
-        [
-            (
-                own_halves, other_halves, slice(ATTENDED_AT, ATTENDED_AT + half),
-                whole, whole_other, slice(2 * FF, 2 * FF + width),
-            ),
-            (
-                first_own, first_other, slice(0, half),
-                grad_q, swap_cores(grad_q), slice(0, width),
-            ),
-        ],
-    )
-    grad_k, grad_v = key_grads(halves, sent_halves, own_cos, own_sin, rows)
-    tokens_grad, gain_attn_part = last_part(
-        own, grad_middle, grad_q, grad_k, grad_v, full_qkv, attn_gain
-    )
-    key_rows = grad_rows(
-        width,
-        pieces,
-        [
-            (first_own, first_other, slice(0, half), grad_k, swap_cores(grad_k), slice(0, width)),
-            (first_own, first_other, slice(0, half), grad_v, swap_cores(grad_v), slice(0, width)),
-        ],
-        gain_pair(gain_attn_part),
-    )
-
-    mlp_grad, gain_mlp_grad = unpack(mlp_rows, [(half_ff, width)], True)
-    (in_grad,) = unpack(in_rows, [(half, 2 * FF)])
-    out_grad, q_grad = unpack(out_rows, [(half, width), (half, width)])
-    kv_grad, gain_attn_grad = unpack(key_rows, [(half, 2 * width)], True)
+
+    grad_q, grad_k, grad_v = attend_back(queries, halves, grads, logs_deltas, cos, sin)
+    first_rows, qkv_own, qkv_other = back_project(
+        core.reshape(1), pieces, gathered, grad_q, grad_k, grad_v, full_qkv, attn_gain
+    )
+    tokens_grad = last_part(own, grad_middle, scatter_context(first_rows), attn_gain)
+
+    mlp_grad, out_grad, gain_mlp_grad = unpack([mlp_rows], [(half_ff, width), (half, width)], True)
+    (in_grad,) = unpack([in_rows], [(half, 2 * FF)])
+    qkv_grad, gain_attn_grad = unpack([qkv_own, swap_cores(qkv_other)], [(half, 3 * width)], True)
     return (
         layer_out.reshape(seqs_here, rows, width),
         tokens_grad.reshape(seqs_here, rows, width),
-        jnp.concatenate([q_grad, kv_grad], axis=1),
+        qkv_grad,
         out_grad,
         in_grad,
         mlp_grad,

time: 246 us -> 238 us (0.967)
  waiting for transfers between devices: 109 us -> 100 us
  starting transfers between devices: 53 us -> 48.3 us
  other arithmetic: 20.2 us -> 23.2 us
    ppermute x38 -> x30, waiting for transfers between devices: 109 us -> 95.5 us  [flip(): return lax.ppermute(block, ('seq', 'ctx', 'wsh'), route)]
    convert_element_type x12 -> x10, other arithmetic: 2.52 us -> 11.1 us  [side(): return (cut[0].astype(F32) + cut[1].astype(F32)).astype(BF16)]
    ppermute x14 -> x10, waiting for transfers between devices: 0.04 us -> 4.52 us  [swap_cores(): return lax.ppermute(block, 'wsh', [(0, 1), (1, 0)])]
    ppermute x38 -> x30, starting transfers between devices: 49.6 us -> 46.2 us  [flip(): return lax.ppermute(block, ('seq', 'ctx', 'wsh'), route)]
    concatenate x1 -> x0, other arithmetic: 3.29 us -> none  [local(): jnp.concatenate([q_grad, kv_grad], axis=1)]
    pallas_call x9 -> x7, Pallas kernels: 28.4 us -> 29.7 us  [the longest x1 9.55 us: back_project(): pl.pallas_call(back_project_kernel, grid=(rows // step,), in_specs=[SMEM_...]
    unnamed x84 -> x58, local copies, waits for them, and re-layouts: 14 us -> 14.5 us
  transfers between devices with their start and end apart: 52 -> 40, of which waited for: 22 -> 20; matrix products, arithmetic and copies ran while one was open for 7% -> 10% of each run, Pallas kernels for 17% -> 6%
where the time goes in v2:
time: 238 us; the launch traced here: 235 us
  waiting for transfers between devices  100 us (42%)
  starting transfers between devices  48.3 us (20%)
  Pallas kernels  43.6 us (18%)
  other arithmetic  23.2 us (10%)
  local copies, waits for them, and re-layouts  18.8 us (8%)
    ppermute x30, waiting for transfers between devices, flip(): return lax.ppermute(block, ('seq', 'ctx', 'wsh'), route)  95.5 us
    ppermute x30, starting transfers between devices, flip(): return lax.ppermute(block, ('seq', 'ctx', 'wsh'), route)  46.2 us
    unnamed x58, local copies, waits for them, and re-layouts  14.5 us
    convert_element_type x10, other arithmetic, side(): return (cut[0].astype(F32) + cut[1].astype(F32)).astype(BF16)  11.1 us
    pallas_call x1, Pallas kernels, back_project(): pl.pallas_call(back_project_kernel, grid=(rows // step,), in_specs=[SMEM_...  9.55 us
    pallas_call x1, Pallas kernels, attend_back(): pl.pallas_call(attend_back_kernel, grid=(pairs,), in_specs=[queries, keys...  7.43 us
    pallas_call x3, Pallas kernels, unpack(): pl.pallas_call(partial(unpack_kernel, places, gained), in_specs=[SMEM_SPE...  7.01 us
  transfers between devices with their start and end apart: 40, of which 20 were waited for; matrix products, arithmetic and copies ran while one was open for 10% of the time, Pallas kernels for 6%

profile of v2, /device:TPU:0, one launch (start us, length us, event | category | flops | bytes accessed | tf_op | source)
XLA Modules:
  0.0 235.3 jit_solution(10264732108165385842)
XLA Ops:
  0.6 4.1 %collective-permute-start = (bf16[128,768]{1,0:T(8,128)(2,1)}, bf16[128,768]{1,0:T(8,128)(2,1)S(1)}, u32[]{:S(2)}, u32[]{:S(2)}) collective-permute-start(bf16[128,768]{1,0:T(8,128)(2,1)} %bitcast.8), channel_id=1, source_target_pairs={{0,8},{1,3},{2,10},{3,1},{4,12},{5,7},{6,14},{7,5},{8,0},{9,11},{1... | collective-permute-start | bytes 589832 | tf_op jit(solution)/shard_map/ppermute | solution.py:39
  12.7 10.2 %collective-permute-done.1 = bf16[256,768]{1,0:T(8,128)(2,1)S(1)} collective-permute-done((bf16[256,768]{1,0:T(8,128)(2,1)S(1)}, bf16[256,768]{1,0:T(8,128)(2,1)S(1)}, u32[]{:S(2)}, u32[]{:S(2)}) %collective-permute-start.1) | collective-permute-done | bytes 393248 | tf_op jit(solution)/shard_map/ppermute | solution.py:39
  33.5 3.4 %attend_first.1 = (f32[128,768]{1,0:T(8,128)S(1)}, f32[128,128]{1,0:T(8,128)S(1)}, f32[128,128]{1,0:T(8,128)S(1)}) custom-call(bf16[128,768]{1,0:T(8,128)(2,1)S(1)} %get-tuple-element.38.queries, bf16[512,1536]{1,0:T(8,128)(2,1)S(1)} %get-tuple-element.39.keys.values.keys_a.values_a, bf16[512,1536]{1,0:T(8,128)(2,1)S(1)} %get-tuple-element.39.keys.values.keys_a.values_a), custom_call_target="tpu_custom_call" | custom-call | flops 402653184 | bytes 2359296 | tf_op jit(solution)/shard_map/attend_first/pallas_call | solution.py:303
  42.2 4.6 %attend_last.1 = (f32[128,768]{1,0:T(8,128)S(1)}, f32[128,128]{1,0:T(8,128)S(1)}) custom-call(bf16[128,768]{1,0:T(8,128)(2,1)S(1)} %get-tuple-element.38.queries, bf16[512,1536]{1,0:T(8,128)(2,1)S(1)} %project.3.keys.values.keys_b.values_b, bf16[512,1536]{1,0:T(8,128)(2,1)S(1)} %project.3.keys.values.keys_b.values_b, ...), custom_call_target="tpu_custom_call" | custom-call | flops 402653184 | bytes 2359296 | tf_op jit(solution)/shard_map/attend_last/pallas_call | solution.py:313
  46.9 4.7 %middle.1 = (bf16[128,768]{1,0:T(8,128)(2,1)}, bf16[128,1408]{1,0:T(8,128)(2,1)S(1)}, bf16[128,1408]{1,0:T(8,128)(2,1)}, bf16[128,3072]{1,0:T(8,128)(2,1)S(1)}, ...) custom-call(s32[1]{0:T(128)} %bitcast.core, ...), custom_call_target="tpu_custom_call" | custom-call | flops 3321888768 | bytes 25165824 | tf_op jit(solution)/shard_map/middle/pallas_call | solution.py:398
  51.5 7.4 %attend_back.1 = (bf16[128,768]{1,0:T(8,128)(2,1)S(1)}, bf16[1024,768]{1,0:T(8,128)(2,1)S(1)}, bf16[1024,768]{1,0:T(8,128)(2,1)S(1)}) custom-call(bf16[128,768]{1,0:T(8,128)(2,1)S(1)} %get-tuple-element.38.queries, bf16[512,1536]{1,0:T(8,128)(2,1)S(1)} %get-tuple-element.39.keys.values.keys_a.values_a, ...), custom_call_target="tpu_custom_call" | custom-call | flops 2013265920 | bytes 7864320 | tf_op jit(solution)/shard_map/attend_back/pallas_call | solution.py:550
  59.0 9.5 %back_project.1 = (bf16[1024,768]{1,0:T(8,128)(2,1)S(1)}, bf16[1280,768]{1,0:T(8,128)(2,1)S(1)}, bf16[1280,768]{1,0:T(8,128)(2,1)}) custom-call(s32[1]{0:T(128)} %bitcast.core, bf16[512,768]{1,0:T(8,128)(2,1)S(1)} %pad_maximum_fusion.6.tokens.tokens_a, bf16[512,768]{1,0:T(8,128)(2,1)S(1)} %collective-permute-done.4.tokens.tokens_b, ...), custom_call_target="tpu_custom_call" | custom-call | flops 4831838208 | bytes 9437184 | tf_op jit(solution)/shard_map/back_project/pallas_call | solution.py:631
  72.0 4.5 %collective-permute-done.21.refs_3_ = bf16[128,768]{1,0:T(8,128)(2,1)S(1)} collective-permute-done((bf16[128,768]{1,0:T(8,128)(2,1)S(1)}, bf16[128,768]{1,0:T(8,128)(2,1)S(1)}, u32[]{:S(2)}, u32[]{:S(2)}) %collective-permute-start.21) | collective-permute-done | bytes 196640 | tf_op jit(solution)/shard_map/ppermute | solution.py:43
  98.5 3.3 %add_convert_fusion.1 = (bf16[640,768]{1,0:T(8,128)(2,1)}, bf16[640,768]{1,0:T(8,128)(2,1)}) fusion(bf16[1280,768]{1,0:T(8,128)(2,1)} %collective-permute-done.11, s32[]{:T(128)S(6)} %select_n.332, bf16[1280,768]{1,0:T(8,128)(2,1)S(1)} %copy-done.11, s32[]{:T(128)S(6)} %select_n.334), kind=kLoop, calls=%fused_computation.3 | loop fusion | flops 3932160 | bytes 5898248 | tf_op jit(solution)/shard_map/convert_element_type | solution.py:99
  126.9 3.5 %collective-permute-start.28 = (bf16[64,768]{1,0:T(8,128)(2,1)S(1)}, bf16[64,768]{1,0:T(8,128)(2,1)S(1)}, u32[]{:S(2)}, u32[]{:S(2)}) collective-permute-start(bf16[64,768]{1,0:T(8,128)(2,1)S(1)} %add_convert_fusion.24), channel_id=1, source_target_pairs={{0,8},{1,9},{2,10},{3,11},{4,12},{5,13},{6,14},{7,15},{8,0},{9,1},... | collective-permute-start | bytes 294920 | tf_op jit(solution)/shard_map/ppermute | solution.py:39
  130.5 6.3 %collective-permute-done.28 = bf16[64,768]{1,0:T(8,128)(2,1)S(1)} collective-permute-done((bf16[64,768]{1,0:T(8,128)(2,1)S(1)}, bf16[64,768]{1,0:T(8,128)(2,1)S(1)}, u32[]{:S(2)}, u32[]{:S(2)}) %collective-permute-start.28) | collective-permute-done | bytes 98336 | tf_op jit(solution)/shard_map/ppermute | solution.py:39
  136.9 3.6 %collective-permute-done.13 = bf16[320,768]{1,0:T(8,128)(2,1)S(1)} collective-permute-done((bf16[320,768]{1,0:T(8,128)(2,1)S(1)}, bf16[320,768]{1,0:T(8,128)(2,1)S(1)}, u32[]{:S(2)}, u32[]{:S(2)}) %collective-permute-start.13) | collective-permute-done | bytes 491552 | tf_op jit(solution)/shard_map/ppermute | solution.py:39
  142.8 3.3 %collective-permute-start.36 = (bf16[72,768]{1,0:T(8,128)(2,1)S(1)}, bf16[72,768]{1,0:T(8,128)(2,1)S(1)}, u32[]{:S(2)}, u32[]{:S(2)}) collective-permute-start(bf16[72,768]{1,0:T(8,128)(2,1)S(1)} %add_convert_fusion.21), channel_id=1, source_target_pairs={{0,8},{1,9},{2,10},{3,11},{4,12},{5,13},{6,14},{7,15},{8,0},{9,1},... | collective-permute-start | bytes 331784 | tf_op jit(solution)/shard_map/ppermute | solution.py:39
  146.9 3.3 %collective-permute-start.15 = (bf16[80,768]{1,0:T(8,128)(2,1)S(1)}, bf16[80,768]{1,0:T(8,128)(2,1)S(1)}, u32[]{:S(2)}, u32[]{:S(2)}) collective-permute-start(bf16[80,768]{1,0:T(8,128)(2,1)S(1)} %add_convert_fusion.19), channel_id=1, source_target_pairs={{0,8},{1,9},{2,10},{3,11},{4,12},{5,13},{6,14},{7,15},{8,0},{9,1},... | collective-permute-start | bytes 368648 | tf_op jit(solution)/shard_map/ppermute | solution.py:39
  150.2 3.2 %collective-permute-done.36 = bf16[72,768]{1,0:T(8,128)(2,1)S(1)} collective-permute-done((bf16[72,768]{1,0:T(8,128)(2,1)S(1)}, bf16[72,768]{1,0:T(8,128)(2,1)S(1)}, u32[]{:S(2)}, u32[]{:S(2)}) %collective-permute-start.36) | collective-permute-done | bytes 110624 | tf_op jit(solution)/shard_map/ppermute | solution.py:39
  159.7 5.6 %collective-permute-done.16 = bf16[80,768]{1,0:T(8,128)(2,1)S(1)} collective-permute-done((bf16[80,768]{1,0:T(8,128)(2,1)S(1)}, bf16[80,768]{1,0:T(8,128)(2,1)S(1)}, u32[]{:S(2)}, u32[]{:S(2)}) %collective-permute-start.16) | collective-permute-done | bytes 122912 | tf_op jit(solution)/shard_map/ppermute | solution.py:39
  165.3 3.2 %collective-permute-start.17 = (bf16[160,768]{1,0:T(8,128)(2,1)S(1)}, bf16[160,768]{1,0:T(8,128)(2,1)S(1)}, u32[]{:S(2)}, u32[]{:S(2)}) collective-permute-start(bf16[160,768]{1,0:T(8,128)(2,1)S(1)} %pad_maximum_fusion.14), channel_id=1, source_target_pairs={{0,2},{1,17},{2,0},{3,19},{4,6},{5,21},{6,4},{7,23},{8,10},{9,25},... | collective-permute-start | bytes 737288 | tf_op jit(solution)/shard_map/ppermute | solution.py:39
  168.7 4.0 %collective-permute-done.17 = bf16[160,768]{1,0:T(8,128)(2,1)S(1)} collective-permute-done((bf16[160,768]{1,0:T(8,128)(2,1)S(1)}, bf16[160,768]{1,0:T(8,128)(2,1)S(1)}, u32[]{:S(2)}, u32[]{:S(2)}) %collective-permute-start.17) | collective-permute-done | bytes 245792 | tf_op jit(solution)/shard_map/ppermute | solution.py:39
  173.0 8.8 %collective-permute-done.38 = bf16[288,768]{1,0:T(8,128)(2,1)S(1)} collective-permute-done((bf16[288,768]{1,0:T(8,128)(2,1)S(1)}, bf16[288,768]{1,0:T(8,128)(2,1)S(1)}, u32[]{:S(2)}, u32[]{:S(2)}) %collective-permute-start.38) | collective-permute-done | bytes 442400 | tf_op jit(solution)/shard_map/ppermute | solution.py:39
  181.9 10.4 %collective-permute-done.18 = bf16[320,768]{1,0:T(8,128)(2,1)S(1)} collective-permute-done((bf16[320,768]{1,0:T(8,128)(2,1)S(1)}, bf16[320,768]{1,0:T(8,128)(2,1)S(1)}, u32[]{:S(2)}, u32[]{:S(2)}) %collective-permute-start.18) | collective-permute-done | bytes 491552 | tf_op jit(solution)/shard_map/ppermute | solution.py:39
  192.5 4.6 %collective-permute-start.19 = (bf16[640,768]{1,0:T(8,128)(2,1)S(1)}, bf16[640,768]{1,0:T(8,128)(2,1)S(1)}, u32[]{:S(2)}, u32[]{:S(2)}) collective-permute-start(bf16[640,768]{1,0:T(8,128)(2,1)S(1)} %pad_maximum_fusion.4.own), channel_id=1, source_target_pairs={{0,16},{1,3},{2,18},{3,1},{4,20},{5,7},{6,22},{7,5},{8,24},{9,11},... | collective-permute-start | bytes 2949128 | tf_op jit(solution)/shard_map/ppermute | solution.py:39
  200.5 7.8 %collective-permute-done.10.part_b = bf16[128,768]{1,0:T(8,128)(2,1)S(1)} collective-permute-done((bf16[128,768]{1,0:T(8,128)(2,1)S(1)}, bf16[128,768]{1,0:T(8,128)(2,1)S(1)}, u32[]{:S(2)}, u32[]{:S(2)}) %collective-permute-start.10) | collective-permute-done | bytes 196640 | tf_op jit(solution)/shard_map/ppermute | solution.py:39
  209.3 17.8 %collective-permute-done.31.other = bf16[512,768]{1,0:T(8,128)(2,1)S(1)} collective-permute-done((bf16[512,768]{1,0:T(8,128)(2,1)S(1)}, bf16[512,768]{1,0:T(8,128)(2,1)S(1)}, u32[]{:S(2)}, u32[]{:S(2)}) %collective-permute-start.31) | collective-permute-done | bytes 786464 | tf_op jit(solution)/shard_map/ppermute | solution.py:39
  229.5 3.2 %unpack.5 = f32[384,2304]{1,0:T(8,128)} custom-call(s32[1]{0:T(128)} %bitcast.6.bit, bf16[576,768]{1,0:T(8,128)(2,1)S(1)} %pad_maximum_fusion.5.own, bf16[576,768]{1,0:T(8,128)(2,1)} %collective-permute-done.39.other), custom_call_target="tpu_custom_call" | custom-call | bytes 5308416 | tf_op jit(solution)/shard_map/unpack/pallas_call | solution.py:492
  (187 shorter events, 93.9 us)
Async XLA Ops:
  4.7 18.6 %collective-permute-start.6 = (bf16[384,2304]{1,0:T(8,128)(2,1)}, bf16[384,2304]{1,0:T(8,128)(2,1)}, u32[]{:S(2)}, u32[]{:S(2)}) collective-permute-start(bf16[384,2304]{1,0:T(8,128)(2,1)} %param.13), channel_id=1, source_target_pairs={{0,1},{1,0},{2,3},{3,2},{4,5},{5,4},{6,7},{7,6},{8,9},{9,8},{10,11... | collective-permute-start | bytes 5308424 | tf_op jit(solution)/shard_map/ppermute | solution.py:43
  4.7 18.6 %collective-permute-start.2 = (bf16[384,2304]{1,0:T(8,128)(2,1)}, bf16[384,2304]{1,0:T(8,128)(2,1)}, u32[]{:S(2)}, u32[]{:S(2)}) collective-permute-start(bf16[384,2304]{1,0:T(8,128)(2,1)} %param.11), channel_id=1, source_target_pairs={{0,1},{1,0},{2,3},{3,2},{4,5},{5,4},{6,7},{7,6},{8,9},{9,8},{10,11... | collective-permute-start | bytes 5308424 | tf_op jit(solution)/shard_map/ppermute | solution.py:43
  6.7 16.3 %collective-permute-start.5 = (bf16[384,768]{1,0:T(8,128)(2,1)}, bf16[384,768]{1,0:T(8,128)(2,1)S(1)}, u32[]{:S(2)}, u32[]{:S(2)}) collective-permute-start(bf16[384,768]{1,0:T(8,128)(2,1)} %param.12), channel_id=1, source_target_pairs={{0,1},{1,0},{2,3},{3,2},{4,5},{5,4},{6,7},{7,6},{8,9},{9,8},{10,11... | collective-permute-start | bytes 1769480 | tf_op jit(solution)/shard_map/ppermute | solution.py:43
  10.9 12.1 %collective-permute-start.1 = (bf16[256,768]{1,0:T(8,128)(2,1)S(1)}, bf16[256,768]{1,0:T(8,128)(2,1)S(1)}, u32[]{:S(2)}, u32[]{:S(2)}) collective-permute-start(bf16[256,768]{1,0:T(8,128)(2,1)S(1)} %pad_maximum_fusion.12), channel_id=1, source_target_pairs={{0,4},{1,9},{2,6},{3,11},{4,0},{5,13},{6,2},{7,15},{8,12},{9,1},{1... | collective-permute-start | bytes 1179656 | tf_op jit(solution)/shard_map/ppermute | solution.py:39
  28.0 12.1 %collective-permute-start.4 = (bf16[512,768]{1,0:T(8,128)(2,1)S(1)}, bf16[512,768]{1,0:T(8,128)(2,1)S(1)}, u32[]{:S(2)}, u32[]{:S(2)}) collective-permute-start(bf16[512,768]{1,0:T(8,128)(2,1)S(1)} %pad_maximum_fusion.6.tokens.tokens_a), channel_id=1, source_target_pairs={{0,2},{1,5},{2,0},{3,7},{4,6},{5,1},{6,4},{7,3},{8,10},{9,13},{10,... | collective-permute-start | bytes 2359304 | tf_op jit(solution)/shard_map/ppermute | solution.py:39
  71.0 27.6 %collective-permute-start.11 = (bf16[1280,768]{1,0:T(8,128)(2,1)}, bf16[1280,768]{1,0:T(8,128)(2,1)}, u32[]{:S(2)}, u32[]{:S(2)}) collective-permute-start(bf16[1280,768]{1,0:T(8,128)(2,1)} %get-tuple-element.54), channel_id=1, source_target_pairs={{0,1},{1,0},{2,3},{3,2},{4,5},{5,4},{6,7},{7,6},{8,9},{9,8},{10,11... | collective-permute-start | bytes 5898248 | tf_op jit(solution)/shard_map/ppermute | solution.py:43
  83.8 12.3 %collective-permute-start.24 = (bf16[512,768]{1,0:T(8,128)(2,1)}, bf16[512,768]{1,0:T(8,128)(2,1)}, u32[]{:S(2)}, u32[]{:S(2)}) collective-permute-start(bf16[512,768]{1,0:T(8,128)(2,1)} %constant_dynamic-slice_fusion), channel_id=1, source_target_pairs={{0,16},{1,3},{2,18},{3,1},{4,20},{5,7},{6,22},{7,5},{8,24},{9,11},... | collective-permute-start | bytes 2359304 | tf_op jit(solution)/shard_map/ppermute | solution.py:39
  91.2 14.4 %collective-permute-start.32 = (bf16[576,768]{1,0:T(8,128)(2,1)}, bf16[576,768]{1,0:T(8,128)(2,1)}, u32[]{:S(2)}, u32[]{:S(2)}) collective-permute-start(bf16[576,768]{1,0:T(8,128)(2,1)} %constant_dynamic-slice_fusion.1), channel_id=1, source_target_pairs={{0,16},{1,3},{2,18},{3,1},{4,20},{5,7},{6,22},{7,5},{8,24},{9,11},... | collective-permute-start | bytes 2654216 | tf_op jit(solution)/shard_map/ppermute | solution.py:39
  92.9 20.9 %collective-permute-start.8 = (bf16[512,768]{1,0:T(8,128)(2,1)}, bf16[512,768]{1,0:T(8,128)(2,1)}, u32[]{:S(2)}, u32[]{:S(2)}) collective-permute-start(bf16[512,768]{1,0:T(8,128)(2,1)} %slice.55), channel_id=1, source_target_pairs={{0,2},{1,5},{2,0},{3,7},{4,6},{5,1},{6,4},{7,3},{8,10},{9,13},{10,... | collective-permute-start | bytes 2359304 | tf_op jit(solution)/shard_map/ppermute | solution.py:39
  98.4 12.4 %collective-permute-start.25 = (bf16[256,768]{1,0:T(8,128)(2,1)}, bf16[256,768]{1,0:T(8,128)(2,1)}, u32[]{:S(2)}, u32[]{:S(2)}) collective-permute-start(bf16[256,768]{1,0:T(8,128)(2,1)} %get-tuple-element.73), channel_id=1, source_target_pairs={{0,4},{1,5},{2,6},{3,7},{4,0},{5,1},{6,2},{7,3},{8,12},{9,13},{10,... | collective-permute-start | bytes 1179656 | tf_op jit(solution)/shard_map/ppermute | solution.py:39
  101.8 20.4 %collective-permute-start.12 = (bf16[640,768]{1,0:T(8,128)(2,1)}, bf16[640,768]{1,0:T(8,128)(2,1)}, u32[]{:S(2)}, u32[]{:S(2)}) collective-permute-start(bf16[640,768]{1,0:T(8,128)(2,1)} %get-tuple-element.65), channel_id=1, source_target_pairs={{0,16},{1,3},{2,18},{3,1},{4,20},{5,7},{6,22},{7,5},{8,24},{9,11},... | collective-permute-start | bytes 2949128 | tf_op jit(solution)/shard_map/ppermute | solution.py:39
  115.1 84.3 %collective-permute-start.9 = (bf16[256,768]{1,0:T(8,128)(2,1)S(1)}, bf16[256,768]{1,0:T(8,128)(2,1)S(1)}, u32[]{:S(2)}, u32[]{:S(2)}) collective-permute-start(bf16[256,768]{1,0:T(8,128)(2,1)S(1)} %get-tuple-element.75), channel_id=1, source_target_pairs={{0,4},{1,9},{2,6},{3,11},{4,0},{5,13},{6,2},{7,15},{8,12},{9,1},{1... | collective-permute-start | bytes 1179656 | tf_op jit(solution)/shard_map/ppermute | solution.py:39
  117.5 12.8 %collective-permute-start.34 = (bf16[144,768]{1,0:T(8,128)(2,1)S(1)}, bf16[144,768]{1,0:T(8,128)(2,1)S(1)}, u32[]{:S(2)}, u32[]{:S(2)}) collective-permute-start(bf16[144,768]{1,0:T(8,128)(2,1)S(1)} %get-tuple-element.89), channel_id=1, source_target_pairs={{0,2},{1,17},{2,0},{3,19},{4,6},{5,21},{6,4},{7,23},{8,10},{9,25},... | collective-permute-start | bytes 663560 | tf_op jit(solution)/shard_map/ppermute | solution.py:39
  123.7 16.8 %collective-permute-start.13 = (bf16[320,768]{1,0:T(8,128)(2,1)S(1)}, bf16[320,768]{1,0:T(8,128)(2,1)S(1)}, u32[]{:S(2)}, u32[]{:S(2)}) collective-permute-start(bf16[320,768]{1,0:T(8,128)(2,1)S(1)} %get-tuple-element.77), channel_id=1, source_target_pairs={{0,4},{1,5},{2,6},{3,7},{4,0},{5,1},{6,2},{7,3},{8,12},{9,13},{10,... | collective-permute-start | bytes 1474568 | tf_op jit(solution)/shard_map/ppermute | solution.py:39
  130.4 12.4 %collective-permute-start.35 = (bf16[72,768]{1,0:T(8,128)(2,1)S(1)}, bf16[72,768]{1,0:T(8,128)(2,1)S(1)}, u32[]{:S(2)}, u32[]{:S(2)}) collective-permute-start(bf16[72,768]{1,0:T(8,128)(2,1)S(1)} %add_convert_fusion.22), channel_id=1, source_target_pairs={{0,8},{1,9},{2,10},{3,11},{4,12},{5,13},{6,14},{7,15},{8,0},{9,1},... | collective-permute-start | bytes 331784 | tf_op jit(solution)/shard_map/ppermute | solution.py:39
  142.0 16.0 %collective-permute-start.29 = (bf16[128,768]{1,0:T(8,128)(2,1)S(1)}, bf16[128,768]{1,0:T(8,128)(2,1)S(1)}, u32[]{:S(2)}, u32[]{:S(2)}) collective-permute-start(bf16[128,768]{1,0:T(8,128)(2,1)S(1)} %pad_maximum_fusion.16), channel_id=1, source_target_pairs={{0,2},{1,17},{2,0},{3,19},{4,6},{5,21},{6,4},{7,23},{8,10},{9,25},... | collective-permute-start | bytes 589832 | tf_op jit(solution)/shard_map/ppermute | solution.py:39
  146.9 10.9 %collective-permute-start.15 = (bf16[80,768]{1,0:T(8,128)(2,1)S(1)}, bf16[80,768]{1,0:T(8,128)(2,1)S(1)}, u32[]{:S(2)}, u32[]{:S(2)}) collective-permute-start(bf16[80,768]{1,0:T(8,128)(2,1)S(1)} %add_convert_fusion.19), channel_id=1, source_target_pairs={{0,8},{1,9},{2,10},{3,11},{4,12},{5,13},{6,14},{7,15},{8,0},{9,1},... | collective-permute-start | bytes 368648 | tf_op jit(solution)/shard_map/ppermute | solution.py:39
  153.5 15.0 %collective-permute-start.37 = (bf16[144,768]{1,0:T(8,128)(2,1)S(1)}, bf16[144,768]{1,0:T(8,128)(2,1)S(1)}, u32[]{:S(2)}, u32[]{:S(2)}) collective-permute-start(bf16[144,768]{1,0:T(8,128)(2,1)S(1)} %pad_maximum_fusion.15), channel_id=1, source_target_pairs={{0,2},{1,17},{2,0},{3,19},{4,6},{5,21},{6,4},{7,23},{8,10},{9,25},... | collective-permute-start | bytes 663560 | tf_op jit(solution)/shard_map/ppermute | solution.py:39
  158.1 14.7 %collective-permute-start.30 = (bf16[256,768]{1,0:T(8,128)(2,1)S(1)}, bf16[256,768]{1,0:T(8,128)(2,1)S(1)}, u32[]{:S(2)}, u32[]{:S(2)}) collective-permute-start(bf16[256,768]{1,0:T(8,128)(2,1)S(1)} %pad_maximum_fusion.13), channel_id=1, source_target_pairs={{0,4},{1,5},{2,6},{3,7},{4,0},{5,1},{6,2},{7,3},{8,12},{9,13},{10,... | collective-permute-start | bytes 1179656 | tf_op jit(solution)/shard_map/ppermute | solution.py:39
  168.6 13.2 %collective-permute-start.38 = (bf16[288,768]{1,0:T(8,128)(2,1)S(1)}, bf16[288,768]{1,0:T(8,128)(2,1)S(1)}, u32[]{:S(2)}, u32[]{:S(2)}) collective-permute-start(bf16[288,768]{1,0:T(8,128)(2,1)S(1)} %pad_maximum_fusion.11), channel_id=1, source_target_pairs={{0,4},{1,5},{2,6},{3,7},{4,0},{5,1},{6,2},{7,3},{8,12},{9,13},{10,... | collective-permute-start | bytes 1327112 | tf_op jit(solution)/shard_map/ppermute | solution.py:39
  172.8 19.5 %collective-permute-start.18 = (bf16[320,768]{1,0:T(8,128)(2,1)S(1)}, bf16[320,768]{1,0:T(8,128)(2,1)S(1)}, u32[]{:S(2)}, u32[]{:S(2)}) collective-permute-start(bf16[320,768]{1,0:T(8,128)(2,1)S(1)} %pad_maximum_fusion.10), channel_id=1, source_target_pairs={{0,4},{1,5},{2,6},{3,7},{4,0},{5,1},{6,2},{7,3},{8,12},{9,13},{10,... | collective-permute-start | bytes 1474568 | tf_op jit(solution)/shard_map/ppermute | solution.py:39
  192.5 40.1 %collective-permute-start.19 = (bf16[640,768]{1,0:T(8,128)(2,1)S(1)}, bf16[640,768]{1,0:T(8,128)(2,1)S(1)}, u32[]{:S(2)}, u32[]{:S(2)}) collective-permute-start(bf16[640,768]{1,0:T(8,128)(2,1)S(1)} %pad_maximum_fusion.4.own), channel_id=1, source_target_pairs={{0,16},{1,3},{2,18},{3,1},{4,20},{5,7},{6,22},{7,5},{8,24},{9,11},... | collective-permute-start | bytes 2949128 | tf_op jit(solution)/shard_map/ppermute | solution.py:39
  197.2 32.3 %collective-permute-start.39 = (bf16[576,768]{1,0:T(8,128)(2,1)S(1)}, bf16[576,768]{1,0:T(8,128)(2,1)}, u32[]{:S(2)}, u32[]{:S(2)}) collective-permute-start(bf16[576,768]{1,0:T(8,128)(2,1)S(1)} %pad_maximum_fusion.5.own), channel_id=1, source_target_pairs={{0,16},{1,3},{2,18},{3,1},{4,20},{5,7},{6,22},{7,5},{8,24},{9,11},... | collective-permute-start | bytes 2654216 | tf_op jit(solution)/shard_map/ppermute | solution.py:39
  197.3 29.8 %collective-permute-start.31 = (bf16[512,768]{1,0:T(8,128)(2,1)S(1)}, bf16[512,768]{1,0:T(8,128)(2,1)S(1)}, u32[]{:S(2)}, u32[]{:S(2)}) collective-permute-start(bf16[512,768]{1,0:T(8,128)(2,1)S(1)} %pad_maximum_fusion.7.own), channel_id=1, source_target_pairs={{0,16},{1,3},{2,18},{3,1},{4,20},{5,7},{6,22},{7,5},{8,24},{9,11},... | collective-permute-start | bytes 2359304 | tf_op jit(solution)/shard_map/ppermute | solution.py:39
  (45 other events, 266.5 us)

commit v3 on v2

--- a/solution.py
+++ b/solution.py
@@ -15,6 +15,9 @@
 NORMED_AT = 640
 ATTENDED_AT = 1024
 HALVES_WIDTH = 1408
+MLP_ORDERS = ("yaxb", "ybxa")
+IN_ORDERS = ("xyba", "axyb")
+LATE_ORDERS = ("xyab", "bxya")
 MIB = 1 << 20
 BF16 = jnp.bfloat16
 F32 = jnp.float32
@@ -48,23 +51,29 @@
     return bits[::-1], bits[:1] + bits[:0:-1]
 
 
-def gather_context(block, ready):
+def gather_context(block):
     stages = list(zip(*gather_orders()))
     for first, second in stages[:-1]:
         block = jnp.concatenate([block, flip(block, first, second)], axis=0)
-    block, ready = lax.optimization_barrier((block, ready))
-    return (block, flip(block, *stages[-1])), ready
-
-
-def scatter_context(rows):
-    parts = [rows]
-    for first, second in list(zip(*gather_orders()))[::-1]:
-        half = parts[0].shape[0] // 2
+    return block, flip(block, *stages[-1])
+
+
+class ContextSum:
+    def __init__(self, rows):
+        self.parts = [rows]
+        self.stages = list(zip(*gather_orders()))[::-1]
+
+    def step(self):
+        half = self.parts[0].shape[0] // 2
         away, kept = (
-            sum(part[at : at + half].astype(F32) for part in parts).astype(BF16) for at in (half, 0)
+            sum(part[at : at + half].astype(F32) for part in self.parts).astype(BF16)
+            for at in (half, 0)
         )
-        parts = [kept, flip(away, first, second)]
-    return parts
+        self.parts = [kept, flip(away, *self.stages.pop(0))]
+
+    @property
+    def left(self):
+        return len(self.stages)
 
 
 def gathered_blocks():
@@ -78,40 +87,68 @@
     return mine ^ lax.axis_index("ctx")
 
 
-def sum_orders():
-    seq, ctx = bits_of("seq"), bits_of("ctx")
-    return list(zip(seq + ctx[1:2] + ctx[:1] + ctx[2:], ctx[:2] + seq + ctx[2:]))
+def sum_orders(orders):
+    ctx = bits_of("ctx")
+    bits = {"x": bits_of("seq"), "y": ctx[:1], "a": ctx[1:2], "b": ctx[2:]}
+    return list(zip(*[sum((bits[letter] for letter in order), []) for order in orders]))
 
 
 def stage_bit(first, second):
     return jnp.where(lax.axis_index("wsh") == 0, my_bit(*first), my_bit(*second))
 
 
-def scatter_sum(parts):
-    for first, second in sum_orders():
-        bit = stage_bit(first, second)
-        half = parts[0].shape[0] // 2
-
-        def side(which):
-            cut = [lax.dynamic_slice_in_dim(part, which * half, half, 0) for part in parts]
-            if len(cut) == 1:
-                return cut[0]
-            return (cut[0].astype(F32) + cut[1].astype(F32)).astype(BF16)
-
-        away = side(1 - bit)
-        parts = [side(bit), flip(away, first, second)]
-    return (parts[0].astype(F32) + parts[1].astype(F32)).astype(BF16)
-
-
-def gather_rows(rows):
-    stages = sum_orders()[::-1]
-    for first, second in stages[:-1]:
-        bit = stage_bit(first, second)
-        other = flip(rows, first, second)
-        low = jnp.where(bit == 0, rows, other)
-        high = jnp.where(bit == 0, other, rows)
-        rows = jnp.concatenate([low, high], axis=0)
-    return rows, flip(rows, *stages[-1]), stage_bit(*stages[-1])
+def after(arrays, *made):
+    return lax.optimization_barrier((*arrays, *made))[: len(arrays)]
+
+
+class RowsSum:
+    def __init__(self, parts, orders):
+        self.parts = parts
+        self.starts = [0] * len(parts)
+        self.size = parts[0].shape[0]
+        self.stages = sum_orders(orders)
+        self.at = 0
+
+    def summed(self, start, size):
+        cut = [
+            lax.dynamic_slice_in_dim(part, first + start, size, 0).astype(F32)
+            for part, first in zip(self.parts, self.starts)
+        ]
+        return sum(cut[1:], cut[0]).astype(BF16)
+
+    def first_away(self):
+        return self.summed((1 - stage_bit(*self.stages[0])) * (self.size // 2), self.size // 2)
+
+    def step(self, away=None):
+        count, at = len(self.stages), self.at
+        self.at += 1
+        if at < count:
+            stage = self.stages[at]
+            bit = stage_bit(*stage)
+            self.size //= 2
+            if away is None:
+                away = self.summed((1 - bit) * self.size, self.size)
+            if at == 0:
+                kept, starts = self.parts, [start + bit * self.size for start in self.starts]
+            else:
+                kept, starts = [self.summed(bit * self.size, self.size)], [0]
+            self.parts = [*kept, flip(away, *stage)]
+            self.starts = [*starts, 0]
+            return
+        stage = self.stages[2 * count - 1 - at]
+        if at == count:
+            rows = self.summed(0, self.size)
+        else:
+            own, other = self.parts
+            low = jnp.where(self.bit == 0, own, other)
+            high = jnp.where(self.bit == 0, other, own)
+            rows = jnp.concatenate([low, high], axis=0)
+        self.bit = stage_bit(*stage)
+        self.parts = [rows, flip(rows, *stage)]
+
+    @property
+    def left(self):
+        return 2 * len(self.stages) - self.at
 
 
 def both_halves(block):
@@ -134,11 +171,16 @@
     return lax.dot_general(a, b, (((0,), (0,)), ((), ())), preferred_element_type=F32)
 
 
+SMEM_SPEC = pl.BlockSpec(memory_space=pltpu.SMEM)
+WHOLE = pl.BlockSpec()
+
+
 def cost(flops, moved):
     return pl.CostEstimate(flops=int(flops), bytes_accessed=int(moved), transcendentals=0)
 
 
-PARAMS = pltpu.CompilerParams(vmem_limit_bytes=40 * MIB)
+def params(mib):
+    return pltpu.CompilerParams(vmem_limit_bytes=mib * MIB)
 
 
 def normalize(inputs):
@@ -164,10 +206,21 @@
     return jnp.where(first, pltpu.roll(vectors, LANES - 32, 1), pltpu.roll(vectors, 32, 1))
 
 
-def project_kernel(tokens, weights, gain, cos, sin, out, *out_queries):
+def project_kernel(core, tokens, weights, other, gain, cos, sin, out, out_low, *more):
+    width = tokens.shape[1]
+    half = width // 2
+    if more:
+        queries, joined = more
+
+        @pl.when(pl.program_id(0) == 0)
+        def _():
+            joined[pl.ds(pl.multiple_of(core[0] * half, half), half), :] = weights[...]
+            joined[pl.ds(pl.multiple_of((1 - core[0]) * half, half), half), :] = other[...]
+
+        weights = joined
     normed, _ = normalize(tokens[...].astype(F32))
     low = (normed * gain[...].astype(F32)).astype(BF16)
-    width = tokens.shape[1]
+    out_low[...] = low
 
     def put(ref, start, rows, columns, turned, scale):
         for j in range(width // LANES):
@@ -179,38 +232,51 @@
     rows = tokens.shape[0]
     put(out, 0, rows, dot_nn(low, weights[:, width : 2 * width]), True, 1.0)
     put(out, width, rows, dot_nn(low, weights[:, 2 * width :]), False, 1.0)
-    for ref in out_queries:
+    if more:
 
         @pl.when(pl.program_id(0) == 0)
         def _():
-            own = ref.shape[0]
-            put(ref, 0, own, dot_nn(low[:own], weights[:, :width]), True, 0.125)
-
-
-def project(tokens, weights, gain, cos, sin, own_rows):
+            own = queries.shape[0]
+            put(queries, 0, own, dot_nn(low[:own], weights[:, :width]), True, 0.125)
+
+
+def project(core, tokens, weights, other, gain, cos, sin, own_rows):
     rows, width = tokens.shape
     step = min(rows, 256)
-    out_specs = [pl.BlockSpec((step, 2 * width), lambda i: (i, 0))]
-    out_shape = [jax.ShapeDtypeStruct((rows, 2 * width), BF16)]
+
+    def fixed(shape):
+        return pl.BlockSpec(shape, lambda i: (0, 0))
+
+    out_specs = [
+        pl.BlockSpec((step, 2 * width), lambda i: (i, 0)),
+        pl.BlockSpec((step, width), lambda i: (i, 0)),
+    ]
+    out_shape = [
+        jax.ShapeDtypeStruct((rows, 2 * width), BF16),
+        jax.ShapeDtypeStruct((rows, width), BF16),
+    ]
     if own_rows:
-        out_specs.append(pl.BlockSpec((own_rows, width), lambda i: (0, 0)))
+        out_specs += [fixed((own_rows, width)), fixed((width, 3 * width))]
         out_shape.append(jax.ShapeDtypeStruct((own_rows, width), BF16))
+        out_shape.append(jax.ShapeDtypeStruct((width, 3 * width), BF16))
     return pl.pallas_call(
         project_kernel,
         grid=(rows // step,),
         in_specs=[
+            SMEM_SPEC,
             pl.BlockSpec((step, width), lambda i: (i, 0)),
-            pl.BlockSpec((width, 3 * width), lambda i: (0, 0)),
-            pl.BlockSpec((1, width), lambda i: (0, 0)),
+            fixed(weights.shape),
+            fixed(other.shape),
+            fixed((1, width)),
             pl.BlockSpec((step, LANES), lambda i: (i, 0)),
             pl.BlockSpec((step, LANES), lambda i: (i, 0)),
         ],
         out_specs=out_specs,
         out_shape=out_shape,
-        compiler_params=PARAMS,
+        compiler_params=params(28),
         cost_estimate=cost(4 * rows * width * width, 8 * rows * width),
         name="project",
-    )(tokens, weights, gain, cos, sin)
+    )(core, tokens, weights, other, gain, cos, sin)
 
 
 def two_heads(block):
@@ -306,7 +372,7 @@
         in_specs=[queries, keys, values],
         out_specs=[queries, shared, shared],
         out_shape=[wide, thin, thin],
-        compiler_params=PARAMS,
+        compiler_params=params(24),
         cost_estimate=work,
         name="attend_first",
     )(own_queries, halves[0], halves[0])
@@ -316,7 +382,7 @@
         in_specs=[queries, keys, values, queries, shared, shared],
         out_specs=[queries, shared],
         out_shape=[wide, thin],
-        compiler_params=PARAMS,
+        compiler_params=params(24),
         cost_estimate=work,
         name="attend_last",
     )(own_queries, halves[1], halves[1], mixed, peak, total)
@@ -324,9 +390,9 @@
 
 def middle_kernel(
     core, tokens, attended, log_total, cotangent, w_out, w_in, w_mlp, gain,
-    layer_out, own_halves, other_halves, whole,
-    grad_middle, grads, logs_deltas, gain_grad,
+    layer_out, own_halves, other_halves, whole, grad_middle, grads, logs_deltas,
 ):
+
     rows, width = tokens.shape
     first = core[0] == 0
 
@@ -359,7 +425,6 @@
     whole[:, :FF] = grad_gate
     whole[:, FF : 2 * FF] = grad_up
     grad_second = dot_nt(grad_gate, w_in[:, :FF]) + dot_nt(grad_up, w_in[:, FF:])
-    gain_grad[...] = jnp.sum(grad_second * normed, axis=0, keepdims=True)
     grad_mid = upstream.astype(F32) + norm_back(grad_second, normed, rstd, gain_row)
     grad_middle[...] = grad_mid
     branch = grad_mid.astype(BF16)
@@ -379,81 +444,63 @@
     logs_deltas[...] = both.T
 
 
-SMEM_SPEC = pl.BlockSpec(memory_space=pltpu.SMEM)
-WHOLE = pl.BlockSpec()
-
-
 def middle_part(core, tokens, attended, log_total, cotangent, w_out, w_in, w_mlp, gain):
     rows, width = tokens.shape
+    wide, halves = (rows, width), (rows, HALVES_WIDTH)
     shapes = [
-        ((rows, width), BF16),
-        ((rows, HALVES_WIDTH), BF16),
-        ((rows, HALVES_WIDTH), BF16),
-        ((rows, 2 * FF + width), BF16),
-        ((rows, width), F32),
-        ((rows, width), BF16),
-        ((LANES, rows), F32),
-        ((1, width), F32),
+        (wide, BF16), (halves, BF16), (halves, BF16), ((rows, 2 * FF + width), BF16),
+        (wide, F32), (wide, BF16), ((LANES, rows), F32),
     ]
     return pl.pallas_call(
         middle_kernel,
         in_specs=[SMEM_SPEC] + [WHOLE] * 8,
         out_shape=[jax.ShapeDtypeStruct(*shape) for shape in shapes],
-        compiler_params=PARAMS,
+        compiler_params=params(32),
         cost_estimate=cost(4 * rows * width * (2 * width + 6 * FF), 24 * MIB),
         name="middle",
     )(core, tokens, attended, log_total, cotangent, w_out, w_in, w_mlp, gain)
 
 
-def rows_kernel(width, items, gained, *refs):
-    out = refs[-1]
-    at = 0
-    for k, (left_lanes, right_lanes) in enumerate(items):
-        left_own, left_other, right_own, right_other = refs[4 * k : 4 * k + 4]
-        left = jnp.concatenate([left_own[:, left_lanes], left_other[:, left_lanes]], axis=0)
-        made = left.shape[1]
-        turned = left.T
-        for start in range(right_lanes.start, right_lanes.stop, width):
-            lanes = slice(start, start + width)
-            right = jnp.concatenate([right_own[:, lanes], right_other[:, lanes]], axis=0)
-            out[at : at + made, :] = dot_nn(turned, right).astype(BF16)
-            at += made
-    if at < out.shape[0]:
-        out[at:, :] = jnp.zeros((out.shape[0] - at, width), BF16)
-    if gained:
-        own, other = refs[4 * len(items) : 4 * len(items) + 2]
-        half = own.shape[1]
-        tile = (16, half)
-        top = lax.broadcasted_iota(jnp.int32, tile, 0) == 0
-        row = jnp.broadcast_to(own[...] + other[...], tile)
-        out[at : at + 16, :half] = jnp.where(top, row, 0.0).astype(BF16)
-
-
-def grad_rows(width, pieces, items, gain=None):
-    lanes, arrays, used = [], [], 0
-    for left_own, left_other, left_lanes, right_own, right_other, right_lanes in items:
-        arrays += [left_own, left_other, right_own, right_other]
-        lanes.append((left_lanes, right_lanes))
-        blocks = (right_lanes.stop - right_lanes.start) // width
-        used += (left_lanes.stop - left_lanes.start) * blocks
-    flops = 4 * items[0][0].shape[0] * used * width
-    if gain is not None:
-        arrays += gain
-        used += 1
+def rows_kernel(own, other, upstream, upstream_other, whole, whole_other, out_mlp, out_in):
+    width = out_mlp.shape[1]
+    half, half_ff = width // 2, FF // 2
+    both = jnp.concatenate([own[...], other[...]], axis=0)
+    right = jnp.concatenate([upstream[...], upstream_other[...]], axis=0)
+    out_mlp[:half_ff, :] = dot_tn(both[:, :half_ff], right).astype(BF16)
+    branch = jnp.concatenate([whole[:, 2 * FF :], whole_other[:, 2 * FF :]], axis=0)
+    left = both[:, ATTENDED_AT : ATTENDED_AT + half]
+    out_mlp[half_ff : half_ff + half, :] = dot_tn(left, branch).astype(BF16)
+    turned = both[:, NORMED_AT : NORMED_AT + half].T
+    for k in range(2 * FF // width):
+        lanes = slice(k * width, (k + 1) * width)
+        right = jnp.concatenate([whole[:, lanes], whole_other[:, lanes]], axis=0)
+        out_in[k * half : (k + 1) * half, :] = dot_nn(turned, right).astype(BF16)
+    for out, used in ((out_mlp, half_ff + half), (out_in, 2 * FF // width * half)):
+        if used < out.shape[0]:
+            out[used:, :] = jnp.zeros((out.shape[0] - used, width), BF16)
+
+
+def padded(rows, pieces):
     unit = 8 * pieces
-    total = (used + unit - 1) // unit * unit
+    return (rows + unit - 1) // unit * unit
+
+
+def grad_rows(pieces, width, *arrays):
+    sizes = padded((FF + width) // 2, pieces), padded(FF, pieces)
     return pl.pallas_call(
-        partial(rows_kernel, width, lanes, gain is not None),
-        in_specs=[WHOLE] * len(arrays),
-        out_shape=jax.ShapeDtypeStruct((total, width), BF16),
-        compiler_params=PARAMS,
-        cost_estimate=cost(flops, 4 * total * width),
+        rows_kernel,
+        out_shape=[jax.ShapeDtypeStruct((size, width), BF16) for size in sizes],
+        compiler_params=params(16),
+        cost_estimate=cost(512 * 1728 * width, 12 * MIB),
         name="grad_rows",
     )(*arrays)
 
 
-def unpack_kernel(places, gained, bit, own, other, *outs):
+def unpack_kernel(places, gained, bit, own, other, *refs):
     half = own.shape[0]
+    if gained:
+        weights, gain = refs[:2]
+    outs = refs[2:] if gained else refs
 
     def put(low, high):
         at = 0
@@ -469,10 +516,6 @@
                     start = at + cut - half
                     ref[cut:, columns] = high[start : start + made - cut, :].astype(F32)
                 at += made
-        if gained:
-            ref = outs[-1]
-            source, row = (low, at) if at < half else (high, at - half)
-            ref[...] = source[row : row + 16, : ref.shape[1]].astype(F32)[:1]
 
     @pl.when(bit[0] == 0)
     def _():
@@ -482,21 +525,27 @@
     def _():
         put(other, own)
 
-
-def unpack(parts, shapes, gained=False):
-    own, other, bit = gather_rows(scatter_sum(parts))
+    if gained:
+        products = outs[0][...] * weights[...].astype(F32)
+        sums = jnp.sum(products, axis=1, keepdims=True)
+        row = jnp.broadcast_to(sums, (sums.shape[0], LANES)).T[:1]
+        outs[-1][...] = (row / gain[...].astype(F32)).reshape(outs[-1].shape)
+
+
+def unpack(chain, shapes, gained=()):
+    own, other = chain.parts
     width = own.shape[1]
     places = [(k, shape[1] // width) for k, shape in enumerate(shapes)]
     if gained:
-        shapes = shapes + [(1, width // 2)]
+        shapes = shapes + [gained[1].shape[1:]]
     return pl.pallas_call(
-        partial(unpack_kernel, places, gained),
-        in_specs=[SMEM_SPEC, WHOLE, WHOLE],
+        partial(unpack_kernel, places, bool(gained)),
+        in_specs=[SMEM_SPEC] + [WHOLE] * (2 + len(gained)),
         out_shape=[jax.ShapeDtypeStruct(shape, F32) for shape in shapes],
-        compiler_params=PARAMS,
+        compiler_params=params(24),
         cost_estimate=cost(0, 12 * own.size),
         name="unpack",
-    )(bit.reshape(1), own, other)
+    )(chain.bit.reshape(1), own, other, *gained)
 
 
 def unrotated(block, cos, sin):
@@ -557,7 +606,7 @@
             jax.ShapeDtypeStruct((2 * count, width), BF16),
             jax.ShapeDtypeStruct((2 * count, width), BF16),
         ],
-        compiler_params=PARAMS,
+        compiler_params=params(16 if count <= 1024 else 48),
         cost_estimate=cost(40 * rows * count * width, 20 * count * width),
         name="attend_back",
     )(
@@ -566,89 +615,102 @@
     )
 
 
-def back_project_kernel(
-    core, tokens_a, tokens_b, grad_q, grad_k, grad_v, weights, gain,
-    out_first, out_own, out_other, totals, gain_total,
+def late_rows_kernel(
+    core, low_a, low_b, grad_q, grad_k, grad_v, out_own, out_other, total
 ):
-    step = pl.program_id(0)
-    width = tokens_a.shape[1]
+    step, steps = pl.program_id(0), pl.num_programs(0)
+    own_rows, width = grad_q.shape
     half = width // 2
-    own_rows = grad_q.shape[0]
-    tokens = jnp.where(2 * step < pl.num_programs(0), tokens_a[...], tokens_b[...])
-    normed, _ = normalize(tokens.astype(F32))
-    low = (normed * gain[...].astype(F32)).astype(BF16)
-    grad_first = dot_nt(grad_k[...], weights[:, width : 2 * width])
-    grad_first = grad_first + dot_nt(grad_v[...], weights[:, 2 * width :])
+    low = jnp.where(2 * step < steps, low_a[...], low_b[...])
     turned = low.T
+    made_k, made_v = dot_nn(turned, grad_k[...]), dot_nn(turned, grad_v[...])
 
     @pl.when(step == 0)
     def _():
-        query_part = dot_nt(grad_q[...], weights[:, :width])
-        first = grad_first[:own_rows] + query_part
-        out_first[:own_rows, :] = first.astype(BF16)
-        out_first[own_rows:, :] = grad_first[own_rows:].astype(BF16)
-        gain_total[...] = jnp.sum(grad_first * normed, axis=0, keepdims=True) + jnp.sum(
-            query_part * normed[:own_rows], axis=0, keepdims=True
-        )
-        totals[:, :width] = dot_nn(turned[:, :own_rows], grad_q[...])
-        totals[:, width : 2 * width] = dot_nn(turned, grad_k[...])
-        totals[:, 2 * width :] = dot_nn(turned, grad_v[...])
+        total[:, :width] = dot_nn(turned[:, :own_rows], grad_q[...])
+        total[:, width : 2 * width] = made_k
+        total[:, 2 * width :] = made_v
 
     @pl.when(step > 0)
     def _():
-        out_first[...] = grad_first.astype(BF16)
-        gain_total[...] += jnp.sum(grad_first * normed, axis=0, keepdims=True)
-        totals[:, width : 2 * width] += dot_nn(turned, grad_k[...])
-        totals[:, 2 * width :] += dot_nn(turned, grad_v[...])
-
-    @pl.when(step == pl.num_programs(0) - 1)
+        total[:, width : 2 * width] += made_k
+        total[:, 2 * width :] += made_v
+
+    @pl.when(step == steps - 1)
     def _():
-        tile = (16, half)
-        top = lax.broadcasted_iota(jnp.int32, tile, 0) == 0
-        sides = gain_total[:, :half], gain_total[:, half:]
         for out, side in ((out_own, core[0]), (out_other, 1 - core[0])):
             start = pl.multiple_of(side * half, half)
             for k in range(3):
                 columns = slice(k * width, (k + 1) * width)
-                out[k * half : (k + 1) * half, :] = totals[pl.ds(start, half), columns].astype(BF16)
-            out[3 * half :, :] = jnp.zeros((out.shape[0] - 3 * half, width), BF16)
-            row = jnp.broadcast_to(jnp.where(side == 0, *sides), tile)
-            out[3 * half : 3 * half + 16, :half] = jnp.where(top, row, 0.0).astype(BF16)
-
-
-def back_project(core, pieces, tokens, grad_q, grad_k, grad_v, weights, gain):
-    count, width = tokens[0].shape
-    rows, own_rows = 2 * count, grad_q.shape[0]
-    step = min(count, 2 * own_rows)
+                out[k * half : (k + 1) * half, :] = total[pl.ds(start, half), columns].astype(BF16)
+            if out.shape[0] > 3 * half:
+                out[3 * half :, :] = jnp.zeros((out.shape[0] - 3 * half, width), BF16)
+
+
+def late_rows(core, pieces, lows, grad_q, grad_k, grad_v):
+    count, width = lows[0].shape
+    own_rows = grad_q.shape[0]
+    step = min(count, 512)
     each = count // step
-    unit = 8 * pieces
-    total = (3 * (width // 2) + 1 + unit - 1) // unit * unit
-    block = pl.BlockSpec((step, width), lambda i: (i, 0))
-
-    def fixed(shape):
-        return pl.BlockSpec(shape, lambda i: (0, 0))
-
+    total = padded(3 * width // 2, pieces)
+    grads = pl.BlockSpec((step, width), lambda i: (i, 0))
+    fixed = pl.BlockSpec((own_rows, width), lambda i: (0, 0))
+    made = pl.BlockSpec((total, width), lambda i: (0, 0))
     return pl.pallas_call(
-        back_project_kernel,
-        grid=(rows // step,),
+        late_rows_kernel,
+        grid=(2 * each,),
         in_specs=[
             SMEM_SPEC,
             pl.BlockSpec((step, width), lambda i: (jnp.minimum(i, each - 1), 0)),
             pl.BlockSpec((step, width), lambda i: (jnp.maximum(i - each, 0), 0)),
-            fixed((own_rows, width)), block, block,
-            fixed((width, 3 * width)), fixed((1, width)),
+            fixed, grads, grads,
         ],
-        out_specs=[block, fixed((total, width)), fixed((total, width))],
-        out_shape=[
-            jax.ShapeDtypeStruct((rows, width), BF16),
-            jax.ShapeDtypeStruct((total, width), BF16),
-            jax.ShapeDtypeStruct((total, width), BF16),
+        out_specs=[made, made],
+        out_shape=[jax.ShapeDtypeStruct((total, width), BF16)] * 2,
+        scratch_shapes=[pltpu.VMEM((width, 3 * width), F32)],
+        compiler_params=params(36),
+        cost_estimate=cost(4 * count * width * width, 8 * count * width),
+        name="late_rows",
+    )(core, *lows, grad_q, grad_k, grad_v)
+
+
+def first_rows_kernel(grad_q, grad_k, grad_v, weights, out):
+    width = grad_q.shape[1]
+    own_rows = grad_q.shape[0]
+    made = dot_nt(grad_k[...], weights[:, width : 2 * width])
+    made = made + dot_nt(grad_v[...], weights[:, 2 * width :])
+
+    @pl.when(pl.program_id(0) == 0)
+    def _():
+        own = made[:own_rows] + dot_nt(grad_q[...], weights[:, :width])
+        out[:own_rows, :] = own.astype(BF16)
+        out[own_rows:, :] = made[own_rows:].astype(BF16)
+
+    @pl.when(pl.program_id(0) > 0)
+    def _():
+        out[...] = made.astype(BF16)
+
+
+def first_rows(grad_q, grad_k, grad_v, weights):
+    rows, width = grad_k.shape
+    own_rows = grad_q.shape[0]
+    step = min(rows, 2 * own_rows)
+    block = pl.BlockSpec((step, width), lambda i: (i, 0))
+    return pl.pallas_call(
+        first_rows_kernel,
+        grid=(rows // step,),
+        in_specs=[
+            pl.BlockSpec((own_rows, width), lambda i: (0, 0)),
+            block,
+            block,
+            pl.BlockSpec((width, 3 * width), lambda i: (0, 0)),
         ],
-        scratch_shapes=[pltpu.VMEM((width, 3 * width), F32), pltpu.VMEM((1, width), F32)],
-        compiler_params=PARAMS,
-        cost_estimate=cost(8 * rows * width * width, 12 * rows * width),
-        name="back_project",
-    )(core, *tokens, grad_q, grad_k, grad_v, weights, gain)
+        out_specs=block,
+        out_shape=jax.ShapeDtypeStruct((rows, width), BF16),
+        compiler_params=params(16),
+        cost_estimate=cost(4 * rows * width * width, 8 * rows * width),
+        name="first_rows",
+    )(grad_q, grad_k, grad_v, weights)
 
 
 def last_kernel(tokens, grad_middle, part_a, part_b, gain, out):
@@ -662,7 +724,7 @@
     return pl.pallas_call(
         last_kernel,
         out_shape=jax.ShapeDtypeStruct(tokens.shape, BF16),
-        compiler_params=PARAMS,
+        compiler_params=params(24),
         cost_estimate=cost(20 * tokens.size, 12 * tokens.size),
         name="last",
     )(tokens, grad_middle, *parts, gain)
@@ -687,8 +749,8 @@
     upstream = cotangent.reshape(rows, width)
     pieces = lax.axis_size("seq") * lax.axis_size("ctx")
 
-    full_qkv = both_halves(w_qkv)
-    gathered, full_qkv = gather_context(own, full_qkv)
+    gathered = gather_context(own)
+    qkv_other = swap_cores(w_qkv)
     gains = jnp.stack([gain_attn, gain_mlp])
     gains_other = swap_cores(gains)
     gains_all = jnp.concatenate(
@@ -699,70 +761,59 @@
     full_in = both_halves(w_in)
     full_mlp = both_halves(w_mlp)
     upstream_other = swap_cores(upstream)
+
     blocks = gathered_blocks()
     positions = (blocks[:, None] * rows + jnp.arange(rows, dtype=jnp.int32)[None, :]).reshape(-1)
     cos, sin = rotary_tables(positions.astype(F32), 64)
     count = gathered[0].shape[0]
-    (first_half, queries), (last_half,) = [
-        project(
-            part, full_qkv, attn_gain,
-            cos[k * count : (k + 1) * count], sin[k * count : (k + 1) * count],
-            0 if k else rows,
-        )
-        for k, part in enumerate(gathered)
-    ]
+    core_at = core.reshape(1)
+    first_half, first_low, queries, full_qkv = project(
+        core_at, gathered[0], w_qkv, qkv_other, attn_gain, cos[:count], sin[:count], rows
+    )
+    last_half, last_low = project(
+        core_at, gathered[1], full_qkv, attn_gain, attn_gain, cos[count:], sin[count:], 0
+    )
     halves = first_half, last_half
     attended, log_total = attend(queries, halves)
     (
-        layer_out, own_halves, other_halves, whole,
-        grad_middle, grads, logs_deltas, gain_mlp_part,
+        layer_out, own_halves, other_halves, whole, grad_middle, grads, logs_deltas,
     ) = middle_part(
-        core.reshape(1), own, attended, log_total, upstream,
-        full_out, full_in, full_mlp, mlp_gain,
-    )
-
-    def gain_pair(part):
-        mine = lax.dynamic_slice_in_dim(part, core * half, half, 1)
-        theirs = lax.dynamic_slice_in_dim(part, (1 - core) * half, half, 1)
-        return [mine, swap_cores(theirs)]
-
-    other_halves = swap_cores(other_halves)
-    whole_other = swap_cores(whole)
-    mlp_rows = grad_rows(
-        width,
-        pieces,
-        [
-            (
-                own_halves, other_halves, slice(0, half_ff),
-                upstream, upstream_other, slice(0, width),
-            ),
-            (
-                own_halves, other_halves, slice(ATTENDED_AT, ATTENDED_AT + half),
-                whole, whole_other, slice(2 * FF, 2 * FF + width),
-            ),
-        ],
-        gain_pair(gain_mlp_part),
-    )
-    in_rows = grad_rows(
-        width,
-        pieces,
-        [
-            (
-                own_halves, other_halves, slice(NORMED_AT, NORMED_AT + half),
-                whole, whole_other, slice(0, 2 * FF),
-            )
-        ],
+        core_at, own, attended, log_total, upstream, full_out, full_in, full_mlp, mlp_gain
     )
 
     grad_q, grad_k, grad_v = attend_back(queries, halves, grads, logs_deltas, cos, sin)
-    first_rows, qkv_own, qkv_other = back_project(
-        core.reshape(1), pieces, gathered, grad_q, grad_k, grad_v, full_qkv, attn_gain
-    )
-    tokens_grad = last_part(own, grad_middle, scatter_context(first_rows), attn_gain)
-
-    mlp_grad, out_grad, gain_mlp_grad = unpack([mlp_rows], [(half_ff, width), (half, width)], True)
-    (in_grad,) = unpack([in_rows], [(half, 2 * FF)])
-    qkv_grad, gain_attn_grad = unpack([qkv_own, swap_cores(qkv_other)], [(half, 3 * width)], True)
+    other_halves, whole_other = swap_cores(other_halves), swap_cores(whole)
+    own_halves, grad_q = lax.optimization_barrier((own_halves, grad_q))
+    mlp_rows, in_rows = grad_rows(
+        pieces, width, own_halves, other_halves, upstream, upstream_other,
+        whole, whole_other,
+    )
+    (grad_q,) = after([grad_q], mlp_rows, in_rows)
+    late_own, late_other = late_rows(
+        core_at, pieces, (first_low, last_low), grad_q, grad_k, grad_v
+    )
+    chains = [
+        RowsSum([mlp_rows], MLP_ORDERS),
+        RowsSum([in_rows], IN_ORDERS),
+        RowsSum([late_own, swap_cores(late_other)], LATE_ORDERS),
+    ]
+    aways = lax.optimization_barrier(tuple(chain.first_away() for chain in chains))
+    for chain, away in zip(chains, aways):
+        chain.step(away)
+    (grad_q,) = after([grad_q], *aways)
+    chains.append(ContextSum(first_rows(grad_q, grad_k, grad_v, full_qkv)))
+    while any(chain.left for chain in chains):
+        for chain in chains:
+            if chain.left:
+                chain.step()
+    mlp_grad, out_grad = unpack(chains[0], [(half_ff, width), (half, width)])
+    in_grad, gain_mlp_grad = unpack(
+        chains[1], [(half, 2 * FF)], (w_in, gain_mlp.reshape(1, half))
+    )
+    qkv_grad, gain_attn_grad = unpack(
+        chains[2], [(half, 3 * width)], (w_qkv, gain_attn.reshape(1, half))
+    )
+    tokens_grad = last_part(own, grad_middle, chains[3].parts, attn_gain)
     return (
         layer_out.reshape(seqs_here, rows, width),
         tokens_grad.reshape(seqs_here, rows, width),
@@ -770,8 +821,8 @@
         out_grad,
         in_grad,
         mlp_grad,
-        gain_attn_grad.reshape(half),
-        gain_mlp_grad.reshape(half),
+        gain_attn_grad,
+        gain_mlp_grad,
     )
 
 

time: 238 us -> 209 us (0.88)
  starting transfers between devices: 48.3 us -> 36.2 us
  waiting for transfers between devices: 100 us -> 90.4 us
  other arithmetic: 23.2 us -> 18.3 us
    ppermute x30, starting transfers between devices: 46.2 us -> 34 us  [flip(): return lax.ppermute(block, ('seq', 'ctx', 'wsh'), route)]
    ppermute x30, waiting for transfers between devices: 95.5 us -> 90.4 us  [flip(): return lax.ppermute(block, ('seq', 'ctx', 'wsh'), route)]
    ppermute x10 -> x9, waiting for transfers between devices: 4.52 us -> 0.02 us  [swap_cores(): return lax.ppermute(block, 'wsh', [(0, 1), (1, 0)])]
    unnamed x58 -> x50, local copies, waits for them, and re-layouts: 14.5 us -> 10.2 us
    dynamic_slice x3 -> x2, local copies, waits for them, and re-layouts: 1.97 us -> 4.52 us  [summed(): lax.dynamic_slice_in_dim(part, first + start, size, 0).astype(F32)]
  transfers between devices with their start and end apart: 40 -> 39, of which waited for: 20 -> 13; matrix products, arithmetic and copies ran while one was open for 10% -> 11% of each run, Pallas kernels for 6% -> 12%
where the time goes in v3:
time: 209 us; the launch traced here: 208 us
  waiting for transfers between devices  90.4 us (43%)
  Pallas kernels  44.8 us (21%)
  starting transfers between devices  36.2 us (17%)
  other arithmetic  18.3 us (9%)
  local copies, waits for them, and re-layouts  17.1 us (8%)
    ppermute x30, waiting for transfers between devices, flip(): return lax.ppermute(block, ('seq', 'ctx', 'wsh'), route)  90.4 us
    ppermute x30, starting transfers between devices, flip(): return lax.ppermute(block, ('seq', 'ctx', 'wsh'), route)  34 us
    unnamed x50, local copies, waits for them, and re-layouts  10.2 us
    convert_element_type x13, other arithmetic, summed(): return sum(cut[1:], cut[0]).astype(BF16)  9.9 us
    pallas_call x1, Pallas kernels, attend_back(): pl.pallas_call(attend_back_kernel, grid=(pairs,), in_specs=[queries, keys...  7.42 us
    pallas_call x2, Pallas kernels, project(): pl.pallas_call(project_kernel, grid=(rows // step,), in_specs=[SMEM_SPEC,...  6.68 us
    pallas_call x3, Pallas kernels, unpack(): pl.pallas_call(partial(unpack_kernel, places, bool(gained)), in_specs=[SM...  6.51 us
    pallas_call x1, Pallas kernels, late_rows(): pl.pallas_call(late_rows_kernel, grid=(2 * each,), in_specs=[SMEM_SPEC, p...  5.61 us
  transfers between devices with their start and end apart: 39, of which 13 were waited for; matrix products, arithmetic and copies ran while one was open for 11% of the time, Pallas kernels for 12%

profile of v3, /device:TPU:0, one launch (start us, length us, event | category | flops | bytes accessed | tf_op | source)
XLA Modules:
  0.0 208.3 jit_solution(4979033242744406509)
XLA Ops:
  0.6 4.1 %collective-permute-start = (bf16[128,768]{1,0:T(8,128)(2,1)}, bf16[128,768]{1,0:T(8,128)(2,1)S(1)}, u32[]{:S(2)}, u32[]{:S(2)}) collective-permute-start(bf16[128,768]{1,0:T(8,128)(2,1)} %bitcast.10), channel_id=1, source_target_pairs={{0,8},{1,3},{2,10},{3,1},{4,12},{5,7},{6,14},{7,5},{8,0},{9,11},{1... | collective-permute-start | bytes 589832 | tf_op jit(solution)/shard_map/ppermute | solution.py:42
  12.7 10.2 %collective-permute-done.1 = bf16[256,768]{1,0:T(8,128)(2,1)S(1)} collective-permute-done((bf16[256,768]{1,0:T(8,128)(2,1)S(1)}, bf16[256,768]{1,0:T(8,128)(2,1)S(1)}, u32[]{:S(2)}, u32[]{:S(2)}) %collective-permute-start.1) | collective-permute-done | bytes 393248 | tf_op jit(solution)/shard_map/ppermute | solution.py:42
  28.1 4.5 %project.2 = (bf16[512,1536]{1,0:T(8,128)(2,1)S(1)}, bf16[512,768]{1,0:T(8,128)(2,1)S(1)}, bf16[128,768]{1,0:T(8,128)(2,1)S(1)}, bf16[768,2304]{1,0:T(8,128)(2,1)S(1)}) custom-call(s32[1]{0:T(128)} %bitcast.core, bf16[512,768]{1,0:T(8,128)(2,1)S(1)} %pad_maximum_fusion.5.tokens, bf16[384,2304]{1,0:T(8,128)(2,1)S(1)} %copy-done.1, ...), custom_call_target="tpu_custom_call" | custom-call | flops 1207959552 | bytes 3145728 | tf_op jit(solution)/shard_map/project/pallas_call | solution.py:262
  32.7 3.4 %attend_first.1 = (f32[128,768]{1,0:T(8,128)S(1)}, f32[128,128]{1,0:T(8,128)S(1)}, f32[128,128]{1,0:T(8,128)S(1)}) custom-call(bf16[128,768]{1,0:T(8,128)(2,1)S(1)} %get-tuple-element.46.queries, bf16[512,1536]{1,0:T(8,128)(2,1)S(1)} %get-tuple-element.49.keys.values.keys_a.values_a, bf16[512,1536]{1,0:T(8,128)(2,1)S(1)} %get-tuple-element.49.keys.values.keys_a.values_a), custom_call_target="tpu_custom_call" | custom-call | flops 402653184 | bytes 2359296 | tf_op jit(solution)/shard_map/attend_first/pallas_call | solution.py:369
  38.5 4.6 %attend_last.1 = (f32[128,768]{1,0:T(8,128)S(1)}, f32[128,128]{1,0:T(8,128)S(1)}) custom-call(bf16[128,768]{1,0:T(8,128)(2,1)S(1)} %get-tuple-element.46.queries, bf16[512,1536]{1,0:T(8,128)(2,1)S(1)} %get-tuple-element.48.keys.values.keys_b.values_b, bf16[512,1536]{1,0:T(8,128)(2,1)S(1)} %get-tuple-element.48.keys.values.keys_b.values_b, ...), custom_call_target="tpu_custom_call" | custom-call | flops 402653184 | bytes 2359296 | tf_op jit(solution)/shard_map/attend_last/pallas_call | solution.py:379
  43.1 4.6 %middle.1 = (bf16[128,768]{1,0:T(8,128)(2,1)}, bf16[128,1408]{1,0:T(8,128)(2,1)S(1)}, bf16[128,1408]{1,0:T(8,128)(2,1)S(1)}, bf16[128,3072]{1,0:T(8,128)(2,1)S(1...) custom-call(s32[1]{0:T(128)} %bitcast.core, bf16[128,768]{1,0:T(8,128)(2,1)S(1)} %bitcast.13, ...), custom_call_target="tpu_custom_call" | custom-call | flops 3321888768 | bytes 25165824 | tf_op jit(solution)/shard_map/middle/pallas_call | solution.py:454
  48.4 7.4 %attend_back.1 = (bf16[128,768]{1,0:T(8,128)(2,1)S(1)}, bf16[1024,768]{1,0:T(8,128)(2,1)S(1)}, bf16[1024,768]{1,0:T(8,128)(2,1)S(1)}) custom-call(bf16[128,768]{1,0:T(8,128)(2,1)S(1)} %get-tuple-element.46.queries, bf16[512,1536]{1,0:T(8,128)(2,1)S(1)} %get-tuple-element.49.keys.values.keys_a.values_a, ...), custom_call_target="tpu_custom_call" | custom-call | flops 2013265920 | bytes 7864320 | tf_op jit(solution)/shard_map/attend_back/pallas_call | solution.py:599
  59.3 5.6 %late_rows.1 = (bf16[1152,768]{1,0:T(8,128)(2,1)S(1)}, bf16[1152,768]{1,0:T(8,128)(2,1)}) custom-call(s32[1]{0:T(128)} %bitcast.core, bf16[512,768]{1,0:T(8,128)(2,1)S(1)} %get-tuple-element.68.low_a, bf16[512,768]{1,0:T(8,128)(2,1)S(1)} %get-tuple-element.69.low_b, bf16[128,768]{1,0:T(8,128)(2,1)S(1)} %get-tuple-element.77.grad_q, ...), custom_call_target="tpu_custom_call" | custom-call | flops 1207959552 | bytes 3145728 | tf_op jit(solution)/shard_map/late_rows/pallas_call | solution.py:659
  72.4 2.4 %add_convert_fusion = bf16[576,768]{1,0:T(8,128)(2,1)} fusion(bf16[1152,768]{1,0:T(8,128)(2,1)} %collective-permute-done.11, s32[]{:T(128)S(6)} %select_n.308, bf16[1152,768]{1,0:T(8,128)(2,1)S(1)} %copy-done.5), kind=kLoop, calls=%fused_computation.2 | loop fusion | flops 1769472 | bytes 2654212 | tf_op jit(solution)/shard_map/convert_element_type | solution.py:117
  80.1 3.9 %first_rows.1 = bf16[1024,768]{1,0:T(8,128)(2,1)S(1)} custom-call(bf16[128,768]{1,0:T(8,128)(2,1)S(1)} %copy-done.20, bf16[1024,768]{1,0:T(8,128)(2,1)S(1)} %copy-done.11, bf16[1024,768]{1,0:T(8,128)(2,1)S(1)} %copy-done.13, bf16[768,2304]{1,0:T(8,128)(2,1)S(1)} %copy-done.3), custom_call_target="tpu_custom_call" | custom-call | flops 2415919104 | bytes 6291456 | tf_op jit(solution)/shard_map/first_rows/pallas_call | solution.py:699
  87.6 7.0 %collective-permute-done.23 = bf16[512,768]{1,0:T(8,128)(2,1)} collective-permute-done((bf16[512,768]{1,0:T(8,128)(2,1)}, bf16[512,768]{1,0:T(8,128)(2,1)}, u32[]{:S(2)}, u32[]{:S(2)}) %collective-permute-start.23) | collective-permute-done | bytes 786464 | tf_op jit(solution)/shard_map/ppermute | solution.py:42
  94.6 2.4 %add_convert_fusion.6 = (bf16[256,768]{1,0:T(8,128)(2,1)}, bf16[256,768]{1,0:T(8,128)(2,1)}) fusion(bf16[512,768]{1,0:T(8,128)(2,1)} %collective-permute-done.23, s32[]{:T(128)S(6)} %select_n.334, bf16[1024,768]{1,0:T(8,128)(2,1)} %copy-done.16, s32[]{:T(128)S(6)} %select_n.333, s32[]{:T(128)S(6)} %select_n.337, s32[]{:T(128)S(6)} %select_n.336), kind=kLoop, calls=%fused_computation.17 | loop fusion | flops 1572864 | bytes 2359312 | tf_op jit(solution)/shard_map/convert_element_type | solution.py:117
  102.7 10.1 %collective-permute-done.24 = bf16[256,768]{1,0:T(8,128)(2,1)} collective-permute-done((bf16[256,768]{1,0:T(8,128)(2,1)}, bf16[256,768]{1,0:T(8,128)(2,1)}, u32[]{:S(2)}, u32[]{:S(2)}) %collective-permute-start.24) | collective-permute-done | bytes 393248 | tf_op jit(solution)/shard_map/ppermute | solution.py:42
  124.2 6.6 %collective-permute-done.26 = bf16[64,768]{1,0:T(8,128)(2,1)S(1)} collective-permute-done((bf16[64,768]{1,0:T(8,128)(2,1)S(1)}, bf16[64,768]{1,0:T(8,128)(2,1)S(1)}, u32[]{:S(2)}, u32[]{:S(2)}) %collective-permute-start.26) | collective-permute-done | bytes 98336 | tf_op jit(solution)/shard_map/ppermute | solution.py:42
  130.9 3.5 %collective-permute-start.27 = (bf16[64,768]{1,0:T(8,128)(2,1)S(1)}, bf16[64,768]{1,0:T(8,128)(2,1)S(1)}, u32[]{:S(2)}, u32[]{:S(2)}) collective-permute-start(bf16[64,768]{1,0:T(8,128)(2,1)S(1)} %add_convert_fusion.23), channel_id=1, source_target_pairs={{0,8},{1,5},{2,10},{3,7},{4,12},{5,1},{6,14},{7,3},{8,0},{9,13},{1... | collective-permute-start | bytes 294920 | tf_op jit(solution)/shard_map/ppermute | solution.py:42
  134.5 5.3 %collective-permute-done.17 = bf16[144,768]{1,0:T(8,128)(2,1)S(1)} collective-permute-done((bf16[144,768]{1,0:T(8,128)(2,1)S(1)}, bf16[144,768]{1,0:T(8,128)(2,1)S(1)}, u32[]{:S(2)}, u32[]{:S(2)}) %collective-permute-start.17) | collective-permute-done | bytes 221216 | tf_op jit(solution)/shard_map/ppermute | solution.py:42
  142.0 5.6 %collective-permute-done.18 = bf16[72,768]{1,0:T(8,128)(2,1)S(1)} collective-permute-done((bf16[72,768]{1,0:T(8,128)(2,1)S(1)}, bf16[72,768]{1,0:T(8,128)(2,1)S(1)}, u32[]{:S(2)}, u32[]{:S(2)}) %collective-permute-start.18) | collective-permute-done | bytes 110624 | tf_op jit(solution)/shard_map/ppermute | solution.py:42
  149.6 7.5 %collective-permute-done.19 = bf16[72,768]{1,0:T(8,128)(2,1)S(1)} collective-permute-done((bf16[72,768]{1,0:T(8,128)(2,1)S(1)}, bf16[72,768]{1,0:T(8,128)(2,1)S(1)}, u32[]{:S(2)}, u32[]{:S(2)}) %collective-permute-start.19) | collective-permute-done | bytes 110624 | tf_op jit(solution)/shard_map/ppermute | solution.py:42
  160.1 3.0 %collective-permute-done.20 = bf16[144,768]{1,0:T(8,128)(2,1)S(1)} collective-permute-done((bf16[144,768]{1,0:T(8,128)(2,1)S(1)}, bf16[144,768]{1,0:T(8,128)(2,1)S(1)}, u32[]{:S(2)}, u32[]{:S(2)}) %collective-permute-start.20) | collective-permute-done | bytes 221216 | tf_op jit(solution)/shard_map/ppermute | solution.py:42
  165.3 15.1 %collective-permute-done.36 = bf16[144,768]{1,0:T(8,128)(2,1)S(1)} collective-permute-done((bf16[144,768]{1,0:T(8,128)(2,1)S(1)}, bf16[144,768]{1,0:T(8,128)(2,1)S(1)}, u32[]{:S(2)}, u32[]{:S(2)}) %collective-permute-start.36) | collective-permute-done | bytes 221216 | tf_op jit(solution)/shard_map/ppermute | solution.py:42
  181.5 7.3 %collective-permute-done.37 = bf16[288,768]{1,0:T(8,128)(2,1)S(1)} collective-permute-done((bf16[288,768]{1,0:T(8,128)(2,1)S(1)}, bf16[288,768]{1,0:T(8,128)(2,1)S(1)}, u32[]{:S(2)}, u32[]{:S(2)}) %collective-permute-start.37) | collective-permute-done | bytes 442400 | tf_op jit(solution)/shard_map/ppermute | solution.py:42
  190.0 7.6 %collective-permute-done.14.part_b = bf16[128,768]{1,0:T(8,128)(2,1)S(1)} collective-permute-done((bf16[128,768]{1,0:T(8,128)(2,1)S(1)}, bf16[128,768]{1,0:T(8,128)(2,1)S(1)}, u32[]{:S(2)}, u32[]{:S(2)}) %collective-permute-start.14) | collective-permute-done | bytes 196640 | tf_op jit(solution)/shard_map/ppermute | solution.py:42
  198.6 3.1 %collective-permute-done.30.other = bf16[512,768]{1,0:T(8,128)(2,1)S(1)} collective-permute-done((bf16[512,768]{1,0:T(8,128)(2,1)S(1)}, bf16[512,768]{1,0:T(8,128)(2,1)S(1)}, u32[]{:S(2)}, u32[]{:S(2)}) %collective-permute-start.30) | collective-permute-done | bytes 786464 | tf_op jit(solution)/shard_map/ppermute | solution.py:42
  205.9 2.4 %unpack.5 = (f32[384,2304]{1,0:T(8,128)}, f32[384]{0:T(512)}) custom-call(s32[1]{0:T(128)} %bitcast.8.bit, bf16[576,768]{1,0:T(8,128)(2,1)S(1)} %pad_maximum_fusion.4.own, bf16[576,768]{1,0:T(8,128)(2,1)S(1)} %collective-permute-done.38.other, bf16[384,2304]{1,0:T(8,128)(2,1)S(1)} %copy-done, bf16[1,384]{1,0:T(2,128)(2,1)S(1)} %stack.10.refs_1_), custom_call_target="tpu_custom_call" | custom-call | bytes 5308416 | tf_op jit(solution)/shard_map/unpack/pallas_call | solution.py:541
  (173 shorter events, 69.6 us)
Async XLA Ops:
  4.7 23.4 %collective-permute-start.2 = (bf16[384,2304]{1,0:T(8,128)(2,1)}, bf16[384,2304]{1,0:T(8,128)(2,1)}, u32[]{:S(2)}, u32[]{:S(2)}) collective-permute-start(bf16[384,2304]{1,0:T(8,128)(2,1)} %refs_0_.2), channel_id=1, source_target_pairs={{0,1},{1,0},{2,3},{3,2},{4,5},{5,4},{6,7},{7,6},{8,9},{9,8},{10,11... | collective-permute-start | bytes 5308424 | tf_op jit(solution)/shard_map/ppermute | solution.py:46
  6.7 17.9 %collective-permute-start.5 = (bf16[384,768]{1,0:T(8,128)(2,1)}, bf16[384,768]{1,0:T(8,128)(2,1)S(1)}, u32[]{:S(2)}, u32[]{:S(2)}) collective-permute-start(bf16[384,768]{1,0:T(8,128)(2,1)} %param.12), channel_id=1, source_target_pairs={{0,1},{1,0},{2,3},{3,2},{4,5},{5,4},{6,7},{7,6},{8,9},{9,8},{10,11... | collective-permute-start | bytes 1769480 | tf_op jit(solution)/shard_map/ppermute | solution.py:46
  6.8 18.3 %collective-permute-start.6 = (bf16[384,2304]{1,0:T(8,128)(2,1)}, bf16[384,2304]{1,0:T(8,128)(2,1)}, u32[]{:S(2)}, u32[]{:S(2)}) collective-permute-start(bf16[384,2304]{1,0:T(8,128)(2,1)} %refs_0_.3), channel_id=1, source_target_pairs={{0,1},{1,0},{2,3},{3,2},{4,5},{5,4},{6,7},{7,6},{8,9},{9,8},{10,11... | collective-permute-start | bytes 5308424 | tf_op jit(solution)/shard_map/ppermute | solution.py:46
  10.9 12.1 %collective-permute-start.1 = (bf16[256,768]{1,0:T(8,128)(2,1)S(1)}, bf16[256,768]{1,0:T(8,128)(2,1)S(1)}, u32[]{:S(2)}, u32[]{:S(2)}) collective-permute-start(bf16[256,768]{1,0:T(8,128)(2,1)S(1)} %pad_maximum_fusion.11), channel_id=1, source_target_pairs={{0,4},{1,9},{2,6},{3,11},{4,0},{5,13},{6,2},{7,15},{8,12},{9,1},{1... | collective-permute-start | bytes 1179656 | tf_op jit(solution)/shard_map/ppermute | solution.py:42
  12.6 12.2 %collective-permute-start.7 = (bf16[576,768]{1,0:T(8,128)(2,1)S(1)}, bf16[576,768]{1,0:T(8,128)(2,1)S(1)}, u32[]{:S(2)}, u32[]{:S(2)}) collective-permute-start(bf16[576,768]{1,0:T(8,128)(2,1)S(1)} %copy-done.23), channel_id=1, source_target_pairs={{0,1},{1,0},{2,3},{3,2},{4,5},{5,4},{6,7},{7,6},{8,9},{9,8},{10,11... | collective-permute-start | bytes 2654216 | tf_op jit(solution)/shard_map/ppermute | solution.py:46
  23.0 13.3 %collective-permute-start.4 = (bf16[512,768]{1,0:T(8,128)(2,1)S(1)}, bf16[512,768]{1,0:T(8,128)(2,1)S(1)}, u32[]{:S(2)}, u32[]{:S(2)}) collective-permute-start(bf16[512,768]{1,0:T(8,128)(2,1)S(1)} %pad_maximum_fusion.5.tokens), channel_id=1, source_target_pairs={{0,2},{1,5},{2,0},{3,7},{4,6},{5,1},{6,4},{7,3},{8,10},{9,13},{10,... | collective-permute-start | bytes 2359304 | tf_op jit(solution)/shard_map/ppermute | solution.py:42
  74.7 19.8 %collective-permute-start.23 = (bf16[512,768]{1,0:T(8,128)(2,1)}, bf16[512,768]{1,0:T(8,128)(2,1)}, u32[]{:S(2)}, u32[]{:S(2)}) collective-permute-start(bf16[512,768]{1,0:T(8,128)(2,1)} %constant_dynamic-slice_fusion.1), channel_id=1, source_target_pairs={{0,2},{1,3},{2,0},{3,1},{4,6},{5,7},{6,4},{7,5},{8,10},{9,11},{10,... | collective-permute-start | bytes 2359304 | tf_op jit(solution)/shard_map/ppermute | solution.py:42
  75.2 21.8 %collective-permute-start.15 = (bf16[576,768]{1,0:T(8,128)(2,1)}, bf16[576,768]{1,0:T(8,128)(2,1)}, u32[]{:S(2)}, u32[]{:S(2)}) collective-permute-start(bf16[576,768]{1,0:T(8,128)(2,1)} %add_convert_fusion), channel_id=1, source_target_pairs={{0,16},{1,9},{2,18},{3,11},{4,20},{5,13},{6,22},{7,15},{8,24},{9,1... | collective-permute-start | bytes 2654216 | tf_op jit(solution)/shard_map/ppermute | solution.py:42
  76.7 23.6 %collective-permute-start.31 = (bf16[576,768]{1,0:T(8,128)(2,1)}, bf16[576,768]{1,0:T(8,128)(2,1)}, u32[]{:S(2)}, u32[]{:S(2)}) collective-permute-start(bf16[576,768]{1,0:T(8,128)(2,1)} %constant_dynamic-slice_fusion), channel_id=1, source_target_pairs={{0,16},{1,5},{2,18},{3,7},{4,20},{5,1},{6,22},{7,3},{8,24},{9,13},... | collective-permute-start | bytes 2654216 | tf_op jit(solution)/shard_map/ppermute | solution.py:42
  86.1 29.4 %collective-permute-start.12 = (bf16[512,768]{1,0:T(8,128)(2,1)}, bf16[512,768]{1,0:T(8,128)(2,1)}, u32[]{:S(2)}, u32[]{:S(2)}) collective-permute-start(bf16[512,768]{1,0:T(8,128)(2,1)} %slice.70), channel_id=1, source_target_pairs={{0,2},{1,5},{2,0},{3,7},{4,6},{5,1},{6,4},{7,3},{8,10},{9,13},{10,... | collective-permute-start | bytes 2359304 | tf_op jit(solution)/shard_map/ppermute | solution.py:42
  97.0 15.8 %collective-permute-start.24 = (bf16[256,768]{1,0:T(8,128)(2,1)}, bf16[256,768]{1,0:T(8,128)(2,1)}, u32[]{:S(2)}, u32[]{:S(2)}) collective-permute-start(bf16[256,768]{1,0:T(8,128)(2,1)} %get-tuple-element.91), channel_id=1, source_target_pairs={{0,4},{1,9},{2,6},{3,11},{4,0},{5,13},{6,2},{7,15},{8,12},{9,1},{1... | collective-permute-start | bytes 1179656 | tf_op jit(solution)/shard_map/ppermute | solution.py:42
  99.2 17.7 %collective-permute-start.16 = (bf16[288,768]{1,0:T(8,128)(2,1)S(1)}, bf16[288,768]{1,0:T(8,128)(2,1)S(1)}, u32[]{:S(2)}, u32[]{:S(2)}) collective-permute-start(bf16[288,768]{1,0:T(8,128)(2,1)S(1)} %get-tuple-element.85), channel_id=1, source_target_pairs={{0,2},{1,17},{2,0},{3,19},{4,6},{5,21},{6,4},{7,23},{8,10},{9,25},... | collective-permute-start | bytes 1327112 | tf_op jit(solution)/shard_map/ppermute | solution.py:42
  101.6 21.1 %collective-permute-start.32 = (bf16[288,768]{1,0:T(8,128)(2,1)S(1)}, bf16[288,768]{1,0:T(8,128)(2,1)S(1)}, u32[]{:S(2)}, u32[]{:S(2)}) collective-permute-start(bf16[288,768]{1,0:T(8,128)(2,1)S(1)} %get-tuple-element.89), channel_id=1, source_target_pairs={{0,2},{1,17},{2,0},{3,19},{4,6},{5,21},{6,4},{7,23},{8,10},{9,25},... | collective-permute-start | bytes 1327112 | tf_op jit(solution)/shard_map/ppermute | solution.py:42
  116.8 73.0 %collective-permute-start.13 = (bf16[256,768]{1,0:T(8,128)(2,1)S(1)}, bf16[256,768]{1,0:T(8,128)(2,1)S(1)}, u32[]{:S(2)}, u32[]{:S(2)}) collective-permute-start(bf16[256,768]{1,0:T(8,128)(2,1)S(1)} %get-tuple-element.93), channel_id=1, source_target_pairs={{0,4},{1,9},{2,6},{3,11},{4,0},{5,13},{6,2},{7,15},{8,12},{9,1},{1... | collective-permute-start | bytes 1179656 | tf_op jit(solution)/shard_map/ppermute | solution.py:42
  117.0 22.7 %collective-permute-start.17 = (bf16[144,768]{1,0:T(8,128)(2,1)S(1)}, bf16[144,768]{1,0:T(8,128)(2,1)S(1)}, u32[]{:S(2)}, u32[]{:S(2)}) collective-permute-start(bf16[144,768]{1,0:T(8,128)(2,1)S(1)} %get-tuple-element.105), channel_id=1, source_target_pairs={{0,4},{1,3},{2,6},{3,1},{4,0},{5,7},{6,2},{7,5},{8,12},{9,11},{10,... | collective-permute-start | bytes 663560 | tf_op jit(solution)/shard_map/ppermute | solution.py:42
  122.9 17.0 %collective-permute-start.33 = (bf16[144,768]{1,0:T(8,128)(2,1)S(1)}, bf16[144,768]{1,0:T(8,128)(2,1)S(1)}, u32[]{:S(2)}, u32[]{:S(2)}) collective-permute-start(bf16[144,768]{1,0:T(8,128)(2,1)S(1)} %get-tuple-element.101), channel_id=1, source_target_pairs={{0,8},{1,3},{2,10},{3,1},{4,12},{5,7},{6,14},{7,5},{8,0},{9,11},{1... | collective-permute-start | bytes 663560 | tf_op jit(solution)/shard_map/ppermute | solution.py:42
  141.4 15.9 %collective-permute-start.28 = (bf16[128,768]{1,0:T(8,128)(2,1)S(1)}, bf16[128,768]{1,0:T(8,128)(2,1)S(1)}, u32[]{:S(2)}, u32[]{:S(2)}) collective-permute-start(bf16[128,768]{1,0:T(8,128)(2,1)S(1)} %pad_maximum_fusion.15), channel_id=1, source_target_pairs={{0,16},{1,17},{2,18},{3,19},{4,20},{5,21},{6,22},{7,23},{8,24},{9,... | collective-permute-start | bytes 589832 | tf_op jit(solution)/shard_map/ppermute | solution.py:42
  147.8 11.6 %collective-permute-start.35 = (bf16[72,768]{1,0:T(8,128)(2,1)S(1)}, bf16[72,768]{1,0:T(8,128)(2,1)S(1)}, u32[]{:S(2)}, u32[]{:S(2)}) collective-permute-start(bf16[72,768]{1,0:T(8,128)(2,1)S(1)} %add_convert_fusion.17), channel_id=1, source_target_pairs={{0,4},{1,9},{2,6},{3,11},{4,0},{5,13},{6,2},{7,15},{8,12},{9,1},{1... | collective-permute-start | bytes 331784 | tf_op jit(solution)/shard_map/ppermute | solution.py:42
  157.4 23.2 %collective-permute-start.29 = (bf16[256,768]{1,0:T(8,128)(2,1)S(1)}, bf16[256,768]{1,0:T(8,128)(2,1)S(1)}, u32[]{:S(2)}, u32[]{:S(2)}) collective-permute-start(bf16[256,768]{1,0:T(8,128)(2,1)S(1)} %pad_maximum_fusion.12), channel_id=1, source_target_pairs={{0,4},{1,9},{2,6},{3,11},{4,0},{5,13},{6,2},{7,15},{8,12},{9,1},{1... | collective-permute-start | bytes 1179656 | tf_op jit(solution)/shard_map/ppermute | solution.py:42
  159.5 20.8 %collective-permute-start.36 = (bf16[144,768]{1,0:T(8,128)(2,1)S(1)}, bf16[144,768]{1,0:T(8,128)(2,1)S(1)}, u32[]{:S(2)}, u32[]{:S(2)}) collective-permute-start(bf16[144,768]{1,0:T(8,128)(2,1)S(1)} %pad_maximum_fusion.14), channel_id=1, source_target_pairs={{0,8},{1,3},{2,10},{3,1},{4,12},{5,7},{6,14},{7,5},{8,0},{9,11},{1... | collective-permute-start | bytes 663560 | tf_op jit(solution)/shard_map/ppermute | solution.py:42
  163.3 17.4 %collective-permute-start.21 = (bf16[288,768]{1,0:T(8,128)(2,1)S(1)}, bf16[288,768]{1,0:T(8,128)(2,1)S(1)}, u32[]{:S(2)}, u32[]{:S(2)}) collective-permute-start(bf16[288,768]{1,0:T(8,128)(2,1)S(1)} %pad_maximum_fusion.9), channel_id=1, source_target_pairs={{0,2},{1,17},{2,0},{3,19},{4,6},{5,21},{6,4},{7,23},{8,10},{9,25},... | collective-permute-start | bytes 1327112 | tf_op jit(solution)/shard_map/ppermute | solution.py:42
  180.9 22.6 %collective-permute-start.22 = (bf16[576,768]{1,0:T(8,128)(2,1)S(1)}, bf16[576,768]{1,0:T(8,128)(2,1)S(1)}, u32[]{:S(2)}, u32[]{:S(2)}) collective-permute-start(bf16[576,768]{1,0:T(8,128)(2,1)S(1)} %pad_maximum_fusion.3.own), channel_id=1, source_target_pairs={{0,16},{1,9},{2,18},{3,11},{4,20},{5,13},{6,22},{7,15},{8,24},{9,1... | collective-permute-start | bytes 2654216 | tf_op jit(solution)/shard_map/ppermute | solution.py:42
  189.1 16.8 %collective-permute-start.38 = (bf16[576,768]{1,0:T(8,128)(2,1)S(1)}, bf16[576,768]{1,0:T(8,128)(2,1)S(1)}, u32[]{:S(2)}, u32[]{:S(2)}) collective-permute-start(bf16[576,768]{1,0:T(8,128)(2,1)S(1)} %pad_maximum_fusion.4.own), channel_id=1, source_target_pairs={{0,16},{1,5},{2,18},{3,7},{4,20},{5,1},{6,22},{7,3},{8,24},{9,13},... | collective-permute-start | bytes 2654216 | tf_op jit(solution)/shard_map/ppermute | solution.py:42
  189.7 12.1 %collective-permute-start.30 = (bf16[512,768]{1,0:T(8,128)(2,1)S(1)}, bf16[512,768]{1,0:T(8,128)(2,1)S(1)}, u32[]{:S(2)}, u32[]{:S(2)}) collective-permute-start(bf16[512,768]{1,0:T(8,128)(2,1)S(1)} %pad_maximum_fusion.6.own), channel_id=1, source_target_pairs={{0,2},{1,3},{2,0},{3,1},{4,6},{5,7},{6,4},{7,5},{8,10},{9,11},{10,... | collective-permute-start | bytes 2359304 | tf_op jit(solution)/shard_map/ppermute | solution.py:42
  (40 other events, 251.4 us)

commit v4 on v3

--- a/solution.py
+++ b/solution.py
@@ -15,9 +15,9 @@
 NORMED_AT = 640
 ATTENDED_AT = 1024
 HALVES_WIDTH = 1408
-MLP_ORDERS = ("yaxb", "ybxa")
-IN_ORDERS = ("xyba", "axyb")
-LATE_ORDERS = ("xyab", "bxya")
+MLP_ORDERS = ("axyb", "byxa")
+IN_ORDERS = ("xyab", "yxba")
+LATE_ORDERS = ("xayb", "ybxa")
 MIB = 1 << 20
 BF16 = jnp.bfloat16
 F32 = jnp.float32
@@ -668,7 +668,7 @@
         out_specs=[made, made],
         out_shape=[jax.ShapeDtypeStruct((total, width), BF16)] * 2,
         scratch_shapes=[pltpu.VMEM((width, 3 * width), F32)],
-        compiler_params=params(36),
+        compiler_params=params(24),
         cost_estimate=cost(4 * count * width * width, 8 * count * width),
         name="late_rows",
     )(core, *lows, grad_q, grad_k, grad_v)

time: 209 us -> 199 us (0.952)
  waiting for transfers between devices: 90.4 us -> 77.4 us
    ppermute x30, waiting for transfers between devices: 90.4 us -> 77.4 us  [flip(): return lax.ppermute(block, ('seq', 'ctx', 'wsh'), route)]
  transfers between devices with their start and end apart: 39 -> 39, of which waited for: 13 -> 15; matrix products, arithmetic and copies ran while one was open for 11% -> 12% of each run, Pallas kernels for 12% -> 12%
where the time goes in v4:
time: 199 us; the launch traced here: 197 us
  waiting for transfers between devices  77.4 us (39%)
  Pallas kernels  44.9 us (23%)
  starting transfers between devices  38 us (19%)
  other arithmetic  18.4 us (9%)
  local copies, waits for them, and re-layouts  17.1 us (9%)
    ppermute x30, waiting for transfers between devices, flip(): return lax.ppermute(block, ('seq', 'ctx', 'wsh'), route)  77.4 us
    ppermute x30, starting transfers between devices, flip(): return lax.ppermute(block, ('seq', 'ctx', 'wsh'), route)  35.8 us
    unnamed x50, local copies, waits for them, and re-layouts  10.2 us
    convert_element_type x13, other arithmetic, summed(): return sum(cut[1:], cut[0]).astype(BF16)  9.99 us
    pallas_call x1, Pallas kernels, attend_back(): pl.pallas_call(attend_back_kernel, grid=(pairs,), in_specs=[queries, keys...  7.42 us
    pallas_call x2, Pallas kernels, project(): pl.pallas_call(project_kernel, grid=(rows // step,), in_specs=[SMEM_SPEC,...  6.68 us
    pallas_call x3, Pallas kernels, unpack(): pl.pallas_call(partial(unpack_kernel, places, bool(gained)), in_specs=[SM...  6.51 us
    pallas_call x1, Pallas kernels, late_rows(): pl.pallas_call(late_rows_kernel, grid=(2 * each,), in_specs=[SMEM_SPEC, p...  5.65 us
  transfers between devices with their start and end apart: 39, of which 15 were waited for; matrix products, arithmetic and copies ran while one was open for 12% of the time, Pallas kernels for 12%

profile of v4, /device:TPU:0, one launch (start us, length us, event | category | flops | bytes accessed | tf_op | source)
XLA Modules:
  0.0 197.1 jit_solution(13943473602417769062)
XLA Ops:
  0.6 4.1 %collective-permute-start = (bf16[128,768]{1,0:T(8,128)(2,1)}, bf16[128,768]{1,0:T(8,128)(2,1)S(1)}, u32[]{:S(2)}, u32[]{:S(2)}) collective-permute-start(bf16[128,768]{1,0:T(8,128)(2,1)} %bitcast.9), channel_id=1, source_target_pairs={{0,8},{1,3},{2,10},{3,1},{4,12},{5,7},{6,14},{7,5},{8,0},{9,11},{1... | collective-permute-start | bytes 589832 | tf_op jit(solution)/shard_map/ppermute | solution.py:42
  12.7 10.2 %collective-permute-done.1 = bf16[256,768]{1,0:T(8,128)(2,1)S(1)} collective-permute-done((bf16[256,768]{1,0:T(8,128)(2,1)S(1)}, bf16[256,768]{1,0:T(8,128)(2,1)S(1)}, u32[]{:S(2)}, u32[]{:S(2)}) %collective-permute-start.1) | collective-permute-done | bytes 393248 | tf_op jit(solution)/shard_map/ppermute | solution.py:42
  28.1 4.5 %project.2 = (bf16[512,1536]{1,0:T(8,128)(2,1)S(1)}, bf16[512,768]{1,0:T(8,128)(2,1)S(1)}, bf16[128,768]{1,0:T(8,128)(2,1)S(1)}, bf16[768,2304]{1,0:T(8,128)(2,1)S(1)}) custom-call(s32[1]{0:T(128)} %bitcast.core, bf16[512,768]{1,0:T(8,128)(2,1)S(1)} %pad_maximum_fusion.5.tokens, bf16[384,2304]{1,0:T(8,128)(2,1)S(1)} %copy-done.1, ...), custom_call_target="tpu_custom_call" | custom-call | flops 1207959552 | bytes 3145728 | tf_op jit(solution)/shard_map/project/pallas_call | solution.py:262
  32.7 3.4 %attend_first.1 = (f32[128,768]{1,0:T(8,128)S(1)}, f32[128,128]{1,0:T(8,128)S(1)}, f32[128,128]{1,0:T(8,128)S(1)}) custom-call(bf16[128,768]{1,0:T(8,128)(2,1)S(1)} %get-tuple-element.46.queries, bf16[512,1536]{1,0:T(8,128)(2,1)S(1)} %get-tuple-element.49.keys.values.keys_a.values_a, bf16[512,1536]{1,0:T(8,128)(2,1)S(1)} %get-tuple-element.49.keys.values.keys_a.values_a), custom_call_target="tpu_custom_call" | custom-call | flops 402653184 | bytes 2359296 | tf_op jit(solution)/shard_map/attend_first/pallas_call | solution.py:369
  38.5 4.6 %attend_last.1 = (f32[128,768]{1,0:T(8,128)S(1)}, f32[128,128]{1,0:T(8,128)S(1)}) custom-call(bf16[128,768]{1,0:T(8,128)(2,1)S(1)} %get-tuple-element.46.queries, bf16[512,1536]{1,0:T(8,128)(2,1)S(1)} %get-tuple-element.48.keys.values.keys_b.values_b, bf16[512,1536]{1,0:T(8,128)(2,1)S(1)} %get-tuple-element.48.keys.values.keys_b.values_b, ...), custom_call_target="tpu_custom_call" | custom-call | flops 402653184 | bytes 2359296 | tf_op jit(solution)/shard_map/attend_last/pallas_call | solution.py:379
  43.1 4.6 %middle.1 = (bf16[128,768]{1,0:T(8,128)(2,1)}, bf16[128,1408]{1,0:T(8,128)(2,1)S(1)}, bf16[128,1408]{1,0:T(8,128)(2,1)S(1)}, bf16[128,3072]{1,0:T(8,128)(2,1)S(1...) custom-call(s32[1]{0:T(128)} %bitcast.core, bf16[128,768]{1,0:T(8,128)(2,1)S(1)} %bitcast.12, ...), custom_call_target="tpu_custom_call" | custom-call | flops 3321888768 | bytes 25165824 | tf_op jit(solution)/shard_map/middle/pallas_call | solution.py:454
  48.4 7.4 %attend_back.1 = (bf16[128,768]{1,0:T(8,128)(2,1)S(1)}, bf16[1024,768]{1,0:T(8,128)(2,1)S(1)}, bf16[1024,768]{1,0:T(8,128)(2,1)S(1)}) custom-call(bf16[128,768]{1,0:T(8,128)(2,1)S(1)} %get-tuple-element.46.queries, bf16[512,1536]{1,0:T(8,128)(2,1)S(1)} %get-tuple-element.49.keys.values.keys_a.values_a, ...), custom_call_target="tpu_custom_call" | custom-call | flops 2013265920 | bytes 7864320 | tf_op jit(solution)/shard_map/attend_back/pallas_call | solution.py:599
  59.3 5.7 %late_rows.1 = (bf16[1152,768]{1,0:T(8,128)(2,1)S(1)}, bf16[1152,768]{1,0:T(8,128)(2,1)}) custom-call(s32[1]{0:T(128)} %bitcast.core, bf16[512,768]{1,0:T(8,128)(2,1)S(1)} %get-tuple-element.68.low_a, bf16[512,768]{1,0:T(8,128)(2,1)S(1)} %get-tuple-element.69.low_b, bf16[128,768]{1,0:T(8,128)(2,1)S(1)} %get-tuple-element.77.grad_q, ...), custom_call_target="tpu_custom_call" | custom-call | flops 1207959552 | bytes 3145728 | tf_op jit(solution)/shard_map/late_rows/pallas_call | solution.py:659
  72.4 2.4 %add_convert_fusion = bf16[576,768]{1,0:T(8,128)(2,1)} fusion(bf16[1152,768]{1,0:T(8,128)(2,1)} %collective-permute-done.11, s32[]{:T(128)S(6)} %select_n.299, bf16[1152,768]{1,0:T(8,128)(2,1)S(1)} %copy-done.5), kind=kLoop, calls=%fused_computation.2 | loop fusion | flops 1769472 | bytes 2654212 | tf_op jit(solution)/shard_map/convert_element_type | solution.py:117
  79.6 3.9 %first_rows.1 = bf16[1024,768]{1,0:T(8,128)(2,1)S(1)} custom-call(bf16[128,768]{1,0:T(8,128)(2,1)S(1)} %copy-done.20, bf16[1024,768]{1,0:T(8,128)(2,1)S(1)} %copy-done.11, bf16[1024,768]{1,0:T(8,128)(2,1)S(1)} %copy-done.13, bf16[768,2304]{1,0:T(8,128)(2,1)S(1)} %copy-done.3), custom_call_target="tpu_custom_call" | custom-call | flops 2415919104 | bytes 6291456 | tf_op jit(solution)/shard_map/first_rows/pallas_call | solution.py:699
  86.3 12.0 %collective-permute-done.23 = bf16[512,768]{1,0:T(8,128)(2,1)} collective-permute-done((bf16[512,768]{1,0:T(8,128)(2,1)}, bf16[512,768]{1,0:T(8,128)(2,1)}, u32[]{:S(2)}, u32[]{:S(2)}) %collective-permute-start.23) | collective-permute-done | bytes 786464 | tf_op jit(solution)/shard_map/ppermute | solution.py:42
  98.3 2.4 %add_convert_fusion.6 = (bf16[256,768]{1,0:T(8,128)(2,1)}, bf16[256,768]{1,0:T(8,128)(2,1)}) fusion(bf16[512,768]{1,0:T(8,128)(2,1)} %collective-permute-done.23, s32[]{:T(128)S(6)} %select_n.323, bf16[1024,768]{1,0:T(8,128)(2,1)} %copy-done.16, s32[]{:T(128)S(6)} %select_n.322, s32[]{:T(128)S(6)} %select_n.326, s32[]{:T(128)S(6)} %select_n.325), kind=kLoop, calls=%fused_computation.17 | loop fusion | flops 1572864 | bytes 2359312 | tf_op jit(solution)/shard_map/convert_element_type | solution.py:117
  112.5 3.6 %collective-permute-done.16 = bf16[288,768]{1,0:T(8,128)(2,1)S(1)} collective-permute-done((bf16[288,768]{1,0:T(8,128)(2,1)S(1)}, bf16[288,768]{1,0:T(8,128)(2,1)S(1)}, u32[]{:S(2)}, u32[]{:S(2)}) %collective-permute-start.16) | collective-permute-done | bytes 442400 | tf_op jit(solution)/shard_map/ppermute | solution.py:42
  117.4 3.9 %collective-permute-start.26 = (bf16[64,768]{1,0:T(8,128)(2,1)S(1)}, bf16[64,768]{1,0:T(8,128)(2,1)S(1)}, u32[]{:S(2)}, u32[]{:S(2)}) collective-permute-start(bf16[64,768]{1,0:T(8,128)(2,1)S(1)} %add_convert_fusion.24), channel_id=1, source_target_pairs={{0,8},{1,5},{2,10},{3,7},{4,12},{5,1},{6,14},{7,3},{8,0},{9,13},{1... | collective-permute-start | bytes 294920 | tf_op jit(solution)/shard_map/ppermute | solution.py:42
  122.4 6.9 %collective-permute-done.26 = bf16[64,768]{1,0:T(8,128)(2,1)S(1)} collective-permute-done((bf16[64,768]{1,0:T(8,128)(2,1)S(1)}, bf16[64,768]{1,0:T(8,128)(2,1)S(1)}, u32[]{:S(2)}, u32[]{:S(2)}) %collective-permute-start.26) | collective-permute-done | bytes 98336 | tf_op jit(solution)/shard_map/ppermute | solution.py:42
  129.4 3.0 %collective-permute-start.18 = (bf16[72,768]{1,0:T(8,128)(2,1)S(1)}, bf16[72,768]{1,0:T(8,128)(2,1)S(1)}, u32[]{:S(2)}, u32[]{:S(2)}) collective-permute-start(bf16[72,768]{1,0:T(8,128)(2,1)S(1)} %add_convert_fusion.21), channel_id=1, source_target_pairs={{0,8},{1,5},{2,10},{3,7},{4,12},{5,1},{6,14},{7,3},{8,0},{9,13},{1... | collective-permute-start | bytes 331784 | tf_op jit(solution)/shard_map/ppermute | solution.py:42
  132.5 5.9 %collective-permute-done.27 = bf16[64,768]{1,0:T(8,128)(2,1)S(1)} collective-permute-done((bf16[64,768]{1,0:T(8,128)(2,1)S(1)}, bf16[64,768]{1,0:T(8,128)(2,1)S(1)}, u32[]{:S(2)}, u32[]{:S(2)}) %collective-permute-start.27) | collective-permute-done | bytes 98336 | tf_op jit(solution)/shard_map/ppermute | solution.py:42
  143.9 3.2 %collective-permute-done.19 = bf16[72,768]{1,0:T(8,128)(2,1)S(1)} collective-permute-done((bf16[72,768]{1,0:T(8,128)(2,1)S(1)}, bf16[72,768]{1,0:T(8,128)(2,1)S(1)}, u32[]{:S(2)}, u32[]{:S(2)}) %collective-permute-start.19) | collective-permute-done | bytes 110624 | tf_op jit(solution)/shard_map/ppermute | solution.py:42
  150.3 4.1 %collective-permute-done.20 = bf16[144,768]{1,0:T(8,128)(2,1)S(1)} collective-permute-done((bf16[144,768]{1,0:T(8,128)(2,1)S(1)}, bf16[144,768]{1,0:T(8,128)(2,1)S(1)}, u32[]{:S(2)}, u32[]{:S(2)}) %collective-permute-start.20) | collective-permute-done | bytes 221216 | tf_op jit(solution)/shard_map/ppermute | solution.py:42
  155.0 2.5 %collective-permute-done.36 = bf16[144,768]{1,0:T(8,128)(2,1)S(1)} collective-permute-done((bf16[144,768]{1,0:T(8,128)(2,1)S(1)}, bf16[144,768]{1,0:T(8,128)(2,1)S(1)}, u32[]{:S(2)}, u32[]{:S(2)}) %collective-permute-start.36) | collective-permute-done | bytes 221216 | tf_op jit(solution)/shard_map/ppermute | solution.py:42
  159.0 8.5 %collective-permute-done.21 = bf16[288,768]{1,0:T(8,128)(2,1)S(1)} collective-permute-done((bf16[288,768]{1,0:T(8,128)(2,1)S(1)}, bf16[288,768]{1,0:T(8,128)(2,1)S(1)}, u32[]{:S(2)}, u32[]{:S(2)}) %collective-permute-start.21) | collective-permute-done | bytes 442400 | tf_op jit(solution)/shard_map/ppermute | solution.py:42
  170.3 3.1 %collective-permute-start.14 = (bf16[128,768]{1,0:T(8,128)(2,1)S(1)}, bf16[128,768]{1,0:T(8,128)(2,1)S(1)}, u32[]{:S(2)}, u32[]{:S(2)}) collective-permute-start(bf16[128,768]{1,0:T(8,128)(2,1)S(1)} %get-tuple-element.110), channel_id=1, source_target_pairs={{0,8},{1,3},{2,10},{3,1},{4,12},{5,7},{6,14},{7,5},{8,0},{9,11},{1... | collective-permute-start | bytes 589832 | tf_op jit(solution)/shard_map/ppermute | solution.py:42
  173.4 14.3 %collective-permute-done.14.part_b = bf16[128,768]{1,0:T(8,128)(2,1)S(1)} collective-permute-done((bf16[128,768]{1,0:T(8,128)(2,1)S(1)}, bf16[128,768]{1,0:T(8,128)(2,1)S(1)}, u32[]{:S(2)}, u32[]{:S(2)}) %collective-permute-start.14) | collective-permute-done | bytes 196640 | tf_op jit(solution)/shard_map/ppermute | solution.py:42
  194.8 2.4 %unpack.5 = (f32[384,2304]{1,0:T(8,128)}, f32[384]{0:T(512)}) custom-call(s32[1]{0:T(128)} %bitcast.6.bit, bf16[576,768]{1,0:T(8,128)(2,1)S(1)} %pad_maximum_fusion.4.own, bf16[576,768]{1,0:T(8,128)(2,1)S(1)} %collective-permute-done.38.other, bf16[384,2304]{1,0:T(8,128)(2,1)S(1)} %copy-done, bf16[1,384]{1,0:T(2,128)(2,1)S(1)} %stack.10.refs_1_), custom_call_target="tpu_custom_call" | custom-call | bytes 5308416 | tf_op jit(solution)/shard_map/unpack/pallas_call | solution.py:541
  (173 shorter events, 69.5 us)
Async XLA Ops:
  4.7 23.4 %collective-permute-start.2 = (bf16[384,2304]{1,0:T(8,128)(2,1)}, bf16[384,2304]{1,0:T(8,128)(2,1)}, u32[]{:S(2)}, u32[]{:S(2)}) collective-permute-start(bf16[384,2304]{1,0:T(8,128)(2,1)} %refs_0_.2), channel_id=1, source_target_pairs={{0,1},{1,0},{2,3},{3,2},{4,5},{5,4},{6,7},{7,6},{8,9},{9,8},{10,11... | collective-permute-start | bytes 5308424 | tf_op jit(solution)/shard_map/ppermute | solution.py:46
  6.7 17.9 %collective-permute-start.5 = (bf16[384,768]{1,0:T(8,128)(2,1)}, bf16[384,768]{1,0:T(8,128)(2,1)S(1)}, u32[]{:S(2)}, u32[]{:S(2)}) collective-permute-start(bf16[384,768]{1,0:T(8,128)(2,1)} %param.12), channel_id=1, source_target_pairs={{0,1},{1,0},{2,3},{3,2},{4,5},{5,4},{6,7},{7,6},{8,9},{9,8},{10,11... | collective-permute-start | bytes 1769480 | tf_op jit(solution)/shard_map/ppermute | solution.py:46
  6.8 18.3 %collective-permute-start.6 = (bf16[384,2304]{1,0:T(8,128)(2,1)}, bf16[384,2304]{1,0:T(8,128)(2,1)}, u32[]{:S(2)}, u32[]{:S(2)}) collective-permute-start(bf16[384,2304]{1,0:T(8,128)(2,1)} %refs_0_.3), channel_id=1, source_target_pairs={{0,1},{1,0},{2,3},{3,2},{4,5},{5,4},{6,7},{7,6},{8,9},{9,8},{10,11... | collective-permute-start | bytes 5308424 | tf_op jit(solution)/shard_map/ppermute | solution.py:46
  10.9 12.1 %collective-permute-start.1 = (bf16[256,768]{1,0:T(8,128)(2,1)S(1)}, bf16[256,768]{1,0:T(8,128)(2,1)S(1)}, u32[]{:S(2)}, u32[]{:S(2)}) collective-permute-start(bf16[256,768]{1,0:T(8,128)(2,1)S(1)} %pad_maximum_fusion.11), channel_id=1, source_target_pairs={{0,4},{1,9},{2,6},{3,11},{4,0},{5,13},{6,2},{7,15},{8,12},{9,1},{1... | collective-permute-start | bytes 1179656 | tf_op jit(solution)/shard_map/ppermute | solution.py:42
  12.6 12.2 %collective-permute-start.7 = (bf16[576,768]{1,0:T(8,128)(2,1)S(1)}, bf16[576,768]{1,0:T(8,128)(2,1)S(1)}, u32[]{:S(2)}, u32[]{:S(2)}) collective-permute-start(bf16[576,768]{1,0:T(8,128)(2,1)S(1)} %copy-done.23), channel_id=1, source_target_pairs={{0,1},{1,0},{2,3},{3,2},{4,5},{5,4},{6,7},{7,6},{8,9},{9,8},{10,11... | collective-permute-start | bytes 2654216 | tf_op jit(solution)/shard_map/ppermute | solution.py:46
  23.0 13.3 %collective-permute-start.4 = (bf16[512,768]{1,0:T(8,128)(2,1)S(1)}, bf16[512,768]{1,0:T(8,128)(2,1)S(1)}, u32[]{:S(2)}, u32[]{:S(2)}) collective-permute-start(bf16[512,768]{1,0:T(8,128)(2,1)S(1)} %pad_maximum_fusion.5.tokens), channel_id=1, source_target_pairs={{0,2},{1,5},{2,0},{3,7},{4,6},{5,1},{6,4},{7,3},{8,10},{9,13},{10,... | collective-permute-start | bytes 2359304 | tf_op jit(solution)/shard_map/ppermute | solution.py:42
  74.8 23.5 %collective-permute-start.23 = (bf16[512,768]{1,0:T(8,128)(2,1)}, bf16[512,768]{1,0:T(8,128)(2,1)}, u32[]{:S(2)}, u32[]{:S(2)}) collective-permute-start(bf16[512,768]{1,0:T(8,128)(2,1)} %constant_dynamic-slice_fusion.1), channel_id=1, source_target_pairs={{0,4},{1,9},{2,6},{3,11},{4,0},{5,13},{6,2},{7,15},{8,12},{9,1},{1... | collective-permute-start | bytes 2359304 | tf_op jit(solution)/shard_map/ppermute | solution.py:42
  74.8 27.4 %collective-permute-start.15 = (bf16[576,768]{1,0:T(8,128)(2,1)}, bf16[576,768]{1,0:T(8,128)(2,1)}, u32[]{:S(2)}, u32[]{:S(2)}) collective-permute-start(bf16[576,768]{1,0:T(8,128)(2,1)} %add_convert_fusion), channel_id=1, source_target_pairs={{0,16},{1,3},{2,18},{3,1},{4,20},{5,7},{6,22},{7,5},{8,24},{9,11},... | collective-permute-start | bytes 2654216 | tf_op jit(solution)/shard_map/ppermute | solution.py:42
  76.2 28.2 %collective-permute-start.31 = (bf16[576,768]{1,0:T(8,128)(2,1)}, bf16[576,768]{1,0:T(8,128)(2,1)}, u32[]{:S(2)}, u32[]{:S(2)}) collective-permute-start(bf16[576,768]{1,0:T(8,128)(2,1)} %constant_dynamic-slice_fusion), channel_id=1, source_target_pairs={{0,16},{1,3},{2,18},{3,1},{4,20},{5,7},{6,22},{7,5},{8,24},{9,11},... | collective-permute-start | bytes 2654216 | tf_op jit(solution)/shard_map/ppermute | solution.py:42
  85.6 24.8 %collective-permute-start.12 = (bf16[512,768]{1,0:T(8,128)(2,1)}, bf16[512,768]{1,0:T(8,128)(2,1)}, u32[]{:S(2)}, u32[]{:S(2)}) collective-permute-start(bf16[512,768]{1,0:T(8,128)(2,1)} %slice.70), channel_id=1, source_target_pairs={{0,2},{1,5},{2,0},{3,7},{4,6},{5,1},{6,4},{7,3},{8,10},{9,13},{10,... | collective-permute-start | bytes 2359304 | tf_op jit(solution)/shard_map/ppermute | solution.py:42
  104.4 11.7 %collective-permute-start.16 = (bf16[288,768]{1,0:T(8,128)(2,1)S(1)}, bf16[288,768]{1,0:T(8,128)(2,1)S(1)}, u32[]{:S(2)}, u32[]{:S(2)}) collective-permute-start(bf16[288,768]{1,0:T(8,128)(2,1)S(1)} %get-tuple-element.85), channel_id=1, source_target_pairs={{0,4},{1,9},{2,6},{3,11},{4,0},{5,13},{6,2},{7,15},{8,12},{9,1},{1... | collective-permute-start | bytes 1327112 | tf_op jit(solution)/shard_map/ppermute | solution.py:42
  106.0 15.3 %collective-permute-start.32 = (bf16[288,768]{1,0:T(8,128)(2,1)S(1)}, bf16[288,768]{1,0:T(8,128)(2,1)S(1)}, u32[]{:S(2)}, u32[]{:S(2)}) collective-permute-start(bf16[288,768]{1,0:T(8,128)(2,1)S(1)} %get-tuple-element.89), channel_id=1, source_target_pairs={{0,2},{1,17},{2,0},{3,19},{4,6},{5,21},{6,4},{7,23},{8,10},{9,25},... | collective-permute-start | bytes 1327112 | tf_op jit(solution)/shard_map/ppermute | solution.py:42
  111.8 58.4 %collective-permute-start.13 = (bf16[256,768]{1,0:T(8,128)(2,1)S(1)}, bf16[256,768]{1,0:T(8,128)(2,1)S(1)}, u32[]{:S(2)}, u32[]{:S(2)}) collective-permute-start(bf16[256,768]{1,0:T(8,128)(2,1)S(1)} %get-tuple-element.93), channel_id=1, source_target_pairs={{0,4},{1,9},{2,6},{3,11},{4,0},{5,13},{6,2},{7,15},{8,12},{9,1},{1... | collective-permute-start | bytes 1179656 | tf_op jit(solution)/shard_map/ppermute | solution.py:42
  116.2 13.2 %collective-permute-start.17 = (bf16[144,768]{1,0:T(8,128)(2,1)S(1)}, bf16[144,768]{1,0:T(8,128)(2,1)S(1)}, u32[]{:S(2)}, u32[]{:S(2)}) collective-permute-start(bf16[144,768]{1,0:T(8,128)(2,1)S(1)} %get-tuple-element.105), channel_id=1, source_target_pairs={{0,2},{1,17},{2,0},{3,19},{4,6},{5,21},{6,4},{7,23},{8,10},{9,25},... | collective-permute-start | bytes 663560 | tf_op jit(solution)/shard_map/ppermute | solution.py:42
  117.4 11.8 %collective-permute-start.26 = (bf16[64,768]{1,0:T(8,128)(2,1)S(1)}, bf16[64,768]{1,0:T(8,128)(2,1)S(1)}, u32[]{:S(2)}, u32[]{:S(2)}) collective-permute-start(bf16[64,768]{1,0:T(8,128)(2,1)S(1)} %add_convert_fusion.24), channel_id=1, source_target_pairs={{0,8},{1,5},{2,10},{3,7},{4,12},{5,1},{6,14},{7,3},{8,0},{9,13},{1... | collective-permute-start | bytes 294920 | tf_op jit(solution)/shard_map/ppermute | solution.py:42
  121.4 11.0 %collective-permute-start.33 = (bf16[144,768]{1,0:T(8,128)(2,1)S(1)}, bf16[144,768]{1,0:T(8,128)(2,1)S(1)}, u32[]{:S(2)}, u32[]{:S(2)}) collective-permute-start(bf16[144,768]{1,0:T(8,128)(2,1)S(1)} %get-tuple-element.101), channel_id=1, source_target_pairs={{0,4},{1,9},{2,6},{3,11},{4,0},{5,13},{6,2},{7,15},{8,12},{9,1},{1... | collective-permute-start | bytes 663560 | tf_op jit(solution)/shard_map/ppermute | solution.py:42
  129.4 11.4 %collective-permute-start.18 = (bf16[72,768]{1,0:T(8,128)(2,1)S(1)}, bf16[72,768]{1,0:T(8,128)(2,1)S(1)}, u32[]{:S(2)}, u32[]{:S(2)}) collective-permute-start(bf16[72,768]{1,0:T(8,128)(2,1)S(1)} %add_convert_fusion.21), channel_id=1, source_target_pairs={{0,8},{1,5},{2,10},{3,7},{4,12},{5,1},{6,14},{7,3},{8,0},{9,13},{1... | collective-permute-start | bytes 331784 | tf_op jit(solution)/shard_map/ppermute | solution.py:42
  148.3 10.6 %collective-permute-start.29 = (bf16[256,768]{1,0:T(8,128)(2,1)S(1)}, bf16[256,768]{1,0:T(8,128)(2,1)S(1)}, u32[]{:S(2)}, u32[]{:S(2)}) collective-permute-start(bf16[256,768]{1,0:T(8,128)(2,1)S(1)} %pad_maximum_fusion.12), channel_id=1, source_target_pairs={{0,16},{1,3},{2,18},{3,1},{4,20},{5,7},{6,22},{7,5},{8,24},{9,11},... | collective-permute-start | bytes 1179656 | tf_op jit(solution)/shard_map/ppermute | solution.py:42
  154.4 13.0 %collective-permute-start.21 = (bf16[288,768]{1,0:T(8,128)(2,1)S(1)}, bf16[288,768]{1,0:T(8,128)(2,1)S(1)}, u32[]{:S(2)}, u32[]{:S(2)}) collective-permute-start(bf16[288,768]{1,0:T(8,128)(2,1)S(1)} %pad_maximum_fusion.9), channel_id=1, source_target_pairs={{0,4},{1,9},{2,6},{3,11},{4,0},{5,13},{6,2},{7,15},{8,12},{9,1},{1... | collective-permute-start | bytes 1327112 | tf_op jit(solution)/shard_map/ppermute | solution.py:42
  157.6 11.5 %collective-permute-start.37 = (bf16[288,768]{1,0:T(8,128)(2,1)S(1)}, bf16[288,768]{1,0:T(8,128)(2,1)S(1)}, u32[]{:S(2)}, u32[]{:S(2)}) collective-permute-start(bf16[288,768]{1,0:T(8,128)(2,1)S(1)} %pad_maximum_fusion.10), channel_id=1, source_target_pairs={{0,2},{1,17},{2,0},{3,19},{4,6},{5,21},{6,4},{7,23},{8,10},{9,25},... | collective-permute-start | bytes 1327112 | tf_op jit(solution)/shard_map/ppermute | solution.py:42
  167.7 24.8 %collective-permute-start.22 = (bf16[576,768]{1,0:T(8,128)(2,1)S(1)}, bf16[576,768]{1,0:T(8,128)(2,1)S(1)}, u32[]{:S(2)}, u32[]{:S(2)}) collective-permute-start(bf16[576,768]{1,0:T(8,128)(2,1)S(1)} %pad_maximum_fusion.3.own), channel_id=1, source_target_pairs={{0,16},{1,3},{2,18},{3,1},{4,20},{5,7},{6,22},{7,5},{8,24},{9,11},... | collective-permute-start | bytes 2654216 | tf_op jit(solution)/shard_map/ppermute | solution.py:42
  169.3 25.4 %collective-permute-start.38 = (bf16[576,768]{1,0:T(8,128)(2,1)S(1)}, bf16[576,768]{1,0:T(8,128)(2,1)S(1)}, u32[]{:S(2)}, u32[]{:S(2)}) collective-permute-start(bf16[576,768]{1,0:T(8,128)(2,1)S(1)} %pad_maximum_fusion.4.own), channel_id=1, source_target_pairs={{0,16},{1,3},{2,18},{3,1},{4,20},{5,7},{6,22},{7,5},{8,24},{9,11},... | collective-permute-start | bytes 2654216 | tf_op jit(solution)/shard_map/ppermute | solution.py:42
  170.1 20.5 %collective-permute-start.30 = (bf16[512,768]{1,0:T(8,128)(2,1)S(1)}, bf16[512,768]{1,0:T(8,128)(2,1)S(1)}, u32[]{:S(2)}, u32[]{:S(2)}) collective-permute-start(bf16[512,768]{1,0:T(8,128)(2,1)S(1)} %pad_maximum_fusion.6.own), channel_id=1, source_target_pairs={{0,4},{1,9},{2,6},{3,11},{4,0},{5,13},{6,2},{7,15},{8,12},{9,1},{1... | collective-permute-start | bytes 2359304 | tf_op jit(solution)/shard_map/ppermute | solution.py:42
  170.3 17.4 %collective-permute-start.14 = (bf16[128,768]{1,0:T(8,128)(2,1)S(1)}, bf16[128,768]{1,0:T(8,128)(2,1)S(1)}, u32[]{:S(2)}, u32[]{:S(2)}) collective-permute-start(bf16[128,768]{1,0:T(8,128)(2,1)S(1)} %get-tuple-element.110), channel_id=1, source_target_pairs={{0,8},{1,3},{2,10},{3,1},{4,12},{5,7},{6,14},{7,5},{8,0},{9,11},{1... | collective-permute-start | bytes 589832 | tf_op jit(solution)/shard_map/ppermute | solution.py:42
  (40 other events, 248.2 us)

commit v5 on v4

--- a/solution.py
+++ b/solution.py
@@ -15,9 +15,9 @@
 NORMED_AT = 640
 ATTENDED_AT = 1024
 HALVES_WIDTH = 1408
-MLP_ORDERS = ("axyb", "byxa")
-IN_ORDERS = ("xyab", "yxba")
-LATE_ORDERS = ("xayb", "ybxa")
+MLP_ORDERS = ("xyab", "yxba")
+IN_ORDERS = ("yxab", "xyab")
+LATE_ORDERS = ("ayxb", "bxya")
 MIB = 1 << 20
 BF16 = jnp.bfloat16
 F32 = jnp.float32

time: 199 us -> 196 us (0.985)
  waiting for transfers between devices: 77.4 us -> 63.9 us
  starting transfers between devices: 38 us -> 50.6 us
    ppermute x30, waiting for transfers between devices: 77.4 us -> 63.9 us  [flip(): return lax.ppermute(block, ('seq', 'ctx', 'wsh'), route)]
    ppermute x30, starting transfers between devices: 35.8 us -> 48.4 us  [flip(): return lax.ppermute(block, ('seq', 'ctx', 'wsh'), route)]
  transfers between devices with their start and end apart: 39 -> 39, of which waited for: 15 -> 16; matrix products, arithmetic and copies ran while one was open for 12% -> 12% of each run, Pallas kernels for 12% -> 12%
where the time goes in v5:
time: 196 us
  waiting for transfers between devices  63.9 us (33%)
  starting transfers between devices  50.6 us (26%)
  Pallas kernels  44.9 us (23%)
  other arithmetic  18.2 us (9%)
  local copies, waits for them, and re-layouts  17.1 us (9%)
    ppermute x30, waiting for transfers between devices, flip(): return lax.ppermute(block, ('seq', 'ctx', 'wsh'), route)  63.9 us
    ppermute x30, starting transfers between devices, flip(): return lax.ppermute(block, ('seq', 'ctx', 'wsh'), route)  48.4 us
    unnamed x50, local copies, waits for them, and re-layouts  10.2 us
    convert_element_type x13, other arithmetic, summed(): return sum(cut[1:], cut[0]).astype(BF16)  9.74 us
    pallas_call x1, Pallas kernels, attend_back(): pl.pallas_call(attend_back_kernel, grid=(pairs,), in_specs=[queries, keys...  7.42 us
    pallas_call x2, Pallas kernels, project(): pl.pallas_call(project_kernel, grid=(rows // step,), in_specs=[SMEM_SPEC,...  6.68 us
    pallas_call x3, Pallas kernels, unpack(): pl.pallas_call(partial(unpack_kernel, places, bool(gained)), in_specs=[SM...  6.51 us
    pallas_call x1, Pallas kernels, late_rows(): pl.pallas_call(late_rows_kernel, grid=(2 * each,), in_specs=[SMEM_SPEC, p...  5.65 us
  transfers between devices with their start and end apart: 39, of which 16 were waited for; matrix products, arithmetic and copies ran while one was open for 12% of the time, Pallas kernels for 12%

profile of v5, /device:TPU:0, one launch (start us, length us, event | category | flops | bytes accessed | tf_op | source)
XLA Modules:
  0.0 196.0 jit_solution(420301808260394456)
XLA Ops:
  0.6 4.1 %collective-permute-start = (bf16[128,768]{1,0:T(8,128)(2,1)}, bf16[128,768]{1,0:T(8,128)(2,1)S(1)}, u32[]{:S(2)}, u32[]{:S(2)}) collective-permute-start(bf16[128,768]{1,0:T(8,128)(2,1)} %bitcast.10), channel_id=1, source_target_pairs={{0,8},{1,3},{2,10},{3,1},{4,12},{5,7},{6,14},{7,5},{8,0},{9,11},{1... | collective-permute-start | bytes 589832 | tf_op jit(solution)/shard_map/ppermute | solution.py:42
  12.7 10.2 %collective-permute-done.1 = bf16[256,768]{1,0:T(8,128)(2,1)S(1)} collective-permute-done((bf16[256,768]{1,0:T(8,128)(2,1)S(1)}, bf16[256,768]{1,0:T(8,128)(2,1)S(1)}, u32[]{:S(2)}, u32[]{:S(2)}) %collective-permute-start.1) | collective-permute-done | bytes 393248 | tf_op jit(solution)/shard_map/ppermute | solution.py:42
  28.1 4.5 %project.2 = (bf16[512,1536]{1,0:T(8,128)(2,1)S(1)}, bf16[512,768]{1,0:T(8,128)(2,1)S(1)}, bf16[128,768]{1,0:T(8,128)(2,1)S(1)}, bf16[768,2304]{1,0:T(8,128)(2,1)S(1)}) custom-call(s32[1]{0:T(128)} %bitcast.core, bf16[512,768]{1,0:T(8,128)(2,1)S(1)} %pad_maximum_fusion.5.tokens, bf16[384,2304]{1,0:T(8,128)(2,1)S(1)} %copy-done.1, ...), custom_call_target="tpu_custom_call" | custom-call | flops 1207959552 | bytes 3145728 | tf_op jit(solution)/shard_map/project/pallas_call | solution.py:262
  32.7 3.4 %attend_first.1 = (f32[128,768]{1,0:T(8,128)S(1)}, f32[128,128]{1,0:T(8,128)S(1)}, f32[128,128]{1,0:T(8,128)S(1)}) custom-call(bf16[128,768]{1,0:T(8,128)(2,1)S(1)} %get-tuple-element.46.queries, bf16[512,1536]{1,0:T(8,128)(2,1)S(1)} %get-tuple-element.49.keys.values.keys_a.values_a, bf16[512,1536]{1,0:T(8,128)(2,1)S(1)} %get-tuple-element.49.keys.values.keys_a.values_a), custom_call_target="tpu_custom_call" | custom-call | flops 402653184 | bytes 2359296 | tf_op jit(solution)/shard_map/attend_first/pallas_call | solution.py:369
  38.5 4.6 %attend_last.1 = (f32[128,768]{1,0:T(8,128)S(1)}, f32[128,128]{1,0:T(8,128)S(1)}) custom-call(bf16[128,768]{1,0:T(8,128)(2,1)S(1)} %get-tuple-element.46.queries, bf16[512,1536]{1,0:T(8,128)(2,1)S(1)} %get-tuple-element.48.keys.values.keys_b.values_b, bf16[512,1536]{1,0:T(8,128)(2,1)S(1)} %get-tuple-element.48.keys.values.keys_b.values_b, ...), custom_call_target="tpu_custom_call" | custom-call | flops 402653184 | bytes 2359296 | tf_op jit(solution)/shard_map/attend_last/pallas_call | solution.py:379
  43.1 4.6 %middle.1 = (bf16[128,768]{1,0:T(8,128)(2,1)}, bf16[128,1408]{1,0:T(8,128)(2,1)S(1)}, bf16[128,1408]{1,0:T(8,128)(2,1)S(1)}, bf16[128,3072]{1,0:T(8,128)(2,1)S(1...) custom-call(s32[1]{0:T(128)} %bitcast.core, bf16[128,768]{1,0:T(8,128)(2,1)S(1)} %bitcast.13, ...), custom_call_target="tpu_custom_call" | custom-call | flops 3321888768 | bytes 25165824 | tf_op jit(solution)/shard_map/middle/pallas_call | solution.py:454
  48.4 7.4 %attend_back.1 = (bf16[128,768]{1,0:T(8,128)(2,1)S(1)}, bf16[1024,768]{1,0:T(8,128)(2,1)S(1)}, bf16[1024,768]{1,0:T(8,128)(2,1)S(1)}) custom-call(bf16[128,768]{1,0:T(8,128)(2,1)S(1)} %get-tuple-element.46.queries, bf16[512,1536]{1,0:T(8,128)(2,1)S(1)} %get-tuple-element.49.keys.values.keys_a.values_a, ...), custom_call_target="tpu_custom_call" | custom-call | flops 2013265920 | bytes 7864320 | tf_op jit(solution)/shard_map/attend_back/pallas_call | solution.py:599
  59.3 5.7 %late_rows.1 = (bf16[1152,768]{1,0:T(8,128)(2,1)S(1)}, bf16[1152,768]{1,0:T(8,128)(2,1)}) custom-call(s32[1]{0:T(128)} %bitcast.core, bf16[512,768]{1,0:T(8,128)(2,1)S(1)} %get-tuple-element.68.low_a, bf16[512,768]{1,0:T(8,128)(2,1)S(1)} %get-tuple-element.69.low_b, bf16[128,768]{1,0:T(8,128)(2,1)S(1)} %get-tuple-element.77.grad_q, ...), custom_call_target="tpu_custom_call" | custom-call | flops 1207959552 | bytes 3145728 | tf_op jit(solution)/shard_map/late_rows/pallas_call | solution.py:659
  79.8 3.9 %first_rows.1 = bf16[1024,768]{1,0:T(8,128)(2,1)S(1)} custom-call(bf16[128,768]{1,0:T(8,128)(2,1)S(1)} %copy-done.20, bf16[1024,768]{1,0:T(8,128)(2,1)S(1)} %copy-done.11, bf16[1024,768]{1,0:T(8,128)(2,1)S(1)} %copy-done.13, bf16[768,2304]{1,0:T(8,128)(2,1)S(1)} %copy-done.3), custom_call_target="tpu_custom_call" | custom-call | flops 2415919104 | bytes 6291456 | tf_op jit(solution)/shard_map/first_rows/pallas_call | solution.py:699
  87.1 7.8 %collective-permute-done.23 = bf16[512,768]{1,0:T(8,128)(2,1)} collective-permute-done((bf16[512,768]{1,0:T(8,128)(2,1)}, bf16[512,768]{1,0:T(8,128)(2,1)}, u32[]{:S(2)}, u32[]{:S(2)}) %collective-permute-start.23) | collective-permute-done | bytes 786464 | tf_op jit(solution)/shard_map/ppermute | solution.py:42
  97.4 4.3 %collective-permute-done.15 = bf16[576,768]{1,0:T(8,128)(2,1)} collective-permute-done((bf16[576,768]{1,0:T(8,128)(2,1)}, bf16[576,768]{1,0:T(8,128)(2,1)}, u32[]{:S(2)}, u32[]{:S(2)}) %collective-permute-start.15) | collective-permute-done | bytes 884768 | tf_op jit(solution)/shard_map/ppermute | solution.py:42
  107.7 3.9 %collective-permute-done.24 = bf16[256,768]{1,0:T(8,128)(2,1)} collective-permute-done((bf16[256,768]{1,0:T(8,128)(2,1)}, bf16[256,768]{1,0:T(8,128)(2,1)}, u32[]{:S(2)}, u32[]{:S(2)}) %collective-permute-start.24) | collective-permute-done | bytes 393248 | tf_op jit(solution)/shard_map/ppermute | solution.py:42
  116.1 4.0 %collective-permute-done.16 = bf16[288,768]{1,0:T(8,128)(2,1)S(1)} collective-permute-done((bf16[288,768]{1,0:T(8,128)(2,1)S(1)}, bf16[288,768]{1,0:T(8,128)(2,1)S(1)}, u32[]{:S(2)}, u32[]{:S(2)}) %collective-permute-start.16) | collective-permute-done | bytes 442400 | tf_op jit(solution)/shard_map/ppermute | solution.py:42
  125.3 2.5 %collective-permute-start.33 = (bf16[144,768]{1,0:T(8,128)(2,1)S(1)}, bf16[144,768]{1,0:T(8,128)(2,1)S(1)}, u32[]{:S(2)}, u32[]{:S(2)}) collective-permute-start(bf16[144,768]{1,0:T(8,128)(2,1)S(1)} %get-tuple-element.101), channel_id=1, source_target_pairs={{0,4},{1,5},{2,6},{3,7},{4,0},{5,1},{6,2},{7,3},{8,12},{9,13},{10,... | collective-permute-start | bytes 663560 | tf_op jit(solution)/shard_map/ppermute | solution.py:42
  128.7 3.5 %collective-permute-start.27 = (bf16[64,768]{1,0:T(8,128)(2,1)S(1)}, bf16[64,768]{1,0:T(8,128)(2,1)S(1)}, u32[]{:S(2)}, u32[]{:S(2)}) collective-permute-start(bf16[64,768]{1,0:T(8,128)(2,1)S(1)} %add_convert_fusion.23), channel_id=1, source_target_pairs={{0,8},{1,5},{2,10},{3,7},{4,12},{5,1},{6,14},{7,3},{8,0},{9,13},{1... | collective-permute-start | bytes 294920 | tf_op jit(solution)/shard_map/ppermute | solution.py:42
  132.3 7.8 %collective-permute-done.33 = bf16[144,768]{1,0:T(8,128)(2,1)S(1)} collective-permute-done((bf16[144,768]{1,0:T(8,128)(2,1)S(1)}, bf16[144,768]{1,0:T(8,128)(2,1)S(1)}, u32[]{:S(2)}, u32[]{:S(2)}) %collective-permute-start.33) | collective-permute-done | bytes 221216 | tf_op jit(solution)/shard_map/ppermute | solution.py:42
  141.8 3.3 %collective-permute-start.19 = (bf16[72,768]{1,0:T(8,128)(2,1)S(1)}, bf16[72,768]{1,0:T(8,128)(2,1)S(1)}, u32[]{:S(2)}, u32[]{:S(2)}) collective-permute-start(bf16[72,768]{1,0:T(8,128)(2,1)S(1)} %add_convert_fusion.20), channel_id=1, source_target_pairs={{0,8},{1,5},{2,10},{3,7},{4,12},{5,1},{6,14},{7,3},{8,0},{9,13},{1... | collective-permute-start | bytes 331784 | tf_op jit(solution)/shard_map/ppermute | solution.py:42
  148.5 4.7 %collective-permute-start.20 = (bf16[144,768]{1,0:T(8,128)(2,1)S(1)}, bf16[144,768]{1,0:T(8,128)(2,1)S(1)}, u32[]{:S(2)}, u32[]{:S(2)}) collective-permute-start(bf16[144,768]{1,0:T(8,128)(2,1)S(1)} %pad_maximum_fusion.13), channel_id=1, source_target_pairs={{0,16},{1,3},{2,18},{3,1},{4,20},{5,7},{6,22},{7,5},{8,24},{9,11},... | collective-permute-start | bytes 663560 | tf_op jit(solution)/shard_map/ppermute | solution.py:42
  153.5 2.5 %collective-permute-start.36 = (bf16[144,768]{1,0:T(8,128)(2,1)S(1)}, bf16[144,768]{1,0:T(8,128)(2,1)S(1)}, u32[]{:S(2)}, u32[]{:S(2)}) collective-permute-start(bf16[144,768]{1,0:T(8,128)(2,1)S(1)} %pad_maximum_fusion.14), channel_id=1, source_target_pairs={{0,4},{1,5},{2,6},{3,7},{4,0},{5,1},{6,2},{7,3},{8,12},{9,13},{10,... | collective-permute-start | bytes 663560 | tf_op jit(solution)/shard_map/ppermute | solution.py:42
  158.2 3.7 %collective-permute-done.36 = bf16[144,768]{1,0:T(8,128)(2,1)S(1)} collective-permute-done((bf16[144,768]{1,0:T(8,128)(2,1)S(1)}, bf16[144,768]{1,0:T(8,128)(2,1)S(1)}, u32[]{:S(2)}, u32[]{:S(2)}) %collective-permute-start.36) | collective-permute-done | bytes 221216 | tf_op jit(solution)/shard_map/ppermute | solution.py:42
  162.0 3.5 %collective-permute-start.37 = (bf16[288,768]{1,0:T(8,128)(2,1)S(1)}, bf16[288,768]{1,0:T(8,128)(2,1)S(1)}, u32[]{:S(2)}, u32[]{:S(2)}) collective-permute-start(bf16[288,768]{1,0:T(8,128)(2,1)S(1)} %pad_maximum_fusion.10), channel_id=1, source_target_pairs={{0,16},{1,3},{2,18},{3,1},{4,20},{5,7},{6,22},{7,5},{8,24},{9,11},... | collective-permute-start | bytes 1327112 | tf_op jit(solution)/shard_map/ppermute | solution.py:42
  168.2 2.6 %collective-permute-start.22 = (bf16[576,768]{1,0:T(8,128)(2,1)S(1)}, bf16[576,768]{1,0:T(8,128)(2,1)S(1)}, u32[]{:S(2)}, u32[]{:S(2)}) collective-permute-start(bf16[576,768]{1,0:T(8,128)(2,1)S(1)} %pad_maximum_fusion.3.own), channel_id=1, source_target_pairs={{0,4},{1,9},{2,6},{3,11},{4,0},{5,13},{6,2},{7,15},{8,12},{9,1},{1... | collective-permute-start | bytes 2654216 | tf_op jit(solution)/shard_map/ppermute | solution.py:42
  170.8 5.7 %collective-permute-done.37 = bf16[288,768]{1,0:T(8,128)(2,1)S(1)} collective-permute-done((bf16[288,768]{1,0:T(8,128)(2,1)S(1)}, bf16[288,768]{1,0:T(8,128)(2,1)S(1)}, u32[]{:S(2)}, u32[]{:S(2)}) %collective-permute-start.37) | collective-permute-done | bytes 442400 | tf_op jit(solution)/shard_map/ppermute | solution.py:42
  180.6 7.2 %collective-permute-done.14.part_b = bf16[128,768]{1,0:T(8,128)(2,1)S(1)} collective-permute-done((bf16[128,768]{1,0:T(8,128)(2,1)S(1)}, bf16[128,768]{1,0:T(8,128)(2,1)S(1)}, u32[]{:S(2)}, u32[]{:S(2)}) %collective-permute-start.14) | collective-permute-done | bytes 196640 | tf_op jit(solution)/shard_map/ppermute | solution.py:42
  (173 shorter events, 79.1 us)
Async XLA Ops:
  4.7 23.4 %collective-permute-start.2 = (bf16[384,2304]{1,0:T(8,128)(2,1)}, bf16[384,2304]{1,0:T(8,128)(2,1)}, u32[]{:S(2)}, u32[]{:S(2)}) collective-permute-start(bf16[384,2304]{1,0:T(8,128)(2,1)} %refs_0_.2), channel_id=1, source_target_pairs={{0,1},{1,0},{2,3},{3,2},{4,5},{5,4},{6,7},{7,6},{8,9},{9,8},{10,11... | collective-permute-start | bytes 5308424 | tf_op jit(solution)/shard_map/ppermute | solution.py:46
  6.7 17.9 %collective-permute-start.5 = (bf16[384,768]{1,0:T(8,128)(2,1)}, bf16[384,768]{1,0:T(8,128)(2,1)S(1)}, u32[]{:S(2)}, u32[]{:S(2)}) collective-permute-start(bf16[384,768]{1,0:T(8,128)(2,1)} %param.12), channel_id=1, source_target_pairs={{0,1},{1,0},{2,3},{3,2},{4,5},{5,4},{6,7},{7,6},{8,9},{9,8},{10,11... | collective-permute-start | bytes 1769480 | tf_op jit(solution)/shard_map/ppermute | solution.py:46
  6.8 18.3 %collective-permute-start.6 = (bf16[384,2304]{1,0:T(8,128)(2,1)}, bf16[384,2304]{1,0:T(8,128)(2,1)}, u32[]{:S(2)}, u32[]{:S(2)}) collective-permute-start(bf16[384,2304]{1,0:T(8,128)(2,1)} %refs_0_.3), channel_id=1, source_target_pairs={{0,1},{1,0},{2,3},{3,2},{4,5},{5,4},{6,7},{7,6},{8,9},{9,8},{10,11... | collective-permute-start | bytes 5308424 | tf_op jit(solution)/shard_map/ppermute | solution.py:46
  10.9 12.1 %collective-permute-start.1 = (bf16[256,768]{1,0:T(8,128)(2,1)S(1)}, bf16[256,768]{1,0:T(8,128)(2,1)S(1)}, u32[]{:S(2)}, u32[]{:S(2)}) collective-permute-start(bf16[256,768]{1,0:T(8,128)(2,1)S(1)} %pad_maximum_fusion.11), channel_id=1, source_target_pairs={{0,4},{1,9},{2,6},{3,11},{4,0},{5,13},{6,2},{7,15},{8,12},{9,1},{1... | collective-permute-start | bytes 1179656 | tf_op jit(solution)/shard_map/ppermute | solution.py:42
  12.6 12.2 %collective-permute-start.7 = (bf16[576,768]{1,0:T(8,128)(2,1)S(1)}, bf16[576,768]{1,0:T(8,128)(2,1)S(1)}, u32[]{:S(2)}, u32[]{:S(2)}) collective-permute-start(bf16[576,768]{1,0:T(8,128)(2,1)S(1)} %copy-done.23), channel_id=1, source_target_pairs={{0,1},{1,0},{2,3},{3,2},{4,5},{5,4},{6,7},{7,6},{8,9},{9,8},{10,11... | collective-permute-start | bytes 2654216 | tf_op jit(solution)/shard_map/ppermute | solution.py:46
  23.0 13.3 %collective-permute-start.4 = (bf16[512,768]{1,0:T(8,128)(2,1)S(1)}, bf16[512,768]{1,0:T(8,128)(2,1)S(1)}, u32[]{:S(2)}, u32[]{:S(2)}) collective-permute-start(bf16[512,768]{1,0:T(8,128)(2,1)S(1)} %pad_maximum_fusion.5.tokens), channel_id=1, source_target_pairs={{0,2},{1,5},{2,0},{3,7},{4,6},{5,1},{6,4},{7,3},{8,10},{9,13},{10,... | collective-permute-start | bytes 2359304 | tf_op jit(solution)/shard_map/ppermute | solution.py:42
  74.8 20.1 %collective-permute-start.23 = (bf16[512,768]{1,0:T(8,128)(2,1)}, bf16[512,768]{1,0:T(8,128)(2,1)}, u32[]{:S(2)}, u32[]{:S(2)}) collective-permute-start(bf16[512,768]{1,0:T(8,128)(2,1)} %constant_dynamic-slice_fusion.1), channel_id=1, source_target_pairs={{0,16},{1,3},{2,18},{3,1},{4,20},{5,7},{6,22},{7,5},{8,24},{9,11},... | collective-permute-start | bytes 2359304 | tf_op jit(solution)/shard_map/ppermute | solution.py:42
  76.2 25.4 %collective-permute-start.15 = (bf16[576,768]{1,0:T(8,128)(2,1)}, bf16[576,768]{1,0:T(8,128)(2,1)}, u32[]{:S(2)}, u32[]{:S(2)}) collective-permute-start(bf16[576,768]{1,0:T(8,128)(2,1)} %add_convert_fusion), channel_id=1, source_target_pairs={{0,4},{1,9},{2,6},{3,11},{4,0},{5,13},{6,2},{7,15},{8,12},{9,1},{1... | collective-permute-start | bytes 2654216 | tf_op jit(solution)/shard_map/ppermute | solution.py:42
  76.2 29.0 %collective-permute-start.31 = (bf16[576,768]{1,0:T(8,128)(2,1)}, bf16[576,768]{1,0:T(8,128)(2,1)}, u32[]{:S(2)}, u32[]{:S(2)}) collective-permute-start(bf16[576,768]{1,0:T(8,128)(2,1)} %constant_dynamic-slice_fusion), channel_id=1, source_target_pairs={{0,2},{1,17},{2,0},{3,19},{4,6},{5,21},{6,4},{7,23},{8,10},{9,25},... | collective-permute-start | bytes 2654216 | tf_op jit(solution)/shard_map/ppermute | solution.py:42
  85.8 27.0 %collective-permute-start.12 = (bf16[512,768]{1,0:T(8,128)(2,1)}, bf16[512,768]{1,0:T(8,128)(2,1)}, u32[]{:S(2)}, u32[]{:S(2)}) collective-permute-start(bf16[512,768]{1,0:T(8,128)(2,1)} %slice.70), channel_id=1, source_target_pairs={{0,2},{1,5},{2,0},{3,7},{4,6},{5,1},{6,4},{7,3},{8,10},{9,13},{10,... | collective-permute-start | bytes 2359304 | tf_op jit(solution)/shard_map/ppermute | solution.py:42
  97.4 14.2 %collective-permute-start.24 = (bf16[256,768]{1,0:T(8,128)(2,1)}, bf16[256,768]{1,0:T(8,128)(2,1)}, u32[]{:S(2)}, u32[]{:S(2)}) collective-permute-start(bf16[256,768]{1,0:T(8,128)(2,1)} %get-tuple-element.91), channel_id=1, source_target_pairs={{0,2},{1,17},{2,0},{3,19},{4,6},{5,21},{6,4},{7,23},{8,10},{9,25},... | collective-permute-start | bytes 1179656 | tf_op jit(solution)/shard_map/ppermute | solution.py:42
  103.7 16.4 %collective-permute-start.16 = (bf16[288,768]{1,0:T(8,128)(2,1)S(1)}, bf16[288,768]{1,0:T(8,128)(2,1)S(1)}, u32[]{:S(2)}, u32[]{:S(2)}) collective-permute-start(bf16[288,768]{1,0:T(8,128)(2,1)S(1)} %get-tuple-element.85), channel_id=1, source_target_pairs={{0,2},{1,17},{2,0},{3,19},{4,6},{5,21},{6,4},{7,23},{8,10},{9,25},... | collective-permute-start | bytes 1327112 | tf_op jit(solution)/shard_map/ppermute | solution.py:42
  106.7 18.5 %collective-permute-start.32 = (bf16[288,768]{1,0:T(8,128)(2,1)S(1)}, bf16[288,768]{1,0:T(8,128)(2,1)S(1)}, u32[]{:S(2)}, u32[]{:S(2)}) collective-permute-start(bf16[288,768]{1,0:T(8,128)(2,1)S(1)} %get-tuple-element.89), channel_id=1, source_target_pairs={{0,16},{1,3},{2,18},{3,1},{4,20},{5,7},{6,22},{7,5},{8,24},{9,11},... | collective-permute-start | bytes 1327112 | tf_op jit(solution)/shard_map/ppermute | solution.py:42
  114.1 64.9 %collective-permute-start.13 = (bf16[256,768]{1,0:T(8,128)(2,1)S(1)}, bf16[256,768]{1,0:T(8,128)(2,1)S(1)}, u32[]{:S(2)}, u32[]{:S(2)}) collective-permute-start(bf16[256,768]{1,0:T(8,128)(2,1)S(1)} %get-tuple-element.93), channel_id=1, source_target_pairs={{0,4},{1,9},{2,6},{3,11},{4,0},{5,13},{6,2},{7,15},{8,12},{9,1},{1... | collective-permute-start | bytes 1179656 | tf_op jit(solution)/shard_map/ppermute | solution.py:42
  120.2 12.0 %collective-permute-start.17 = (bf16[144,768]{1,0:T(8,128)(2,1)S(1)}, bf16[144,768]{1,0:T(8,128)(2,1)S(1)}, u32[]{:S(2)}, u32[]{:S(2)}) collective-permute-start(bf16[144,768]{1,0:T(8,128)(2,1)S(1)} %get-tuple-element.105), channel_id=1, source_target_pairs={{0,16},{1,3},{2,18},{3,1},{4,20},{5,7},{6,22},{7,5},{8,24},{9,11},... | collective-permute-start | bytes 663560 | tf_op jit(solution)/shard_map/ppermute | solution.py:42
  125.3 14.9 %collective-permute-start.33 = (bf16[144,768]{1,0:T(8,128)(2,1)S(1)}, bf16[144,768]{1,0:T(8,128)(2,1)S(1)}, u32[]{:S(2)}, u32[]{:S(2)}) collective-permute-start(bf16[144,768]{1,0:T(8,128)(2,1)S(1)} %get-tuple-element.101), channel_id=1, source_target_pairs={{0,4},{1,5},{2,6},{3,7},{4,0},{5,1},{6,2},{7,3},{8,12},{9,13},{10,... | collective-permute-start | bytes 663560 | tf_op jit(solution)/shard_map/ppermute | solution.py:42
  128.7 11.6 %collective-permute-start.27 = (bf16[64,768]{1,0:T(8,128)(2,1)S(1)}, bf16[64,768]{1,0:T(8,128)(2,1)S(1)}, u32[]{:S(2)}, u32[]{:S(2)}) collective-permute-start(bf16[64,768]{1,0:T(8,128)(2,1)S(1)} %add_convert_fusion.23), channel_id=1, source_target_pairs={{0,8},{1,5},{2,10},{3,7},{4,12},{5,1},{6,14},{7,3},{8,0},{9,13},{1... | collective-permute-start | bytes 294920 | tf_op jit(solution)/shard_map/ppermute | solution.py:42
  140.3 12.9 %collective-permute-start.28 = (bf16[128,768]{1,0:T(8,128)(2,1)S(1)}, bf16[128,768]{1,0:T(8,128)(2,1)S(1)}, u32[]{:S(2)}, u32[]{:S(2)}) collective-permute-start(bf16[128,768]{1,0:T(8,128)(2,1)S(1)} %pad_maximum_fusion.15), channel_id=1, source_target_pairs={{0,4},{1,9},{2,6},{3,11},{4,0},{5,13},{6,2},{7,15},{8,12},{9,1},{1... | collective-permute-start | bytes 589832 | tf_op jit(solution)/shard_map/ppermute | solution.py:42
  153.3 12.2 %collective-permute-start.29 = (bf16[256,768]{1,0:T(8,128)(2,1)S(1)}, bf16[256,768]{1,0:T(8,128)(2,1)S(1)}, u32[]{:S(2)}, u32[]{:S(2)}) collective-permute-start(bf16[256,768]{1,0:T(8,128)(2,1)S(1)} %pad_maximum_fusion.12), channel_id=1, source_target_pairs={{0,2},{1,17},{2,0},{3,19},{4,6},{5,21},{6,4},{7,23},{8,10},{9,25},... | collective-permute-start | bytes 1179656 | tf_op jit(solution)/shard_map/ppermute | solution.py:42
  157.2 10.7 %collective-permute-start.21 = (bf16[288,768]{1,0:T(8,128)(2,1)S(1)}, bf16[288,768]{1,0:T(8,128)(2,1)S(1)}, u32[]{:S(2)}, u32[]{:S(2)}) collective-permute-start(bf16[288,768]{1,0:T(8,128)(2,1)S(1)} %pad_maximum_fusion.9), channel_id=1, source_target_pairs={{0,2},{1,17},{2,0},{3,19},{4,6},{5,21},{6,4},{7,23},{8,10},{9,25},... | collective-permute-start | bytes 1327112 | tf_op jit(solution)/shard_map/ppermute | solution.py:42
  162.0 14.5 %collective-permute-start.37 = (bf16[288,768]{1,0:T(8,128)(2,1)S(1)}, bf16[288,768]{1,0:T(8,128)(2,1)S(1)}, u32[]{:S(2)}, u32[]{:S(2)}) collective-permute-start(bf16[288,768]{1,0:T(8,128)(2,1)S(1)} %pad_maximum_fusion.10), channel_id=1, source_target_pairs={{0,16},{1,3},{2,18},{3,1},{4,20},{5,7},{6,22},{7,5},{8,24},{9,11},... | collective-permute-start | bytes 1327112 | tf_op jit(solution)/shard_map/ppermute | solution.py:42
  168.2 23.1 %collective-permute-start.22 = (bf16[576,768]{1,0:T(8,128)(2,1)S(1)}, bf16[576,768]{1,0:T(8,128)(2,1)S(1)}, u32[]{:S(2)}, u32[]{:S(2)}) collective-permute-start(bf16[576,768]{1,0:T(8,128)(2,1)S(1)} %pad_maximum_fusion.3.own), channel_id=1, source_target_pairs={{0,4},{1,9},{2,6},{3,11},{4,0},{5,13},{6,2},{7,15},{8,12},{9,1},{1... | collective-permute-start | bytes 2654216 | tf_op jit(solution)/shard_map/ppermute | solution.py:42
  176.8 16.8 %collective-permute-start.38 = (bf16[576,768]{1,0:T(8,128)(2,1)S(1)}, bf16[576,768]{1,0:T(8,128)(2,1)S(1)}, u32[]{:S(2)}, u32[]{:S(2)}) collective-permute-start(bf16[576,768]{1,0:T(8,128)(2,1)S(1)} %pad_maximum_fusion.4.own), channel_id=1, source_target_pairs={{0,2},{1,17},{2,0},{3,19},{4,6},{5,21},{6,4},{7,23},{8,10},{9,25},... | collective-permute-start | bytes 2654216 | tf_op jit(solution)/shard_map/ppermute | solution.py:42
  177.4 12.1 %collective-permute-start.30 = (bf16[512,768]{1,0:T(8,128)(2,1)S(1)}, bf16[512,768]{1,0:T(8,128)(2,1)S(1)}, u32[]{:S(2)}, u32[]{:S(2)}) collective-permute-start(bf16[512,768]{1,0:T(8,128)(2,1)S(1)} %pad_maximum_fusion.6.own), channel_id=1, source_target_pairs={{0,16},{1,3},{2,18},{3,1},{4,20},{5,7},{6,22},{7,5},{8,24},{9,11},... | collective-permute-start | bytes 2359304 | tf_op jit(solution)/shard_map/ppermute | solution.py:42
  (40 other events, 244.0 us)

commit v6 on v5

--- a/solution.py
+++ b/solution.py
@@ -1,4 +1,5 @@
 from functools import partial
+import math
 
 import jax
 import jax.numpy as jnp
@@ -301,10 +302,6 @@
 def put_pair(ref, pair, values):
     rows = ref.shape[0]
 
-    @pl.when(pair == 0)
-    def _():
-        ref[...] = jnp.zeros_like(ref)
-
     lanes = lane_of((rows, LANES))
     kept = jnp.where(lanes == 2 * pair, values[:rows], ref[...])
     ref[...] = jnp.where(lanes == 2 * pair + 1, values[rows:], kept)
@@ -315,60 +312,77 @@
     return [slice(at, at + step) for at in range(0, count, step)]
 
 
-def attend_over(stacked, keys, values, peak, total, mixed):
+def attend_over(stacked, keys, values, lanes, peak, total, mixed):
     for at in chunks_of(keys.shape[0]):
-        logits = dot_nt(stacked, keys[at, :])
+        logits = dot_nt(stacked, keys[at, lanes])
         top = jnp.max(logits, axis=1, keepdims=True)
         if peak is None:
             weights = jnp.exp(logits - top)
             total = jnp.sum(weights, axis=1, keepdims=True)
-            mixed = dot_nn(weights.astype(BF16), values[at, :])
+            mixed = dot_nn(weights.astype(BF16), values[at, lanes])
         else:
             top = jnp.maximum(peak, top)
             weights = jnp.exp(logits - top)
             factor = jnp.exp(peak - top)
             total = total * factor + jnp.sum(weights, axis=1, keepdims=True)
-            mixed = mixed * factor + dot_nn(weights.astype(BF16), values[at, :])
+            mixed = mixed * factor + dot_nn(weights.astype(BF16), values[at, lanes])
         peak = top
     return peak, total, mixed
 
 
-def attend_first_kernel(queries, keys, values, out_mixed, out_peak, out_total):
-    pair = pl.program_id(0)
-    stacked = two_heads(queries[...])
-    peak, total, mixed = attend_over(stacked, keys, values, None, None, None)
-    out_mixed[...] = one_pair(mixed)
-    put_pair(out_peak, pair, peak)
-    put_pair(out_total, pair, total)
+def pairs_of(per, *shared):
+    @pl.when(pl.program_id(0) == 0)
+    def _():
+        for ref in shared:
+            ref[...] = jnp.zeros_like(ref)
+
+    return [
+        (pl.program_id(0) * per + p, slice(p * LANES, (p + 1) * LANES)) for p in range(per)
+    ]
+
+
+def attend_first_kernel(per, queries, keys, values, out_mixed, out_peak, out_total):
+    for pair, lanes in pairs_of(per, out_peak, out_total):
+        stacked = two_heads(queries[:, lanes])
+        peak, total, mixed = attend_over(stacked, keys, values, lanes, None, None, None)
+        out_mixed[:, lanes] = one_pair(mixed)
+        put_pair(out_peak, pair, peak)
+        put_pair(out_total, pair, total)
 
 
 def attend_last_kernel(
-    queries, keys, values, in_mixed, in_peak, in_total, attended, log_total
+    per, queries, keys, values, in_mixed, in_peak, in_total, attended, log_total
 ):
-    pair = pl.program_id(0)
-    stacked = two_heads(queries[...])
-    peak = column_pair(in_peak[...], 2 * pair)
-    total = column_pair(in_total[...], 2 * pair)
-    mixed = jnp.concatenate([in_mixed[...]] * 2, axis=0)
-    peak, total, mixed = attend_over(stacked, keys, values, peak, total, mixed)
-    attended[...] = one_pair(mixed / total)
-    put_pair(log_total, pair, peak + jnp.log(total))
+    for pair, lanes in pairs_of(per, log_total):
+        stacked = two_heads(queries[:, lanes])
+        peak = column_pair(in_peak[...], 2 * pair)
+        total = column_pair(in_total[...], 2 * pair)
+        mixed = jnp.concatenate([in_mixed[:, lanes]] * 2, axis=0)
+        peak, total, mixed = attend_over(stacked, keys, values, lanes, peak, total, mixed)
+        attended[:, lanes] = one_pair(mixed / total)
+        put_pair(log_total, pair, peak + jnp.log(total))
+
+
+def pairs_per_step(count, pairs):
+    return pairs if count <= 1024 else 1
 
 
 def attend(own_queries, halves):
     count = halves[0].shape[0]
     rows, width = own_queries.shape
     pairs = width // LANES
-    queries = pl.BlockSpec((rows, LANES), lambda j: (0, j))
+    per = pairs_per_step(count, pairs)
+    steps, wide_lanes = pairs // per, per * LANES
+    queries = pl.BlockSpec((rows, wide_lanes), lambda j: (0, j))
     shared = pl.BlockSpec((rows, LANES), lambda j: (0, 0))
-    keys = pl.BlockSpec((count, LANES), lambda j: (0, j))
-    values = pl.BlockSpec((count, LANES), lambda j: (0, pairs + j))
+    keys = pl.BlockSpec((count, wide_lanes), lambda j: (0, j))
+    values = pl.BlockSpec((count, wide_lanes), lambda j: (0, steps + j))
     wide = jax.ShapeDtypeStruct((rows, width), F32)
     thin = jax.ShapeDtypeStruct((rows, LANES), F32)
     work = cost(8 * rows * count * width, 6 * count * width)
     mixed, peak, total = pl.pallas_call(
-        attend_first_kernel,
-        grid=(pairs,),
+        partial(attend_first_kernel, per),
+        grid=(steps,),
         in_specs=[queries, keys, values],
         out_specs=[queries, shared, shared],
         out_shape=[wide, thin, thin],
@@ -377,8 +391,8 @@
         name="attend_first",
     )(own_queries, halves[0], halves[0])
     return pl.pallas_call(
-        attend_last_kernel,
-        grid=(pairs,),
+        partial(attend_last_kernel, per),
+        grid=(steps,),
         in_specs=[queries, keys, values, queries, shared, shared],
         out_specs=[queries, shared],
         out_shape=[wide, thin],
@@ -561,44 +575,46 @@
 
 
 def attend_back_kernel(
-    queries, keys_a, values_a, keys_b, values_b, grads, logs_deltas, cos, sin,
+    per, queries, keys_a, values_a, keys_b, values_b, grads, logs_deltas, cos, sin,
     out_queries, out_keys, out_values,
 ):
-    pair = pl.program_id(0)
     rows, count = queries.shape[0], keys_a.shape[0]
-    queries_two = two_heads(queries[...])
-    grads_two = two_heads(grads[...])
-    logs = row_pair(logs_deltas[...], 2 * pair)
-    deltas = row_pair(logs_deltas[...], HEADS + 2 * pair)
-    total = jnp.zeros((2 * rows, LANES), F32)
-    for base, keys, values in ((0, keys_a, values_a), (count, keys_b, values_b)):
-        for at in chunks_of(count):
-            to = slice(base + at.start, base + at.stop)
-            key_rows = keys[at, :]
-            probs = jnp.exp(dot_nt(key_rows, queries_two) - logs)
-            grad_probs = dot_nt(values[at, :], grads_two)
-            grad_scores = (probs * (grad_probs - deltas)).astype(BF16)
-            out_values[to, :] = dot_nn(probs.astype(BF16), grads_two).astype(BF16)
-            grad_keys = dot_nn(grad_scores, queries_two)
-            out_keys[to, :] = unrotated(grad_keys, cos[to, :], sin[to, :]).astype(BF16)
-            total = total + dot_tn(grad_scores, key_rows)
-    grad = one_pair(total) * 0.125
-    out_queries[...] = unrotated(grad, cos[:rows, :], sin[:rows, :]).astype(BF16)
+    for pair, lanes in pairs_of(per):
+        queries_two = two_heads(queries[:, lanes])
+        grads_two = two_heads(grads[:, lanes])
+        logs = row_pair(logs_deltas[...], 2 * pair)
+        deltas = row_pair(logs_deltas[...], HEADS + 2 * pair)
+        total = jnp.zeros((2 * rows, LANES), F32)
+        for base, keys, values in ((0, keys_a, values_a), (count, keys_b, values_b)):
+            for at in chunks_of(count):
+                to = slice(base + at.start, base + at.stop)
+                key_rows = keys[at, lanes]
+                probs = jnp.exp(dot_nt(key_rows, queries_two) - logs)
+                grad_probs = dot_nt(values[at, lanes], grads_two)
+                grad_scores = (probs * (grad_probs - deltas)).astype(BF16)
+                out_values[to, lanes] = dot_nn(probs.astype(BF16), grads_two).astype(BF16)
+                grad_keys = dot_nn(grad_scores, queries_two)
+                out_keys[to, lanes] = unrotated(grad_keys, cos[to, :], sin[to, :]).astype(BF16)
+                total = total + dot_tn(grad_scores, key_rows)
+        grad = one_pair(total) * 0.125
+        out_queries[:, lanes] = unrotated(grad, cos[:rows, :], sin[:rows, :]).astype(BF16)
 
 
 def attend_back(own_queries, halves, grads, logs_deltas, cos, sin):
     count = halves[0].shape[0]
     rows, width = own_queries.shape
     pairs = width // LANES
-    queries = pl.BlockSpec((rows, LANES), lambda j: (0, j))
+    per = pairs_per_step(count, pairs)
+    steps, wide_lanes = pairs // per, per * LANES
+    queries = pl.BlockSpec((rows, wide_lanes), lambda j: (0, j))
     shared = pl.BlockSpec((LANES, rows), lambda j: (0, 0))
-    keys = pl.BlockSpec((count, LANES), lambda j: (0, j))
-    values = pl.BlockSpec((count, LANES), lambda j: (0, pairs + j))
+    keys = pl.BlockSpec((count, wide_lanes), lambda j: (0, j))
+    values = pl.BlockSpec((count, wide_lanes), lambda j: (0, steps + j))
     table = pl.BlockSpec((2 * count, LANES), lambda j: (0, 0))
-    made = pl.BlockSpec((2 * count, LANES), lambda j: (0, j))
+    made = pl.BlockSpec((2 * count, wide_lanes), lambda j: (0, j))
     return pl.pallas_call(
-        attend_back_kernel,
-        grid=(pairs,),
+        partial(attend_back_kernel, per),
+        grid=(steps,),
         in_specs=[queries, keys, values, keys, values, queries, shared, table, table],
         out_specs=[queries, made, made],
         out_shape=[
@@ -647,12 +663,38 @@
                 out[3 * half :, :] = jnp.zeros((out.shape[0] - 3 * half, width), BF16)
 
 
+def late_rows_whole_kernel(
+    core, low_a, low_b, grad_q, grad_k, grad_v, out_own, out_other, turned
+):
+    count, width = low_a.shape
+    half, own_rows = width // 2, grad_q.shape[0]
+    turned[:, :count] = low_a[...].T
+    turned[:, count:] = low_b[...].T
+    for out, side in ((out_own, core[0]), (out_other, 1 - core[0])):
+        left = turned[pl.ds(pl.multiple_of(side * half, half), half), :]
+        out[:half, :] = dot_nn(left[:, :own_rows], grad_q[...]).astype(BF16)
+        out[half : 2 * half, :] = dot_nn(left, grad_k[...]).astype(BF16)
+        out[2 * half : 3 * half, :] = dot_nn(left, grad_v[...]).astype(BF16)
+        if out.shape[0] > 3 * half:
+            out[3 * half :, :] = jnp.zeros((out.shape[0] - 3 * half, width), BF16)
+
+
 def late_rows(core, pieces, lows, grad_q, grad_k, grad_v):
     count, width = lows[0].shape
     own_rows = grad_q.shape[0]
     step = min(count, 512)
     each = count // step
     total = padded(3 * width // 2, pieces)
+    if each == 1:
+        return pl.pallas_call(
+            late_rows_whole_kernel,
+            in_specs=[SMEM_SPEC] + [WHOLE] * 5,
+            out_shape=[jax.ShapeDtypeStruct((total, width), BF16)] * 2,
+            scratch_shapes=[pltpu.VMEM((width, 2 * count), BF16)],
+            compiler_params=params(16),
+            cost_estimate=cost(4 * count * width * width, 8 * count * width),
+            name="late_rows",
+        )(core, *lows, grad_q, grad_k, grad_v)
     grads = pl.BlockSpec((step, width), lambda i: (i, 0))
     fixed = pl.BlockSpec((own_rows, width), lambda i: (0, 0))
     made = pl.BlockSpec((total, width), lambda i: (0, 0))

time: 196 us -> 193 us (0.985)
  Pallas kernels: 44.9 us -> 39.8 us
  starting transfers between devices: 50.6 us -> 54.3 us
  waiting for transfers between devices: 63.9 us -> 61.6 us
    pallas_call x4, Pallas kernels: 21.1 us -> 15.8 us  [the longest x1 6.22 us: attend_back(): pl.pallas_call(partial(attend_back_kernel, per), grid=(steps,), in_specs=...]
    ppermute x30, starting transfers between devices: 48.4 us -> 52.1 us  [flip(): return lax.ppermute(block, ('seq', 'ctx', 'wsh'), route)]
    ppermute x30, waiting for transfers between devices: 63.9 us -> 61.6 us  [flip(): return lax.ppermute(block, ('seq', 'ctx', 'wsh'), route)]
  transfers between devices with their start and end apart: 39 -> 39, of which waited for: 16 -> 17; matrix products, arithmetic and copies ran while one was open for 12% -> 12% of each run, Pallas kernels for 12% -> 11%
where the time goes in v6:
time: 193 us; the launch traced here: 192 us
  waiting for transfers between devices  61.6 us (32%)
  starting transfers between devices  54.3 us (28%)
  Pallas kernels  39.8 us (21%)
  other arithmetic  18.2 us (9%)
  local copies, waits for them, and re-layouts  17.1 us (9%)
    ppermute x30, waiting for transfers between devices, flip(): return lax.ppermute(block, ('seq', 'ctx', 'wsh'), route)  61.6 us
    ppermute x30, starting transfers between devices, flip(): return lax.ppermute(block, ('seq', 'ctx', 'wsh'), route)  52.1 us
    unnamed x50, local copies, waits for them, and re-layouts  10.2 us
    convert_element_type x13, other arithmetic, summed(): return sum(cut[1:], cut[0]).astype(BF16)  9.74 us
    pallas_call x2, Pallas kernels, project(): pl.pallas_call(project_kernel, grid=(rows // step,), in_specs=[SMEM_SPEC,...  6.66 us
    pallas_call x3, Pallas kernels, unpack(): pl.pallas_call(partial(unpack_kernel, places, bool(gained)), in_specs=[SM...  6.51 us
    pallas_call x1, Pallas kernels, attend_back(): pl.pallas_call(partial(attend_back_kernel, per), grid=(steps,), in_specs=...  6.22 us
    pallas_call x1, Pallas kernels, late_rows(): pl.pallas_call(late_rows_whole_kernel, in_specs=[SMEM_SPEC] + [WHOLE] * 5...  4.65 us
  transfers between devices with their start and end apart: 39, of which 17 were waited for; matrix products, arithmetic and copies ran while one was open for 12% of the time, Pallas kernels for 11%

profile of v6, /device:TPU:0, one launch (start us, length us, event | category | flops | bytes accessed | tf_op | source)
XLA Modules:
  0.0 192.2 jit_solution(16759346184311739120)
XLA Ops:
  0.6 4.1 %collective-permute-start = (bf16[128,768]{1,0:T(8,128)(2,1)}, bf16[128,768]{1,0:T(8,128)(2,1)S(1)}, u32[]{:S(2)}, u32[]{:S(2)}) collective-permute-start(bf16[128,768]{1,0:T(8,128)(2,1)} %bitcast.10), channel_id=1, source_target_pairs={{0,8},{1,3},{2,10},{3,1},{4,12},{5,7},{6,14},{7,5},{8,0},{9,11},{1... | collective-permute-start | bytes 589832 | tf_op jit(solution)/shard_map/ppermute | solution.py:43
  12.7 10.2 %collective-permute-done.1 = bf16[256,768]{1,0:T(8,128)(2,1)S(1)} collective-permute-done((bf16[256,768]{1,0:T(8,128)(2,1)S(1)}, bf16[256,768]{1,0:T(8,128)(2,1)S(1)}, u32[]{:S(2)}, u32[]{:S(2)}) %collective-permute-start.1) | collective-permute-done | bytes 393248 | tf_op jit(solution)/shard_map/ppermute | solution.py:43
  28.1 4.3 %project.2 = (bf16[512,1536]{1,0:T(8,128)(2,1)S(1)}, bf16[512,768]{1,0:T(8,128)(2,1)S(1)}, bf16[128,768]{1,0:T(8,128)(2,1)S(1)}, bf16[768,2304]{1,0:T(8,128)(2,1)S(1)}) custom-call(s32[1]{0:T(128)} %bitcast.core, bf16[512,768]{1,0:T(8,128)(2,1)S(1)} %pad_maximum_fusion.5.tokens, bf16[384,2304]{1,0:T(8,128)(2,1)S(1)} %copy-done.1, ...), custom_call_target="tpu_custom_call" | custom-call | flops 1207959552 | bytes 3145728 | tf_op jit(solution)/shard_map/project/pallas_call | solution.py:263
  37.4 2.9 %attend_last.1 = (f32[128,768]{1,0:T(8,128)S(1)}, f32[128,128]{1,0:T(8,128)S(1)}) custom-call(bf16[128,768]{1,0:T(8,128)(2,1)S(1)} %get-tuple-element.46.queries, bf16[512,1536]{1,0:T(8,128)(2,1)S(1)} %get-tuple-element.48.keys.values.keys_b.values_b, bf16[512,1536]{1,0:T(8,128)(2,1)S(1)} %get-tuple-element.48.keys.values.keys_b.values_b, ...), custom_call_target="tpu_custom_call" | custom-call | flops 402653184 | bytes 2359296 | tf_op jit(solution)/shard_map/attend_last/pallas_call | solution.py:393
  40.2 4.6 %middle.1 = (bf16[128,768]{1,0:T(8,128)(2,1)}, bf16[128,1408]{1,0:T(8,128)(2,1)S(1)}, bf16[128,1408]{1,0:T(8,128)(2,1)S(1)}, bf16[128,3072]{1,0:T(8,128)(2,1)S(1...) custom-call(s32[1]{0:T(128)} %bitcast.core, bf16[128,768]{1,0:T(8,128)(2,1)S(1)} %bitcast.13, ...), custom_call_target="tpu_custom_call" | custom-call | flops 3321888768 | bytes 25165824 | tf_op jit(solution)/shard_map/middle/pallas_call | solution.py:468
  45.5 6.2 %attend_back.1 = (bf16[128,768]{1,0:T(8,128)(2,1)S(1)}, bf16[1024,768]{1,0:T(8,128)(2,1)S(1)}, bf16[1024,768]{1,0:T(8,128)(2,1)S(1)}) custom-call(bf16[128,768]{1,0:T(8,128)(2,1)S(1)} %get-tuple-element.46.queries, bf16[512,1536]{1,0:T(8,128)(2,1)S(1)} %get-tuple-element.49.keys.values.keys_a.values_a, ...), custom_call_target="tpu_custom_call" | custom-call | flops 2013265920 | bytes 7864320 | tf_op jit(solution)/shard_map/attend_back/pallas_call | solution.py:615
  55.5 4.7 %late_rows.1 = (bf16[1152,768]{1,0:T(8,128)(2,1)S(1)}, bf16[1152,768]{1,0:T(8,128)(2,1)}) custom-call(s32[1]{0:T(128)} %bitcast.core, bf16[512,768]{1,0:T(8,128)(2,1)S(1)} %get-tuple-element.68.low_a, bf16[512,768]{1,0:T(8,128)(2,1)S(1)} %get-tuple-element.69.low_b, bf16[128,768]{1,0:T(8,128)(2,1)S(1)} %get-tuple-element.77.grad_q, ...), custom_call_target="tpu_custom_call" | custom-call | flops 1207959552 | bytes 3145728 | tf_op jit(solution)/shard_map/late_rows/pallas_call | solution.py:689
  75.8 3.9 %first_rows.1 = bf16[1024,768]{1,0:T(8,128)(2,1)S(1)} custom-call(bf16[128,768]{1,0:T(8,128)(2,1)S(1)} %copy-done.20, bf16[1024,768]{1,0:T(8,128)(2,1)S(1)} %copy-done.11, bf16[1024,768]{1,0:T(8,128)(2,1)S(1)} %copy-done.13, bf16[768,2304]{1,0:T(8,128)(2,1)S(1)} %copy-done.3), custom_call_target="tpu_custom_call" | custom-call | flops 2415919104 | bytes 6291456 | tf_op jit(solution)/shard_map/first_rows/pallas_call | solution.py:741
  82.4 6.6 %collective-permute-done.23 = bf16[512,768]{1,0:T(8,128)(2,1)} collective-permute-done((bf16[512,768]{1,0:T(8,128)(2,1)}, bf16[512,768]{1,0:T(8,128)(2,1)}, u32[]{:S(2)}, u32[]{:S(2)}) %collective-permute-start.23) | collective-permute-done | bytes 786464 | tf_op jit(solution)/shard_map/ppermute | solution.py:43
  91.4 2.6 %collective-permute-start.24 = (bf16[256,768]{1,0:T(8,128)(2,1)}, bf16[256,768]{1,0:T(8,128)(2,1)}, u32[]{:S(2)}, u32[]{:S(2)}) collective-permute-start(bf16[256,768]{1,0:T(8,128)(2,1)} %get-tuple-element.91), channel_id=1, source_target_pairs={{0,2},{1,17},{2,0},{3,19},{4,6},{5,21},{6,4},{7,23},{8,10},{9,25},... | collective-permute-start | bytes 1179656 | tf_op jit(solution)/shard_map/ppermute | solution.py:43
  94.0 3.8 %collective-permute-done.15 = bf16[576,768]{1,0:T(8,128)(2,1)} collective-permute-done((bf16[576,768]{1,0:T(8,128)(2,1)}, bf16[576,768]{1,0:T(8,128)(2,1)}, u32[]{:S(2)}, u32[]{:S(2)}) %collective-permute-start.15) | collective-permute-done | bytes 884768 | tf_op jit(solution)/shard_map/ppermute | solution.py:43
  103.9 2.5 %collective-permute-done.24 = bf16[256,768]{1,0:T(8,128)(2,1)} collective-permute-done((bf16[256,768]{1,0:T(8,128)(2,1)}, bf16[256,768]{1,0:T(8,128)(2,1)}, u32[]{:S(2)}, u32[]{:S(2)}) %collective-permute-start.24) | collective-permute-done | bytes 393248 | tf_op jit(solution)/shard_map/ppermute | solution.py:43
  110.9 4.3 %collective-permute-done.16 = bf16[288,768]{1,0:T(8,128)(2,1)S(1)} collective-permute-done((bf16[288,768]{1,0:T(8,128)(2,1)S(1)}, bf16[288,768]{1,0:T(8,128)(2,1)S(1)}, u32[]{:S(2)}, u32[]{:S(2)}) %collective-permute-start.16) | collective-permute-done | bytes 442400 | tf_op jit(solution)/shard_map/ppermute | solution.py:43
  119.5 2.5 %collective-permute-start.33 = (bf16[144,768]{1,0:T(8,128)(2,1)S(1)}, bf16[144,768]{1,0:T(8,128)(2,1)S(1)}, u32[]{:S(2)}, u32[]{:S(2)}) collective-permute-start(bf16[144,768]{1,0:T(8,128)(2,1)S(1)} %get-tuple-element.101), channel_id=1, source_target_pairs={{0,4},{1,5},{2,6},{3,7},{4,0},{5,1},{6,2},{7,3},{8,12},{9,13},{10,... | collective-permute-start | bytes 663560 | tf_op jit(solution)/shard_map/ppermute | solution.py:43
  123.5 3.5 %collective-permute-start.27 = (bf16[64,768]{1,0:T(8,128)(2,1)S(1)}, bf16[64,768]{1,0:T(8,128)(2,1)S(1)}, u32[]{:S(2)}, u32[]{:S(2)}) collective-permute-start(bf16[64,768]{1,0:T(8,128)(2,1)S(1)} %add_convert_fusion.23), channel_id=1, source_target_pairs={{0,8},{1,5},{2,10},{3,7},{4,12},{5,1},{6,14},{7,3},{8,0},{9,13},{1... | collective-permute-start | bytes 294920 | tf_op jit(solution)/shard_map/ppermute | solution.py:43
  127.2 6.2 %collective-permute-done.33 = bf16[144,768]{1,0:T(8,128)(2,1)S(1)} collective-permute-done((bf16[144,768]{1,0:T(8,128)(2,1)S(1)}, bf16[144,768]{1,0:T(8,128)(2,1)S(1)}, u32[]{:S(2)}, u32[]{:S(2)}) %collective-permute-start.33) | collective-permute-done | bytes 221216 | tf_op jit(solution)/shard_map/ppermute | solution.py:43
  134.7 2.5 %collective-permute-start.28 = (bf16[128,768]{1,0:T(8,128)(2,1)S(1)}, bf16[128,768]{1,0:T(8,128)(2,1)S(1)}, u32[]{:S(2)}, u32[]{:S(2)}) collective-permute-start(bf16[128,768]{1,0:T(8,128)(2,1)S(1)} %pad_maximum_fusion.15), channel_id=1, source_target_pairs={{0,4},{1,9},{2,6},{3,11},{4,0},{5,13},{6,2},{7,15},{8,12},{9,1},{1... | collective-permute-start | bytes 589832 | tf_op jit(solution)/shard_map/ppermute | solution.py:43
  145.5 4.6 %collective-permute-start.29 = (bf16[256,768]{1,0:T(8,128)(2,1)S(1)}, bf16[256,768]{1,0:T(8,128)(2,1)S(1)}, u32[]{:S(2)}, u32[]{:S(2)}) collective-permute-start(bf16[256,768]{1,0:T(8,128)(2,1)S(1)} %pad_maximum_fusion.12), channel_id=1, source_target_pairs={{0,2},{1,17},{2,0},{3,19},{4,6},{5,21},{6,4},{7,23},{8,10},{9,25},... | collective-permute-start | bytes 1179656 | tf_op jit(solution)/shard_map/ppermute | solution.py:43
  150.1 2.6 %collective-permute-start.36 = (bf16[144,768]{1,0:T(8,128)(2,1)S(1)}, bf16[144,768]{1,0:T(8,128)(2,1)S(1)}, u32[]{:S(2)}, u32[]{:S(2)}) collective-permute-start(bf16[144,768]{1,0:T(8,128)(2,1)S(1)} %pad_maximum_fusion.14), channel_id=1, source_target_pairs={{0,4},{1,5},{2,6},{3,7},{4,0},{5,1},{6,2},{7,3},{8,12},{9,13},{10,... | collective-permute-start | bytes 663560 | tf_op jit(solution)/shard_map/ppermute | solution.py:43
  154.0 4.5 %collective-permute-done.36 = bf16[144,768]{1,0:T(8,128)(2,1)S(1)} collective-permute-done((bf16[144,768]{1,0:T(8,128)(2,1)S(1)}, bf16[144,768]{1,0:T(8,128)(2,1)S(1)}, u32[]{:S(2)}, u32[]{:S(2)}) %collective-permute-start.36) | collective-permute-done | bytes 221216 | tf_op jit(solution)/shard_map/ppermute | solution.py:43
  160.0 5.0 %collective-permute-done.21 = bf16[288,768]{1,0:T(8,128)(2,1)S(1)} collective-permute-done((bf16[288,768]{1,0:T(8,128)(2,1)S(1)}, bf16[288,768]{1,0:T(8,128)(2,1)S(1)}, u32[]{:S(2)}, u32[]{:S(2)}) %collective-permute-start.21) | collective-permute-done | bytes 442400 | tf_op jit(solution)/shard_map/ppermute | solution.py:43
  165.2 2.9 %collective-permute-start.22 = (bf16[576,768]{1,0:T(8,128)(2,1)S(1)}, bf16[576,768]{1,0:T(8,128)(2,1)S(1)}, u32[]{:S(2)}, u32[]{:S(2)}) collective-permute-start(bf16[576,768]{1,0:T(8,128)(2,1)S(1)} %pad_maximum_fusion.3.own), channel_id=1, source_target_pairs={{0,4},{1,9},{2,6},{3,11},{4,0},{5,13},{6,2},{7,15},{8,12},{9,1},{1... | collective-permute-start | bytes 2654216 | tf_op jit(solution)/shard_map/ppermute | solution.py:43
  168.1 3.6 %collective-permute-done.37 = bf16[288,768]{1,0:T(8,128)(2,1)S(1)} collective-permute-done((bf16[288,768]{1,0:T(8,128)(2,1)S(1)}, bf16[288,768]{1,0:T(8,128)(2,1)S(1)}, u32[]{:S(2)}, u32[]{:S(2)}) %collective-permute-start.37) | collective-permute-done | bytes 442400 | tf_op jit(solution)/shard_map/ppermute | solution.py:43
  176.4 7.9 %collective-permute-done.14.part_b = bf16[128,768]{1,0:T(8,128)(2,1)S(1)} collective-permute-done((bf16[128,768]{1,0:T(8,128)(2,1)S(1)}, bf16[128,768]{1,0:T(8,128)(2,1)S(1)}, u32[]{:S(2)}, u32[]{:S(2)}) %collective-permute-start.14) | collective-permute-done | bytes 196640 | tf_op jit(solution)/shard_map/ppermute | solution.py:43
  (173 shorter events, 84.3 us)
Async XLA Ops:
  4.7 23.4 %collective-permute-start.2 = (bf16[384,2304]{1,0:T(8,128)(2,1)}, bf16[384,2304]{1,0:T(8,128)(2,1)}, u32[]{:S(2)}, u32[]{:S(2)}) collective-permute-start(bf16[384,2304]{1,0:T(8,128)(2,1)} %refs_0_.2), channel_id=1, source_target_pairs={{0,1},{1,0},{2,3},{3,2},{4,5},{5,4},{6,7},{7,6},{8,9},{9,8},{10,11... | collective-permute-start | bytes 5308424 | tf_op jit(solution)/shard_map/ppermute | solution.py:47
  6.7 17.9 %collective-permute-start.5 = (bf16[384,768]{1,0:T(8,128)(2,1)}, bf16[384,768]{1,0:T(8,128)(2,1)S(1)}, u32[]{:S(2)}, u32[]{:S(2)}) collective-permute-start(bf16[384,768]{1,0:T(8,128)(2,1)} %param.12), channel_id=1, source_target_pairs={{0,1},{1,0},{2,3},{3,2},{4,5},{5,4},{6,7},{7,6},{8,9},{9,8},{10,11... | collective-permute-start | bytes 1769480 | tf_op jit(solution)/shard_map/ppermute | solution.py:47
  6.8 18.3 %collective-permute-start.6 = (bf16[384,2304]{1,0:T(8,128)(2,1)}, bf16[384,2304]{1,0:T(8,128)(2,1)}, u32[]{:S(2)}, u32[]{:S(2)}) collective-permute-start(bf16[384,2304]{1,0:T(8,128)(2,1)} %refs_0_.3), channel_id=1, source_target_pairs={{0,1},{1,0},{2,3},{3,2},{4,5},{5,4},{6,7},{7,6},{8,9},{9,8},{10,11... | collective-permute-start | bytes 5308424 | tf_op jit(solution)/shard_map/ppermute | solution.py:47
  10.9 12.1 %collective-permute-start.1 = (bf16[256,768]{1,0:T(8,128)(2,1)S(1)}, bf16[256,768]{1,0:T(8,128)(2,1)S(1)}, u32[]{:S(2)}, u32[]{:S(2)}) collective-permute-start(bf16[256,768]{1,0:T(8,128)(2,1)S(1)} %pad_maximum_fusion.11), channel_id=1, source_target_pairs={{0,4},{1,9},{2,6},{3,11},{4,0},{5,13},{6,2},{7,15},{8,12},{9,1},{1... | collective-permute-start | bytes 1179656 | tf_op jit(solution)/shard_map/ppermute | solution.py:43
  12.6 12.2 %collective-permute-start.7 = (bf16[576,768]{1,0:T(8,128)(2,1)S(1)}, bf16[576,768]{1,0:T(8,128)(2,1)S(1)}, u32[]{:S(2)}, u32[]{:S(2)}) collective-permute-start(bf16[576,768]{1,0:T(8,128)(2,1)S(1)} %copy-done.23), channel_id=1, source_target_pairs={{0,1},{1,0},{2,3},{3,2},{4,5},{5,4},{6,7},{7,6},{8,9},{9,8},{10,11... | collective-permute-start | bytes 2654216 | tf_op jit(solution)/shard_map/ppermute | solution.py:47
  23.0 12.1 %collective-permute-start.4 = (bf16[512,768]{1,0:T(8,128)(2,1)S(1)}, bf16[512,768]{1,0:T(8,128)(2,1)S(1)}, u32[]{:S(2)}, u32[]{:S(2)}) collective-permute-start(bf16[512,768]{1,0:T(8,128)(2,1)S(1)} %pad_maximum_fusion.5.tokens), channel_id=1, source_target_pairs={{0,2},{1,5},{2,0},{3,7},{4,6},{5,1},{6,4},{7,3},{8,10},{9,13},{10,... | collective-permute-start | bytes 2359304 | tf_op jit(solution)/shard_map/ppermute | solution.py:43
  69.9 19.0 %collective-permute-start.23 = (bf16[512,768]{1,0:T(8,128)(2,1)}, bf16[512,768]{1,0:T(8,128)(2,1)}, u32[]{:S(2)}, u32[]{:S(2)}) collective-permute-start(bf16[512,768]{1,0:T(8,128)(2,1)} %constant_dynamic-slice_fusion.1), channel_id=1, source_target_pairs={{0,16},{1,3},{2,18},{3,1},{4,20},{5,7},{6,22},{7,5},{8,24},{9,11},... | collective-permute-start | bytes 2359304 | tf_op jit(solution)/shard_map/ppermute | solution.py:43
  71.4 26.4 %collective-permute-start.15 = (bf16[576,768]{1,0:T(8,128)(2,1)}, bf16[576,768]{1,0:T(8,128)(2,1)}, u32[]{:S(2)}, u32[]{:S(2)}) collective-permute-start(bf16[576,768]{1,0:T(8,128)(2,1)} %add_convert_fusion), channel_id=1, source_target_pairs={{0,4},{1,9},{2,6},{3,11},{4,0},{5,13},{6,2},{7,15},{8,12},{9,1},{1... | collective-permute-start | bytes 2654216 | tf_op jit(solution)/shard_map/ppermute | solution.py:43
  71.5 28.9 %collective-permute-start.31 = (bf16[576,768]{1,0:T(8,128)(2,1)}, bf16[576,768]{1,0:T(8,128)(2,1)}, u32[]{:S(2)}, u32[]{:S(2)}) collective-permute-start(bf16[576,768]{1,0:T(8,128)(2,1)} %constant_dynamic-slice_fusion), channel_id=1, source_target_pairs={{0,2},{1,17},{2,0},{3,19},{4,6},{5,21},{6,4},{7,23},{8,10},{9,25},... | collective-permute-start | bytes 2654216 | tf_op jit(solution)/shard_map/ppermute | solution.py:43
  81.8 25.8 %collective-permute-start.12 = (bf16[512,768]{1,0:T(8,128)(2,1)}, bf16[512,768]{1,0:T(8,128)(2,1)}, u32[]{:S(2)}, u32[]{:S(2)}) collective-permute-start(bf16[512,768]{1,0:T(8,128)(2,1)} %slice.70), channel_id=1, source_target_pairs={{0,2},{1,5},{2,0},{3,7},{4,6},{5,1},{6,4},{7,3},{8,10},{9,13},{10,... | collective-permute-start | bytes 2359304 | tf_op jit(solution)/shard_map/ppermute | solution.py:43
  91.4 14.9 %collective-permute-start.24 = (bf16[256,768]{1,0:T(8,128)(2,1)}, bf16[256,768]{1,0:T(8,128)(2,1)}, u32[]{:S(2)}, u32[]{:S(2)}) collective-permute-start(bf16[256,768]{1,0:T(8,128)(2,1)} %get-tuple-element.91), channel_id=1, source_target_pairs={{0,2},{1,17},{2,0},{3,19},{4,6},{5,21},{6,4},{7,23},{8,10},{9,25},... | collective-permute-start | bytes 1179656 | tf_op jit(solution)/shard_map/ppermute | solution.py:43
  99.8 15.4 %collective-permute-start.16 = (bf16[288,768]{1,0:T(8,128)(2,1)S(1)}, bf16[288,768]{1,0:T(8,128)(2,1)S(1)}, u32[]{:S(2)}, u32[]{:S(2)}) collective-permute-start(bf16[288,768]{1,0:T(8,128)(2,1)S(1)} %get-tuple-element.85), channel_id=1, source_target_pairs={{0,2},{1,17},{2,0},{3,19},{4,6},{5,21},{6,4},{7,23},{8,10},{9,25},... | collective-permute-start | bytes 1327112 | tf_op jit(solution)/shard_map/ppermute | solution.py:43
  101.8 17.6 %collective-permute-start.32 = (bf16[288,768]{1,0:T(8,128)(2,1)S(1)}, bf16[288,768]{1,0:T(8,128)(2,1)S(1)}, u32[]{:S(2)}, u32[]{:S(2)}) collective-permute-start(bf16[288,768]{1,0:T(8,128)(2,1)S(1)} %get-tuple-element.89), channel_id=1, source_target_pairs={{0,16},{1,3},{2,18},{3,1},{4,20},{5,7},{6,22},{7,5},{8,24},{9,11},... | collective-permute-start | bytes 1327112 | tf_op jit(solution)/shard_map/ppermute | solution.py:43
  108.9 66.8 %collective-permute-start.13 = (bf16[256,768]{1,0:T(8,128)(2,1)S(1)}, bf16[256,768]{1,0:T(8,128)(2,1)S(1)}, u32[]{:S(2)}, u32[]{:S(2)}) collective-permute-start(bf16[256,768]{1,0:T(8,128)(2,1)S(1)} %get-tuple-element.93), channel_id=1, source_target_pairs={{0,4},{1,9},{2,6},{3,11},{4,0},{5,13},{6,2},{7,15},{8,12},{9,1},{1... | collective-permute-start | bytes 1179656 | tf_op jit(solution)/shard_map/ppermute | solution.py:43
  115.3 11.7 %collective-permute-start.17 = (bf16[144,768]{1,0:T(8,128)(2,1)S(1)}, bf16[144,768]{1,0:T(8,128)(2,1)S(1)}, u32[]{:S(2)}, u32[]{:S(2)}) collective-permute-start(bf16[144,768]{1,0:T(8,128)(2,1)S(1)} %get-tuple-element.105), channel_id=1, source_target_pairs={{0,16},{1,3},{2,18},{3,1},{4,20},{5,7},{6,22},{7,5},{8,24},{9,11},... | collective-permute-start | bytes 663560 | tf_op jit(solution)/shard_map/ppermute | solution.py:43
  119.5 13.8 %collective-permute-start.33 = (bf16[144,768]{1,0:T(8,128)(2,1)S(1)}, bf16[144,768]{1,0:T(8,128)(2,1)S(1)}, u32[]{:S(2)}, u32[]{:S(2)}) collective-permute-start(bf16[144,768]{1,0:T(8,128)(2,1)S(1)} %get-tuple-element.101), channel_id=1, source_target_pairs={{0,4},{1,5},{2,6},{3,7},{4,0},{5,1},{6,2},{7,3},{8,12},{9,13},{10,... | collective-permute-start | bytes 663560 | tf_op jit(solution)/shard_map/ppermute | solution.py:43
  123.5 11.2 %collective-permute-start.27 = (bf16[64,768]{1,0:T(8,128)(2,1)S(1)}, bf16[64,768]{1,0:T(8,128)(2,1)S(1)}, u32[]{:S(2)}, u32[]{:S(2)}) collective-permute-start(bf16[64,768]{1,0:T(8,128)(2,1)S(1)} %add_convert_fusion.23), channel_id=1, source_target_pairs={{0,8},{1,5},{2,10},{3,7},{4,12},{5,1},{6,14},{7,3},{8,0},{9,13},{1... | collective-permute-start | bytes 294920 | tf_op jit(solution)/shard_map/ppermute | solution.py:43
  127.1 10.7 %collective-permute-start.18 = (bf16[72,768]{1,0:T(8,128)(2,1)S(1)}, bf16[72,768]{1,0:T(8,128)(2,1)S(1)}, u32[]{:S(2)}, u32[]{:S(2)}) collective-permute-start(bf16[72,768]{1,0:T(8,128)(2,1)S(1)} %add_convert_fusion.21), channel_id=1, source_target_pairs={{0,8},{1,5},{2,10},{3,7},{4,12},{5,1},{6,14},{7,3},{8,0},{9,13},{1... | collective-permute-start | bytes 331784 | tf_op jit(solution)/shard_map/ppermute | solution.py:43
  145.5 14.3 %collective-permute-start.29 = (bf16[256,768]{1,0:T(8,128)(2,1)S(1)}, bf16[256,768]{1,0:T(8,128)(2,1)S(1)}, u32[]{:S(2)}, u32[]{:S(2)}) collective-permute-start(bf16[256,768]{1,0:T(8,128)(2,1)S(1)} %pad_maximum_fusion.12), channel_id=1, source_target_pairs={{0,2},{1,17},{2,0},{3,19},{4,6},{5,21},{6,4},{7,23},{8,10},{9,25},... | collective-permute-start | bytes 1179656 | tf_op jit(solution)/shard_map/ppermute | solution.py:43
  152.8 12.2 %collective-permute-start.21 = (bf16[288,768]{1,0:T(8,128)(2,1)S(1)}, bf16[288,768]{1,0:T(8,128)(2,1)S(1)}, u32[]{:S(2)}, u32[]{:S(2)}) collective-permute-start(bf16[288,768]{1,0:T(8,128)(2,1)S(1)} %pad_maximum_fusion.9), channel_id=1, source_target_pairs={{0,2},{1,17},{2,0},{3,19},{4,6},{5,21},{6,4},{7,23},{8,10},{9,25},... | collective-permute-start | bytes 1327112 | tf_op jit(solution)/shard_map/ppermute | solution.py:43
  158.6 13.1 %collective-permute-start.37 = (bf16[288,768]{1,0:T(8,128)(2,1)S(1)}, bf16[288,768]{1,0:T(8,128)(2,1)S(1)}, u32[]{:S(2)}, u32[]{:S(2)}) collective-permute-start(bf16[288,768]{1,0:T(8,128)(2,1)S(1)} %pad_maximum_fusion.10), channel_id=1, source_target_pairs={{0,16},{1,3},{2,18},{3,1},{4,20},{5,7},{6,22},{7,5},{8,24},{9,11},... | collective-permute-start | bytes 1327112 | tf_op jit(solution)/shard_map/ppermute | solution.py:43
  165.2 22.2 %collective-permute-start.22 = (bf16[576,768]{1,0:T(8,128)(2,1)S(1)}, bf16[576,768]{1,0:T(8,128)(2,1)S(1)}, u32[]{:S(2)}, u32[]{:S(2)}) collective-permute-start(bf16[576,768]{1,0:T(8,128)(2,1)S(1)} %pad_maximum_fusion.3.own), channel_id=1, source_target_pairs={{0,4},{1,9},{2,6},{3,11},{4,0},{5,13},{6,2},{7,15},{8,12},{9,1},{1... | collective-permute-start | bytes 2654216 | tf_op jit(solution)/shard_map/ppermute | solution.py:43
  172.0 17.8 %collective-permute-start.38 = (bf16[576,768]{1,0:T(8,128)(2,1)S(1)}, bf16[576,768]{1,0:T(8,128)(2,1)S(1)}, u32[]{:S(2)}, u32[]{:S(2)}) collective-permute-start(bf16[576,768]{1,0:T(8,128)(2,1)S(1)} %pad_maximum_fusion.4.own), channel_id=1, source_target_pairs={{0,2},{1,17},{2,0},{3,19},{4,6},{5,21},{6,4},{7,23},{8,10},{9,25},... | collective-permute-start | bytes 2654216 | tf_op jit(solution)/shard_map/ppermute | solution.py:43
  173.6 12.1 %collective-permute-start.30 = (bf16[512,768]{1,0:T(8,128)(2,1)S(1)}, bf16[512,768]{1,0:T(8,128)(2,1)S(1)}, u32[]{:S(2)}, u32[]{:S(2)}) collective-permute-start(bf16[512,768]{1,0:T(8,128)(2,1)S(1)} %pad_maximum_fusion.6.own), channel_id=1, source_target_pairs={{0,16},{1,3},{2,18},{3,1},{4,20},{5,7},{6,22},{7,5},{8,24},{9,11},... | collective-permute-start | bytes 2359304 | tf_op jit(solution)/shard_map/ppermute | solution.py:43
  (40 other events, 238.8 us)

commit v7 on v6

--- a/solution.py
+++ b/solution.py
@@ -243,7 +243,7 @@
 
 def project(core, tokens, weights, other, gain, cos, sin, own_rows):
     rows, width = tokens.shape
-    step = min(rows, 256)
+    step = min(rows, 512)
 
     def fixed(shape):
         return pl.BlockSpec(shape, lambda i: (0, 0))

time: 193 us -> 192 us (level)
  no operation moved by 1% of the time
where the time goes in v7:
time: 192 us
  waiting for transfers between devices  61.8 us (32%)
  starting transfers between devices  54.7 us (28%)
  Pallas kernels  38.9 us (20%)
  other arithmetic  18.2 us (9%)
  local copies, waits for them, and re-layouts  17.1 us (9%)
    ppermute x30, waiting for transfers between devices, flip(): return lax.ppermute(block, ('seq', 'ctx', 'wsh'), route)  61.7 us
    ppermute x30, starting transfers between devices, flip(): return lax.ppermute(block, ('seq', 'ctx', 'wsh'), route)  52.4 us
    unnamed x50, local copies, waits for them, and re-layouts  10.2 us
    convert_element_type x13, other arithmetic, summed(): return sum(cut[1:], cut[0]).astype(BF16)  9.74 us
    pallas_call x3, Pallas kernels, unpack(): pl.pallas_call(partial(unpack_kernel, places, bool(gained)), in_specs=[SM...  6.51 us
    pallas_call x1, Pallas kernels, attend_back(): pl.pallas_call(partial(attend_back_kernel, per), grid=(steps,), in_specs=...  6.22 us
    pallas_call x2, Pallas kernels, project(): pl.pallas_call(project_kernel, grid=(rows // step,), in_specs=[SMEM_SPEC,...  5.6 us
    pallas_call x1, Pallas kernels, late_rows(): pl.pallas_call(late_rows_whole_kernel, in_specs=[SMEM_SPEC] + [WHOLE] * 5...  4.9 us
  transfers between devices with their start and end apart: 39, of which 17 were waited for; matrix products, arithmetic and copies ran while one was open for 12% of the time, Pallas kernels for 11%

profile of v7, /device:TPU:0, one launch (start us, length us, event | category | flops | bytes accessed | tf_op | source)
XLA Modules:
  0.0 191.8 jit_solution(10704882212510475460)
XLA Ops:
  0.6 4.1 %collective-permute-start = (bf16[128,768]{1,0:T(8,128)(2,1)}, bf16[128,768]{1,0:T(8,128)(2,1)S(1)}, u32[]{:S(2)}, u32[]{:S(2)}) collective-permute-start(bf16[128,768]{1,0:T(8,128)(2,1)} %bitcast.10), channel_id=1, source_target_pairs={{0,8},{1,3},{2,10},{3,1},{4,12},{5,7},{6,14},{7,5},{8,0},{9,11},{1... | collective-permute-start | bytes 589832 | tf_op jit(solution)/shard_map/ppermute | solution.py:43
  12.7 10.2 %collective-permute-done.1 = bf16[256,768]{1,0:T(8,128)(2,1)S(1)} collective-permute-done((bf16[256,768]{1,0:T(8,128)(2,1)S(1)}, bf16[256,768]{1,0:T(8,128)(2,1)S(1)}, u32[]{:S(2)}, u32[]{:S(2)}) %collective-permute-start.1) | collective-permute-done | bytes 393248 | tf_op jit(solution)/shard_map/ppermute | solution.py:43
  28.1 3.8 %project.2 = (bf16[512,1536]{1,0:T(8,128)(2,1)S(1)}, bf16[512,768]{1,0:T(8,128)(2,1)S(1)}, bf16[128,768]{1,0:T(8,128)(2,1)S(1)}, bf16[768,2304]{1,0:T(8,128)(2,1)S(1)}) custom-call(s32[1]{0:T(128)} %bitcast.core, bf16[512,768]{1,0:T(8,128)(2,1)S(1)} %pad_maximum_fusion.5.tokens, bf16[384,2304]{1,0:T(8,128)(2,1)S(1)} %copy-done.1, ...), custom_call_target="tpu_custom_call" | custom-call | flops 1207959552 | bytes 3145728 | tf_op jit(solution)/shard_map/project/pallas_call | solution.py:263
  36.8 3.0 %attend_last.1 = (f32[128,768]{1,0:T(8,128)S(1)}, f32[128,128]{1,0:T(8,128)S(1)}) custom-call(bf16[128,768]{1,0:T(8,128)(2,1)S(1)} %get-tuple-element.46.queries, bf16[512,1536]{1,0:T(8,128)(2,1)S(1)} %get-tuple-element.48.keys.values.keys_b.values_b, bf16[512,1536]{1,0:T(8,128)(2,1)S(1)} %get-tuple-element.48.keys.values.keys_b.values_b, ...), custom_call_target="tpu_custom_call" | custom-call | flops 402653184 | bytes 2359296 | tf_op jit(solution)/shard_map/attend_last/pallas_call | solution.py:393
  39.9 4.6 %middle.1 = (bf16[128,768]{1,0:T(8,128)(2,1)}, bf16[128,1408]{1,0:T(8,128)(2,1)S(1)}, bf16[128,1408]{1,0:T(8,128)(2,1)S(1)}, bf16[128,3072]{1,0:T(8,128)(2,1)S(1...) custom-call(s32[1]{0:T(128)} %bitcast.core, bf16[128,768]{1,0:T(8,128)(2,1)S(1)} %bitcast.13, ...), custom_call_target="tpu_custom_call" | custom-call | flops 3321888768 | bytes 25165824 | tf_op jit(solution)/shard_map/middle/pallas_call | solution.py:468
  45.1 6.2 %attend_back.1 = (bf16[128,768]{1,0:T(8,128)(2,1)S(1)}, bf16[1024,768]{1,0:T(8,128)(2,1)S(1)}, bf16[1024,768]{1,0:T(8,128)(2,1)S(1)}) custom-call(bf16[128,768]{1,0:T(8,128)(2,1)S(1)} %get-tuple-element.46.queries, bf16[512,1536]{1,0:T(8,128)(2,1)S(1)} %get-tuple-element.49.keys.values.keys_a.values_a, ...), custom_call_target="tpu_custom_call" | custom-call | flops 2013265920 | bytes 7864320 | tf_op jit(solution)/shard_map/attend_back/pallas_call | solution.py:615
  54.9 4.9 %late_rows.1 = (bf16[1152,768]{1,0:T(8,128)(2,1)S(1)}, bf16[1152,768]{1,0:T(8,128)(2,1)}) custom-call(s32[1]{0:T(128)} %bitcast.core, bf16[512,768]{1,0:T(8,128)(2,1)S(1)} %get-tuple-element.68.low_a, bf16[512,768]{1,0:T(8,128)(2,1)S(1)} %get-tuple-element.69.low_b, bf16[128,768]{1,0:T(8,128)(2,1)S(1)} %get-tuple-element.77.grad_q, ...), custom_call_target="tpu_custom_call" | custom-call | flops 1207959552 | bytes 3145728 | tf_op jit(solution)/shard_map/late_rows/pallas_call | solution.py:689
  75.4 3.9 %first_rows.1 = bf16[1024,768]{1,0:T(8,128)(2,1)S(1)} custom-call(bf16[128,768]{1,0:T(8,128)(2,1)S(1)} %copy-done.20, bf16[1024,768]{1,0:T(8,128)(2,1)S(1)} %copy-done.11, bf16[1024,768]{1,0:T(8,128)(2,1)S(1)} %copy-done.13, bf16[768,2304]{1,0:T(8,128)(2,1)S(1)} %copy-done.3), custom_call_target="tpu_custom_call" | custom-call | flops 2415919104 | bytes 6291456 | tf_op jit(solution)/shard_map/first_rows/pallas_call | solution.py:741
  82.0 6.5 %collective-permute-done.23 = bf16[512,768]{1,0:T(8,128)(2,1)} collective-permute-done((bf16[512,768]{1,0:T(8,128)(2,1)}, bf16[512,768]{1,0:T(8,128)(2,1)}, u32[]{:S(2)}, u32[]{:S(2)}) %collective-permute-start.23) | collective-permute-done | bytes 786464 | tf_op jit(solution)/shard_map/ppermute | solution.py:43
  88.5 2.4 %add_convert_fusion.6 = (bf16[256,768]{1,0:T(8,128)(2,1)}, bf16[256,768]{1,0:T(8,128)(2,1)}) fusion(bf16[512,768]{1,0:T(8,128)(2,1)} %collective-permute-done.23, s32[]{:T(128)S(6)} %select_n.332, bf16[1024,768]{1,0:T(8,128)(2,1)} %copy-done.16, s32[]{:T(128)S(6)} %select_n.331, s32[]{:T(128)S(6)} %select_n.335, s32[]{:T(128)S(6)} %select_n.334), kind=kLoop, calls=%fused_computation.17 | loop fusion | flops 1572864 | bytes 2359312 | tf_op jit(solution)/shard_map/convert_element_type | solution.py:118
  91.0 2.6 %collective-permute-start.24 = (bf16[256,768]{1,0:T(8,128)(2,1)}, bf16[256,768]{1,0:T(8,128)(2,1)}, u32[]{:S(2)}, u32[]{:S(2)}) collective-permute-start(bf16[256,768]{1,0:T(8,128)(2,1)} %get-tuple-element.91), channel_id=1, source_target_pairs={{0,2},{1,17},{2,0},{3,19},{4,6},{5,21},{6,4},{7,23},{8,10},{9,25},... | collective-permute-start | bytes 1179656 | tf_op jit(solution)/shard_map/ppermute | solution.py:43
  93.6 3.8 %collective-permute-done.15 = bf16[576,768]{1,0:T(8,128)(2,1)} collective-permute-done((bf16[576,768]{1,0:T(8,128)(2,1)}, bf16[576,768]{1,0:T(8,128)(2,1)}, u32[]{:S(2)}, u32[]{:S(2)}) %collective-permute-start.15) | collective-permute-done | bytes 884768 | tf_op jit(solution)/shard_map/ppermute | solution.py:43
  110.5 4.3 %collective-permute-done.16 = bf16[288,768]{1,0:T(8,128)(2,1)S(1)} collective-permute-done((bf16[288,768]{1,0:T(8,128)(2,1)S(1)}, bf16[288,768]{1,0:T(8,128)(2,1)S(1)}, u32[]{:S(2)}, u32[]{:S(2)}) %collective-permute-start.16) | collective-permute-done | bytes 442400 | tf_op jit(solution)/shard_map/ppermute | solution.py:43
  119.1 2.5 %collective-permute-start.33 = (bf16[144,768]{1,0:T(8,128)(2,1)S(1)}, bf16[144,768]{1,0:T(8,128)(2,1)S(1)}, u32[]{:S(2)}, u32[]{:S(2)}) collective-permute-start(bf16[144,768]{1,0:T(8,128)(2,1)S(1)} %get-tuple-element.101), channel_id=1, source_target_pairs={{0,4},{1,5},{2,6},{3,7},{4,0},{5,1},{6,2},{7,3},{8,12},{9,13},{10,... | collective-permute-start | bytes 663560 | tf_op jit(solution)/shard_map/ppermute | solution.py:43
  123.0 3.5 %collective-permute-start.27 = (bf16[64,768]{1,0:T(8,128)(2,1)S(1)}, bf16[64,768]{1,0:T(8,128)(2,1)S(1)}, u32[]{:S(2)}, u32[]{:S(2)}) collective-permute-start(bf16[64,768]{1,0:T(8,128)(2,1)S(1)} %add_convert_fusion.23), channel_id=1, source_target_pairs={{0,8},{1,5},{2,10},{3,7},{4,12},{5,1},{6,14},{7,3},{8,0},{9,13},{1... | collective-permute-start | bytes 294920 | tf_op jit(solution)/shard_map/ppermute | solution.py:43
  126.7 5.9 %collective-permute-done.33 = bf16[144,768]{1,0:T(8,128)(2,1)S(1)} collective-permute-done((bf16[144,768]{1,0:T(8,128)(2,1)S(1)}, bf16[144,768]{1,0:T(8,128)(2,1)S(1)}, u32[]{:S(2)}, u32[]{:S(2)}) %collective-permute-start.33) | collective-permute-done | bytes 221216 | tf_op jit(solution)/shard_map/ppermute | solution.py:43
  134.4 2.5 %collective-permute-start.28 = (bf16[128,768]{1,0:T(8,128)(2,1)S(1)}, bf16[128,768]{1,0:T(8,128)(2,1)S(1)}, u32[]{:S(2)}, u32[]{:S(2)}) collective-permute-start(bf16[128,768]{1,0:T(8,128)(2,1)S(1)} %pad_maximum_fusion.15), channel_id=1, source_target_pairs={{0,4},{1,9},{2,6},{3,11},{4,0},{5,13},{6,2},{7,15},{8,12},{9,1},{1... | collective-permute-start | bytes 589832 | tf_op jit(solution)/shard_map/ppermute | solution.py:43
  145.1 4.6 %collective-permute-start.29 = (bf16[256,768]{1,0:T(8,128)(2,1)S(1)}, bf16[256,768]{1,0:T(8,128)(2,1)S(1)}, u32[]{:S(2)}, u32[]{:S(2)}) collective-permute-start(bf16[256,768]{1,0:T(8,128)(2,1)S(1)} %pad_maximum_fusion.12), channel_id=1, source_target_pairs={{0,2},{1,17},{2,0},{3,19},{4,6},{5,21},{6,4},{7,23},{8,10},{9,25},... | collective-permute-start | bytes 1179656 | tf_op jit(solution)/shard_map/ppermute | solution.py:43
  149.8 2.5 %collective-permute-start.36 = (bf16[144,768]{1,0:T(8,128)(2,1)S(1)}, bf16[144,768]{1,0:T(8,128)(2,1)S(1)}, u32[]{:S(2)}, u32[]{:S(2)}) collective-permute-start(bf16[144,768]{1,0:T(8,128)(2,1)S(1)} %pad_maximum_fusion.14), channel_id=1, source_target_pairs={{0,4},{1,5},{2,6},{3,7},{4,0},{5,1},{6,2},{7,3},{8,12},{9,13},{10,... | collective-permute-start | bytes 663560 | tf_op jit(solution)/shard_map/ppermute | solution.py:43
  153.6 4.4 %collective-permute-done.36 = bf16[144,768]{1,0:T(8,128)(2,1)S(1)} collective-permute-done((bf16[144,768]{1,0:T(8,128)(2,1)S(1)}, bf16[144,768]{1,0:T(8,128)(2,1)S(1)}, u32[]{:S(2)}, u32[]{:S(2)}) %collective-permute-start.36) | collective-permute-done | bytes 221216 | tf_op jit(solution)/shard_map/ppermute | solution.py:43
  159.7 5.0 %collective-permute-done.21 = bf16[288,768]{1,0:T(8,128)(2,1)S(1)} collective-permute-done((bf16[288,768]{1,0:T(8,128)(2,1)S(1)}, bf16[288,768]{1,0:T(8,128)(2,1)S(1)}, u32[]{:S(2)}, u32[]{:S(2)}) %collective-permute-start.21) | collective-permute-done | bytes 442400 | tf_op jit(solution)/shard_map/ppermute | solution.py:43
  164.9 2.7 %collective-permute-start.22 = (bf16[576,768]{1,0:T(8,128)(2,1)S(1)}, bf16[576,768]{1,0:T(8,128)(2,1)S(1)}, u32[]{:S(2)}, u32[]{:S(2)}) collective-permute-start(bf16[576,768]{1,0:T(8,128)(2,1)S(1)} %pad_maximum_fusion.3.own), channel_id=1, source_target_pairs={{0,4},{1,9},{2,6},{3,11},{4,0},{5,13},{6,2},{7,15},{8,12},{9,1},{1... | collective-permute-start | bytes 2654216 | tf_op jit(solution)/shard_map/ppermute | solution.py:43
  167.5 3.8 %collective-permute-done.37 = bf16[288,768]{1,0:T(8,128)(2,1)S(1)} collective-permute-done((bf16[288,768]{1,0:T(8,128)(2,1)S(1)}, bf16[288,768]{1,0:T(8,128)(2,1)S(1)}, u32[]{:S(2)}, u32[]{:S(2)}) %collective-permute-start.37) | collective-permute-done | bytes 442400 | tf_op jit(solution)/shard_map/ppermute | solution.py:43
  176.0 7.9 %collective-permute-done.14.part_b = bf16[128,768]{1,0:T(8,128)(2,1)S(1)} collective-permute-done((bf16[128,768]{1,0:T(8,128)(2,1)S(1)}, bf16[128,768]{1,0:T(8,128)(2,1)S(1)}, u32[]{:S(2)}, u32[]{:S(2)}) %collective-permute-start.14) | collective-permute-done | bytes 196640 | tf_op jit(solution)/shard_map/ppermute | solution.py:43
  (173 shorter events, 84.5 us)
Async XLA Ops:
  4.7 23.4 %collective-permute-start.2 = (bf16[384,2304]{1,0:T(8,128)(2,1)}, bf16[384,2304]{1,0:T(8,128)(2,1)}, u32[]{:S(2)}, u32[]{:S(2)}) collective-permute-start(bf16[384,2304]{1,0:T(8,128)(2,1)} %refs_0_.2), channel_id=1, source_target_pairs={{0,1},{1,0},{2,3},{3,2},{4,5},{5,4},{6,7},{7,6},{8,9},{9,8},{10,11... | collective-permute-start | bytes 5308424 | tf_op jit(solution)/shard_map/ppermute | solution.py:47
  6.7 17.9 %collective-permute-start.5 = (bf16[384,768]{1,0:T(8,128)(2,1)}, bf16[384,768]{1,0:T(8,128)(2,1)S(1)}, u32[]{:S(2)}, u32[]{:S(2)}) collective-permute-start(bf16[384,768]{1,0:T(8,128)(2,1)} %param.12), channel_id=1, source_target_pairs={{0,1},{1,0},{2,3},{3,2},{4,5},{5,4},{6,7},{7,6},{8,9},{9,8},{10,11... | collective-permute-start | bytes 1769480 | tf_op jit(solution)/shard_map/ppermute | solution.py:47
  6.8 18.3 %collective-permute-start.6 = (bf16[384,2304]{1,0:T(8,128)(2,1)}, bf16[384,2304]{1,0:T(8,128)(2,1)}, u32[]{:S(2)}, u32[]{:S(2)}) collective-permute-start(bf16[384,2304]{1,0:T(8,128)(2,1)} %refs_0_.3), channel_id=1, source_target_pairs={{0,1},{1,0},{2,3},{3,2},{4,5},{5,4},{6,7},{7,6},{8,9},{9,8},{10,11... | collective-permute-start | bytes 5308424 | tf_op jit(solution)/shard_map/ppermute | solution.py:47
  10.9 12.1 %collective-permute-start.1 = (bf16[256,768]{1,0:T(8,128)(2,1)S(1)}, bf16[256,768]{1,0:T(8,128)(2,1)S(1)}, u32[]{:S(2)}, u32[]{:S(2)}) collective-permute-start(bf16[256,768]{1,0:T(8,128)(2,1)S(1)} %pad_maximum_fusion.11), channel_id=1, source_target_pairs={{0,4},{1,9},{2,6},{3,11},{4,0},{5,13},{6,2},{7,15},{8,12},{9,1},{1... | collective-permute-start | bytes 1179656 | tf_op jit(solution)/shard_map/ppermute | solution.py:43
  12.6 12.2 %collective-permute-start.7 = (bf16[576,768]{1,0:T(8,128)(2,1)S(1)}, bf16[576,768]{1,0:T(8,128)(2,1)S(1)}, u32[]{:S(2)}, u32[]{:S(2)}) collective-permute-start(bf16[576,768]{1,0:T(8,128)(2,1)S(1)} %copy-done.23), channel_id=1, source_target_pairs={{0,1},{1,0},{2,3},{3,2},{4,5},{5,4},{6,7},{7,6},{8,9},{9,8},{10,11... | collective-permute-start | bytes 2654216 | tf_op jit(solution)/shard_map/ppermute | solution.py:47
  23.0 12.1 %collective-permute-start.4 = (bf16[512,768]{1,0:T(8,128)(2,1)S(1)}, bf16[512,768]{1,0:T(8,128)(2,1)S(1)}, u32[]{:S(2)}, u32[]{:S(2)}) collective-permute-start(bf16[512,768]{1,0:T(8,128)(2,1)S(1)} %pad_maximum_fusion.5.tokens), channel_id=1, source_target_pairs={{0,2},{1,5},{2,0},{3,7},{4,6},{5,1},{6,4},{7,3},{8,10},{9,13},{10,... | collective-permute-start | bytes 2359304 | tf_op jit(solution)/shard_map/ppermute | solution.py:43
  69.5 19.0 %collective-permute-start.23 = (bf16[512,768]{1,0:T(8,128)(2,1)}, bf16[512,768]{1,0:T(8,128)(2,1)}, u32[]{:S(2)}, u32[]{:S(2)}) collective-permute-start(bf16[512,768]{1,0:T(8,128)(2,1)} %constant_dynamic-slice_fusion.1), channel_id=1, source_target_pairs={{0,16},{1,3},{2,18},{3,1},{4,20},{5,7},{6,22},{7,5},{8,24},{9,11},... | collective-permute-start | bytes 2359304 | tf_op jit(solution)/shard_map/ppermute | solution.py:43
  71.0 26.4 %collective-permute-start.15 = (bf16[576,768]{1,0:T(8,128)(2,1)}, bf16[576,768]{1,0:T(8,128)(2,1)}, u32[]{:S(2)}, u32[]{:S(2)}) collective-permute-start(bf16[576,768]{1,0:T(8,128)(2,1)} %add_convert_fusion), channel_id=1, source_target_pairs={{0,4},{1,9},{2,6},{3,11},{4,0},{5,13},{6,2},{7,15},{8,12},{9,1},{1... | collective-permute-start | bytes 2654216 | tf_op jit(solution)/shard_map/ppermute | solution.py:43
  71.1 28.9 %collective-permute-start.31 = (bf16[576,768]{1,0:T(8,128)(2,1)}, bf16[576,768]{1,0:T(8,128)(2,1)}, u32[]{:S(2)}, u32[]{:S(2)}) collective-permute-start(bf16[576,768]{1,0:T(8,128)(2,1)} %constant_dynamic-slice_fusion), channel_id=1, source_target_pairs={{0,2},{1,17},{2,0},{3,19},{4,6},{5,21},{6,4},{7,23},{8,10},{9,25},... | collective-permute-start | bytes 2654216 | tf_op jit(solution)/shard_map/ppermute | solution.py:43
  81.4 25.7 %collective-permute-start.12 = (bf16[512,768]{1,0:T(8,128)(2,1)}, bf16[512,768]{1,0:T(8,128)(2,1)}, u32[]{:S(2)}, u32[]{:S(2)}) collective-permute-start(bf16[512,768]{1,0:T(8,128)(2,1)} %slice.70), channel_id=1, source_target_pairs={{0,2},{1,5},{2,0},{3,7},{4,6},{5,1},{6,4},{7,3},{8,10},{9,13},{10,... | collective-permute-start | bytes 2359304 | tf_op jit(solution)/shard_map/ppermute | solution.py:43
  91.0 14.9 %collective-permute-start.24 = (bf16[256,768]{1,0:T(8,128)(2,1)}, bf16[256,768]{1,0:T(8,128)(2,1)}, u32[]{:S(2)}, u32[]{:S(2)}) collective-permute-start(bf16[256,768]{1,0:T(8,128)(2,1)} %get-tuple-element.91), channel_id=1, source_target_pairs={{0,2},{1,17},{2,0},{3,19},{4,6},{5,21},{6,4},{7,23},{8,10},{9,25},... | collective-permute-start | bytes 1179656 | tf_op jit(solution)/shard_map/ppermute | solution.py:43
  99.5 15.4 %collective-permute-start.16 = (bf16[288,768]{1,0:T(8,128)(2,1)S(1)}, bf16[288,768]{1,0:T(8,128)(2,1)S(1)}, u32[]{:S(2)}, u32[]{:S(2)}) collective-permute-start(bf16[288,768]{1,0:T(8,128)(2,1)S(1)} %get-tuple-element.85), channel_id=1, source_target_pairs={{0,2},{1,17},{2,0},{3,19},{4,6},{5,21},{6,4},{7,23},{8,10},{9,25},... | collective-permute-start | bytes 1327112 | tf_op jit(solution)/shard_map/ppermute | solution.py:43
  101.4 17.5 %collective-permute-start.32 = (bf16[288,768]{1,0:T(8,128)(2,1)S(1)}, bf16[288,768]{1,0:T(8,128)(2,1)S(1)}, u32[]{:S(2)}, u32[]{:S(2)}) collective-permute-start(bf16[288,768]{1,0:T(8,128)(2,1)S(1)} %get-tuple-element.89), channel_id=1, source_target_pairs={{0,16},{1,3},{2,18},{3,1},{4,20},{5,7},{6,22},{7,5},{8,24},{9,11},... | collective-permute-start | bytes 1327112 | tf_op jit(solution)/shard_map/ppermute | solution.py:43
  108.4 66.9 %collective-permute-start.13 = (bf16[256,768]{1,0:T(8,128)(2,1)S(1)}, bf16[256,768]{1,0:T(8,128)(2,1)S(1)}, u32[]{:S(2)}, u32[]{:S(2)}) collective-permute-start(bf16[256,768]{1,0:T(8,128)(2,1)S(1)} %get-tuple-element.93), channel_id=1, source_target_pairs={{0,4},{1,9},{2,6},{3,11},{4,0},{5,13},{6,2},{7,15},{8,12},{9,1},{1... | collective-permute-start | bytes 1179656 | tf_op jit(solution)/shard_map/ppermute | solution.py:43
  114.9 11.6 %collective-permute-start.17 = (bf16[144,768]{1,0:T(8,128)(2,1)S(1)}, bf16[144,768]{1,0:T(8,128)(2,1)S(1)}, u32[]{:S(2)}, u32[]{:S(2)}) collective-permute-start(bf16[144,768]{1,0:T(8,128)(2,1)S(1)} %get-tuple-element.105), channel_id=1, source_target_pairs={{0,16},{1,3},{2,18},{3,1},{4,20},{5,7},{6,22},{7,5},{8,24},{9,11},... | collective-permute-start | bytes 663560 | tf_op jit(solution)/shard_map/ppermute | solution.py:43
  119.1 13.6 %collective-permute-start.33 = (bf16[144,768]{1,0:T(8,128)(2,1)S(1)}, bf16[144,768]{1,0:T(8,128)(2,1)S(1)}, u32[]{:S(2)}, u32[]{:S(2)}) collective-permute-start(bf16[144,768]{1,0:T(8,128)(2,1)S(1)} %get-tuple-element.101), channel_id=1, source_target_pairs={{0,4},{1,5},{2,6},{3,7},{4,0},{5,1},{6,2},{7,3},{8,12},{9,13},{10,... | collective-permute-start | bytes 663560 | tf_op jit(solution)/shard_map/ppermute | solution.py:43
  123.0 11.3 %collective-permute-start.27 = (bf16[64,768]{1,0:T(8,128)(2,1)S(1)}, bf16[64,768]{1,0:T(8,128)(2,1)S(1)}, u32[]{:S(2)}, u32[]{:S(2)}) collective-permute-start(bf16[64,768]{1,0:T(8,128)(2,1)S(1)} %add_convert_fusion.23), channel_id=1, source_target_pairs={{0,8},{1,5},{2,10},{3,7},{4,12},{5,1},{6,14},{7,3},{8,0},{9,13},{1... | collective-permute-start | bytes 294920 | tf_op jit(solution)/shard_map/ppermute | solution.py:43
  126.6 10.8 %collective-permute-start.18 = (bf16[72,768]{1,0:T(8,128)(2,1)S(1)}, bf16[72,768]{1,0:T(8,128)(2,1)S(1)}, u32[]{:S(2)}, u32[]{:S(2)}) collective-permute-start(bf16[72,768]{1,0:T(8,128)(2,1)S(1)} %add_convert_fusion.21), channel_id=1, source_target_pairs={{0,8},{1,5},{2,10},{3,7},{4,12},{5,1},{6,14},{7,3},{8,0},{9,13},{1... | collective-permute-start | bytes 331784 | tf_op jit(solution)/shard_map/ppermute | solution.py:43
  145.1 14.4 %collective-permute-start.29 = (bf16[256,768]{1,0:T(8,128)(2,1)S(1)}, bf16[256,768]{1,0:T(8,128)(2,1)S(1)}, u32[]{:S(2)}, u32[]{:S(2)}) collective-permute-start(bf16[256,768]{1,0:T(8,128)(2,1)S(1)} %pad_maximum_fusion.12), channel_id=1, source_target_pairs={{0,2},{1,17},{2,0},{3,19},{4,6},{5,21},{6,4},{7,23},{8,10},{9,25},... | collective-permute-start | bytes 1179656 | tf_op jit(solution)/shard_map/ppermute | solution.py:43
  152.4 12.2 %collective-permute-start.21 = (bf16[288,768]{1,0:T(8,128)(2,1)S(1)}, bf16[288,768]{1,0:T(8,128)(2,1)S(1)}, u32[]{:S(2)}, u32[]{:S(2)}) collective-permute-start(bf16[288,768]{1,0:T(8,128)(2,1)S(1)} %pad_maximum_fusion.9), channel_id=1, source_target_pairs={{0,2},{1,17},{2,0},{3,19},{4,6},{5,21},{6,4},{7,23},{8,10},{9,25},... | collective-permute-start | bytes 1327112 | tf_op jit(solution)/shard_map/ppermute | solution.py:43
  158.2 13.1 %collective-permute-start.37 = (bf16[288,768]{1,0:T(8,128)(2,1)S(1)}, bf16[288,768]{1,0:T(8,128)(2,1)S(1)}, u32[]{:S(2)}, u32[]{:S(2)}) collective-permute-start(bf16[288,768]{1,0:T(8,128)(2,1)S(1)} %pad_maximum_fusion.10), channel_id=1, source_target_pairs={{0,16},{1,3},{2,18},{3,1},{4,20},{5,7},{6,22},{7,5},{8,24},{9,11},... | collective-permute-start | bytes 1327112 | tf_op jit(solution)/shard_map/ppermute | solution.py:43
  164.9 22.2 %collective-permute-start.22 = (bf16[576,768]{1,0:T(8,128)(2,1)S(1)}, bf16[576,768]{1,0:T(8,128)(2,1)S(1)}, u32[]{:S(2)}, u32[]{:S(2)}) collective-permute-start(bf16[576,768]{1,0:T(8,128)(2,1)S(1)} %pad_maximum_fusion.3.own), channel_id=1, source_target_pairs={{0,4},{1,9},{2,6},{3,11},{4,0},{5,13},{6,2},{7,15},{8,12},{9,1},{1... | collective-permute-start | bytes 2654216 | tf_op jit(solution)/shard_map/ppermute | solution.py:43
  171.6 17.9 %collective-permute-start.38 = (bf16[576,768]{1,0:T(8,128)(2,1)S(1)}, bf16[576,768]{1,0:T(8,128)(2,1)S(1)}, u32[]{:S(2)}, u32[]{:S(2)}) collective-permute-start(bf16[576,768]{1,0:T(8,128)(2,1)S(1)} %pad_maximum_fusion.4.own), channel_id=1, source_target_pairs={{0,2},{1,17},{2,0},{3,19},{4,6},{5,21},{6,4},{7,23},{8,10},{9,25},... | collective-permute-start | bytes 2654216 | tf_op jit(solution)/shard_map/ppermute | solution.py:43
  173.2 12.1 %collective-permute-start.30 = (bf16[512,768]{1,0:T(8,128)(2,1)S(1)}, bf16[512,768]{1,0:T(8,128)(2,1)S(1)}, u32[]{:S(2)}, u32[]{:S(2)}) collective-permute-start(bf16[512,768]{1,0:T(8,128)(2,1)S(1)} %pad_maximum_fusion.6.own), channel_id=1, source_target_pairs={{0,16},{1,3},{2,18},{3,1},{4,20},{5,7},{6,22},{7,5},{8,24},{9,11},... | collective-permute-start | bytes 2359304 | tf_op jit(solution)/shard_map/ppermute | solution.py:43
  (40 other events, 239.7 us)
